TPU v7x, 32 devices: a whole 2x2x4 slice. The times are simulated.
32 devices in a mesh: passage: 8 (over z, y), tile: 4 (over x, core).
Axes of the slice: x: 2, y: 2, z: 4, core: 2. Of those that a mesh axis runs over, the one named last changes fastest.
Arguments:
- gas: float32 [2048, 8192], P('passage', 'tile'), may hold values from -6 to 6
- gas_speed: float32 [2048, 8192], P('passage', 'tile'), may hold values from 0.2 to 0.7
- solid: float32 [2048, 8192], P('passage', 'tile'), may hold values from -6 to 6
- material: int32 [2048, 8192], P('passage', 'tile'), may hold values from 0 to 2
- face_cell: int32 [131072], P(('passage', 'tile')), may hold values from 0 to 524287
- face_owner: int32 [131072, 1], P(('passage', 'tile')), may hold values from 0 to 31; in each aligned block of 4096 rows (0 to 4095, 4096 to 8191, ...) at most 256 rows name the same one
- face_surface: int32 [131072], P(('passage', 'tile')), may hold values from 0 to 4095
- film: float32 [131072], P(('passage', 'tile')), may hold values from 0.1 to 1
- wall_previous: float32 [131072], P(('passage', 'tile')), may hold values from -6 to 6
Outputs:
- gas_next: float32 [2048, 8192], P('passage', 'tile')
- solid_next: float32 [2048, 8192], P('passage', 'tile')
- wall_temps: float32 [131072], P(('passage', 'tile'))
Inputs may be any that keep to these rules, and one draw needn't show every extreme that they name: `face_owner`: among the 4096 faces of one gas tile, at most 256 name the same owner, and in some tile one owner is named by exactly 256 faces.
All inputs are finite; a program needn't handle non-finite values.
Results may differ from a plain program's by a relative error of at most 0.00002.
Values sent between devices are 32-bit elements; how exact they have to be, the bound alone decides.
No kernel may reach another device: no remote copies, remote signals or barrier semaphores. Data moves between devices by JAX's collectives and lax.ppermute only.
A program may use at most 128 MiB of HBM per device.

v0:
```python
import jax
import jax.numpy as jnp
from jax import lax
from jax.sharding import PartitionSpec as P

SUBSTEPS = 4


DIFFUSE = 0.05
SOLID_STEP = 0.1
SOFTEN = 0.08


def extended_2(cells, sides, width):
    for axis, dim in sides:
        count = lax.axis_size(axis)
        ends = count - 1
        head = lax.slice_in_dim(cells, 0, width, axis=dim)
        tail = lax.slice_in_dim(cells, cells.shape[dim] - width, cells.shape[dim], axis=dim)
        cells = jnp.concatenate(
            [
                lax.ppermute(tail, axis, [(i, (i + 1) % count) for i in range(ends)]),
                cells,
                lax.ppermute(head, axis, [((i + 1) % count, i) for i in range(ends)]),
            ],
            axis=dim,
        )
    return cells


def gas_tendency(values, speed):
    padded = extended_2(values, (("passage", 0), ("tile", 1)), 1)
    centre = padded[1:-1, 1:-1]
    laplace = (
        padded[2:, 1:-1] + padded[:-2, 1:-1] + padded[1:-1, 2:] + padded[1:-1, :-2] - 4.0 * centre
    )
    return -speed * (centre - padded[1:-1, :-2]) + DIFFUSE * laplace


def stencil(padded_t, padded_k, source):
    centre = padded_t[1:-1, 1:-1]
    conduct = padded_k[1:-1, 1:-1]
    flux = 0.5 * (conduct + padded_k[2:, 1:-1]) * (padded_t[2:, 1:-1] - centre)
    flux = flux + 0.5 * (conduct + padded_k[:-2, 1:-1]) * (padded_t[:-2, 1:-1] - centre)
    flux = flux + 0.5 * (conduct + padded_k[1:-1, 2:]) * (padded_t[1:-1, 2:] - centre)
    flux = flux + 0.5 * (conduct + padded_k[1:-1, :-2]) * (padded_t[1:-1, :-2] - centre)
    return centre + SOLID_STEP * (flux + source)


def base_conductivity(material):
    return jnp.where(
        material == 0,
        jnp.float32(1.0),
        jnp.where(material == 1, jnp.float32(0.3), jnp.float32(0.08)),
    )


def shards(
    gas, gas_speed, solid, material, face_cell, face_owner, face_surface, film, wall_previous
):
    passages = lax.axis_size("passage")
    tile_count = lax.axis_size("tile")
    devices_all = passages * tile_count
    slab_rows, slab_cols = solid.shape
    surface_size = 2 * slab_cols
    section_one = gas + gas_tendency(gas, gas_speed)
    gas_next = 0.5 * (gas + section_one + gas_tendency(section_one, gas_speed))
    heat = film * (gas_next.reshape(-1)[face_cell] - wall_previous)
    owner = face_owner[:, 0]
    target = owner * surface_size + face_surface
    partial_value = jnp.zeros((devices_all * surface_size,), jnp.float32).at[target].add(heat)
    owned = lax.psum_scatter(partial_value, ("passage", "tile"), scatter_dimension=0, tiled=True)
    source = jnp.concatenate(
        [owned.reshape(2, slab_cols), jnp.zeros((slab_rows - 2, slab_cols), jnp.float32)], axis=0
    )
    kbase = base_conductivity(material)
    temper = solid
    for substep in range(SUBSTEPS):
        conduct = kbase * jnp.exp(SOFTEN * temper)
        extended = extended_2(jnp.stack([temper, conduct]), (("passage", 1), ("tile", 2)), 1)
        temper = stencil(extended[0], extended[1], source)
    surface = temper[:2].reshape(-1)
    everywhere = lax.all_gather(surface, ("passage", "tile"), axis=0, tiled=True)
    wall_temps = everywhere[owner * surface_size + face_surface]
    return (gas_next, temper, wall_temps)


def solution(mesh):
    in_specs = (
        P("passage", "tile"),
        P("passage", "tile"),
        P("passage", "tile"),
        P("passage", "tile"),
        P(("passage", "tile")),
        P(("passage", "tile"), None),
        P(("passage", "tile")),
        P(("passage", "tile")),
        P(("passage", "tile")),
    )
    out_specs = (P("passage", "tile"), P("passage", "tile"), P(("passage", "tile")))
    return jax.shard_map(shards, mesh=mesh, in_specs=in_specs, out_specs=out_specs, check_vma=False)
```

profile of v0, /device:TPU:0, one launch (start us, length us, event | category | flops | bytes accessed | tf_op | source)
XLA Modules:
  0.0 445.1 jit_solution(2381807529360925775)
XLA Ops:
  8.1 4.9 %collective-permute-start = (f32[1,2048]{1,0:T(1,128)S(1)}, f32[1,2048]{1,0:T(1,128)S(1)}, u32[]{:S(2)}, u32[]{:S(2)}) collective-permute-start(f32[1,2048]{1,0:T(1,128)S(1)} %get-tuple-element.44), channel_id=1, source_target_pairs={{0,4},{4,8},{8,12},{12,16},{16,20},{20,24},{24,28},{1,5},{5,9},{9,... | collective-permute-start | bytes 24584 | tf_op jit(solution)/shard_map/ppermute | solution.py:22
  14.4 3.2 multiply_bitcast_fusion.3
  18.9 4.7 %collective-permute-start.8 = (f32[2,1,2048]{2,1,0:T(1,128)S(1)}, f32[2,1,2048]{2,1,0:T(1,128)S(1)}, u32[]{:S(2)}, u32[]{:S(2)}) collective-permute-start(f32[2,1,2048]{2,1,0:T(1,128)S(1)} %get-tuple-element.36), channel_id=1, source_target_pairs={{0,4},{4,8},{8,12},{12,16},{16,20},{20,24},{24,28},{1,5},{5,9},{9,... | collective-permute-start | bytes 49160 | tf_op jit(solution)/shard_map/ppermute | solution.py:22
  28.4 3.7 collective-permute-done.3
  32.2 4.6 %fusion.67 = f32[256,2048]{1,0:T(8,128)S(1)} fusion(f32[256,2048]{1,0:T(8,128)S(1)} %copy-done.4, f32[258,1]{1,0:T(8,128)} %collective-permute-done.3, f32[1,2048]{1,0:T(1,128)S(1)} %collective-permute-done.1, f32[1,2048]{1,0:T(1,128)S(1)} %collective-permute-done, f32[258,1]{1,0:T(8,128)S(1)} %collective-permute-done.2, f32[256,2048]{1,0:T(8,128)} %param.10), kind=kLoop, calls=%fused_computation.127 | loop fusion | flops 9961472 | bytes 6309904 | tf_op jit(solution)/shard_map/add | solution.py:66
  36.8 5.0 %collective-permute-start.4 = (f32[1,2048]{1,0:T(1,128)S(1)}, f32[1,2048]{1,0:T(1,128)S(1)}, u32[]{:S(2)}, u32[]{:S(2)}) collective-permute-start(f32[1,2048]{1,0:T(1,128)S(1)} %get-tuple-element.42), channel_id=1, source_target_pairs={{0,4},{4,8},{8,12},{12,16},{16,20},{20,24},{24,28},{1,5},{5,9},{9,... | collective-permute-start | bytes 24584 | tf_op jit(solution)/shard_map/ppermute | solution.py:22
  43.9 4.2 collective-permute-done.5
  48.3 4.3 collective-permute-start.6
  56.1 4.8 %collective-permute-start.10 = (f32[2,258,1]{2,1,0:T(8,128)}, f32[2,258,1]{2,1,0:T(8,128)}, u32[]{:S(2)}, u32[]{:S(2)}) collective-permute-start(f32[2,258,1]{2,1,0:T(8,128)} %get-tuple-element.29), channel_id=1, source_target_pairs={{0,1},{1,2},{2,3},{4,5},{5,6},{6,7},{8,9},{9,10},{10,11},{12,13},{... | collective-permute-start | bytes 6200 | tf_op jit(solution)/shard_map/ppermute | solution.py:22
  60.9 3.5 fusion.58
  65.7 23.0 %gather_fusion = f32[4096]{0:T(1024)S(1)} fusion(f32[524288]{0:T(1024)S(1)} %bitcast.34, s32[4096]{0:T(1024)S(1)} %fusion.73), kind=kCustom, calls=%fused_computation | custom fusion | bytes 49152 | tf_op jit(solution)/shard_map/gather | solution.py:68
  88.8 22.7 %scatter_custom_fusion = f32[131072]{0:T(1024)} fusion(s32[4096]{0:T(1024)S(1)} %get-tuple-element.4, f32[4096]{0:T(1024)S(1)} %subtract_multiply_fusion, f32[]{:T(128)} %constant.5.clone.1), kind=kCustom, calls=%fused_computation.145 | custom fusion | flops 4096 | bytes 524292 | tf_op jit(solution)/shard_map/scatter-add | solution.py:71
  111.5 6.6 %concatenate.70 = f32[2,258,2050]{2,1,0:T(8,128)} concatenate(f32[2,258,1]{2,1,0:T(8,128)} %collective-permute-done.10, f32[2,258,2048]{2,1,0:T(8,128)} %copy-done, f32[2,258,1]{2,1,0:T(8,128)} %collective-permute-done.11), dimensions={2} | concatenate | bytes 8462400 | tf_op jit(solution)/shard_map/concatenate | solution.py:20
  118.1 4.1 slice_bitcast_fusion.6
  122.3 119.5 %all-reduce.4.cloned.1.call-done = f32[131072]{0:T(1024)} async-done(((f32[131072]{0:T(1024)}), f32[131072]{0:T(1024)}) %all-reduce.4.cloned.1.call-update) | async-done | bytes 524304
  242.5 9.3 %multiply_bitcast_fusion.2 = (f32[1,256,2048]{2,1,0:T(8,128)S(1)}, f32[256,2048]{1,0:T(8,128)S(1)}) fusion(pred[256,2048]{1,0:T(8,128)(4,1)S(1)} %get-tuple-element.13, pred[256,2048]{1,0:T(8,128)(4,1)S(1)} %get-tuple-element.12, f32[2,2048]{1,0:T(2,128)S(1)} %reshape.18, f32[258,2050]{1,0:T(8,128)} %get-tuple-element.21, f32[258,2050]{1,0:T(8,128)S(1)} %get-tuple-element.20), kind=kLoop, calls=%fused_computation.140 | loop fusion | flops 13631488 | bytes 26230784 | tf_op jit(solution)/shard_map/stack | solution.py:80
  251.8 3.4 collective-permute-start.12
  256.7 4.1 collective-permute-done.13
  269.0 6.5 %concatenate.73 = f32[2,258,2050]{2,1,0:T(8,128)} concatenate(f32[2,258,1]{2,1,0:T(8,128)S(1)} %collective-permute-done.14, f32[2,258,2048]{2,1,0:T(8,128)} %copy-done.1, f32[2,258,1]{2,1,0:T(8,128)S(1)} %collective-permute-done.15), dimensions={2} | concatenate | bytes 8462400 | tf_op jit(solution)/shard_map/concatenate | solution.py:20
  278.2 4.8 %multiply_bitcast_fusion.1 = (f32[1,256,2048]{2,1,0:T(8,128)S(1)}, f32[256,2048]{1,0:T(8,128)S(1)}) fusion(pred[256,2048]{1,0:T(8,128)(4,1)S(1)} %get-tuple-element.13, pred[256,2048]{1,0:T(8,128)(4,1)S(1)} %get-tuple-element.12, f32[2,2048]{1,0:T(2,128)S(1)} %reshape.18, f32[258,2050]{1,0:T(8,128)S(1)} %get-tuple-element.19, ...), kind=kLoop, calls=%fused_computation.139 | loop fusion | flops 13631488 | bytes 26230784 | tf_op jit(solution)/shard_map/stack | solution.py:80
  283.0 4.2 collective-permute-start.16
  288.7 4.2 collective-permute-done.17
  296.9 4.4 collective-permute-start.18
  302.5 6.5 %concatenate.75 = f32[2,258,2050]{2,1,0:T(8,128)} concatenate(f32[2,258,1]{2,1,0:T(8,128)S(1)} %collective-permute-done.18, f32[2,258,2048]{2,1,0:T(8,128)} %copy-done.2, f32[2,258,1]{2,1,0:T(8,128)S(1)} %collective-permute-done.19), dimensions={2} | concatenate | bytes 8462400 | tf_op jit(solution)/shard_map/concatenate | solution.py:20
  311.7 4.8 %multiply_bitcast_fusion = (f32[1,256,2048]{2,1,0:T(8,128)S(1)}, f32[256,2048]{1,0:T(8,128)S(1)}) fusion(pred[256,2048]{1,0:T(8,128)(4,1)S(1)} %get-tuple-element.13, pred[256,2048]{1,0:T(8,128)(4,1)S(1)} %get-tuple-element.12, f32[2,2048]{1,0:T(2,128)S(1)} %reshape.18, f32[258,2050]{1,0:T(8,128)S(1)} %get-tuple-element.17, ...), kind=kLoop, calls=%fused_computation.138 | loop fusion | flops 13631488 | bytes 26230784 | tf_op jit(solution)/shard_map/stack | solution.py:80
  316.5 3.1 collective-permute-start.20
  321.0 4.2 collective-permute-done.21
  329.2 7.2 %collective-permute-start.22 = (f32[2,258,1]{2,1,0:T(8,128)S(1)}, f32[2,258,1]{2,1,0:T(8,128)S(1)}, u32[]{:S(2)}, u32[]{:S(2)}) collective-permute-start(f32[2,258,1]{2,1,0:T(8,128)S(1)} %get-tuple-element.23), channel_id=1, source_target_pairs={{0,1},{1,2},{2,3},{4,5},{5,6},{6,7},{8,9},{9,10},{10,11},{12,13},{... | collective-permute-start | bytes 6200 | tf_op jit(solution)/shard_map/ppermute | solution.py:22
  337.4 6.5 %concatenate.77 = f32[2,258,2050]{2,1,0:T(8,128)} concatenate(f32[2,258,1]{2,1,0:T(8,128)S(1)} %collective-permute-done.22, f32[2,258,2048]{2,1,0:T(8,128)} %copy-done.3, f32[2,258,1]{2,1,0:T(8,128)S(1)} %collective-permute-done.23), dimensions={2} | concatenate | bytes 8462400 | tf_op jit(solution)/shard_map/concatenate | solution.py:20
  346.5 4.8 %fusion.7 = f32[256,2048]{1,0:T(8,128)S(1)} fusion(f32[2,2048]{1,0:T(2,128)S(1)} %reshape.18, f32[258,2050]{1,0:T(8,128)S(1)} %get-tuple-element.15, f32[258,2050]{1,0:T(8,128)S(1)} %get-tuple-element.14), kind=kLoop, calls=%fused_computation.26 | loop fusion | flops 11534336 | bytes 23085056 | tf_op jit(solution)/shard_map/add | solution.py:47
  351.4 46.3 %all_gather.3 = f32[131072]{0:T(1024)S(1)} all-gather(f32[4096]{0:T(1024)S(1)} %bitcast.44), channel_id=1, replica_groups=mesh['passage'=8,'tile'=4] {'passage','tile'}, dimensions={0}, use_global_device_ids=true | all-gather | bytes 540672 | tf_op jit(solution)/shard_map/all_gather | solution.py:83
  397.7 40.5 %gather_fusion.1 = f32[4096]{0:T(1024)} fusion(f32[131072]{0:T(1024)S(1)} %all_gather.3, s32[4096]{0:T(1024)S(1)} %get-tuple-element.3), kind=kCustom, calls=%fused_computation.1 | custom fusion | bytes 49152 | tf_op jit(solution)/shard_map/gather | solution.py:84
  (97 shorter events, 46.7 us)
Async XLA Ops:
  7.2 234.6 %all-reduce.4.cloned.1.call-start = ((), (), s32[]{:S(2)}) async-start(), calls=%async_computation | async-start | bytes 1048576
  8.1 16.9 %collective-permute-start = (f32[1,2048]{1,0:T(1,128)S(1)}, f32[1,2048]{1,0:T(1,128)S(1)}, u32[]{:S(2)}, u32[]{:S(2)}) collective-permute-start(f32[1,2048]{1,0:T(1,128)S(1)} %get-tuple-element.44), channel_id=1, source_target_pairs={{0,4},{4,8},{8,12},{12,16},{16,20},{20,24},{24,28},{1,5},{5,9},{9,... | collective-permute-start | bytes 24584 | tf_op jit(solution)/shard_map/ppermute | solution.py:22
  13.0 12.0 %collective-permute-start.1 = (f32[1,2048]{1,0:T(1,128)S(1)}, f32[1,2048]{1,0:T(1,128)S(1)}, u32[]{:S(2)}, u32[]{:S(2)}) collective-permute-start(f32[1,2048]{1,0:T(1,128)S(1)} %get-tuple-element.45), channel_id=1, source_target_pairs={{4,0},{8,4},{12,8},{16,12},{20,16},{24,20},{28,24},{5,1},{9,5},{13... | collective-permute-start | bytes 24584 | tf_op jit(solution)/shard_map/ppermute | solution.py:24
  18.9 24.1 %collective-permute-start.8 = (f32[2,1,2048]{2,1,0:T(1,128)S(1)}, f32[2,1,2048]{2,1,0:T(1,128)S(1)}, u32[]{:S(2)}, u32[]{:S(2)}) collective-permute-start(f32[2,1,2048]{2,1,0:T(1,128)S(1)} %get-tuple-element.36), channel_id=1, source_target_pairs={{0,4},{4,8},{8,12},{12,16},{16,20},{20,24},{24,28},{1,5},{5,9},{9,... | collective-permute-start | bytes 49160 | tf_op jit(solution)/shard_map/ppermute | solution.py:22
  23.6 19.4 %collective-permute-start.9 = (f32[2,1,2048]{2,1,0:T(1,128)S(1)}, f32[2,1,2048]{2,1,0:T(1,128)S(1)}, u32[]{:S(2)}, u32[]{:S(2)}) collective-permute-start(f32[2,1,2048]{2,1,0:T(1,128)S(1)} %get-tuple-element.37), channel_id=1, source_target_pairs={{4,0},{8,4},{12,8},{16,12},{20,16},{24,20},{28,24},{5,1},{9,5},{13... | collective-permute-start | bytes 49160 | tf_op jit(solution)/shard_map/ppermute | solution.py:24
  25.8 2.6 collective-permute-start.2
  27.1 5.1 %collective-permute-start.3 = (f32[258,1]{1,0:T(8,128)S(1)}, f32[258,1]{1,0:T(8,128)}, u32[]{:S(2)}, u32[]{:S(2)}) collective-permute-start(f32[258,1]{1,0:T(8,128)S(1)} %get-tuple-element.41), channel_id=1, source_target_pairs={{1,0},{2,1},{3,2},{5,4},{6,5},{7,6},{9,8},{10,9},{11,10},{13,12},{... | collective-permute-start | bytes 3104 | tf_op jit(solution)/shard_map/ppermute | solution.py:24
  28.4 14.6 %copy-start.6 = (f32[256,2048]{1,0:T(8,128)S(1)}, f32[256,2048]{1,0:T(8,128)}, u32[]{:S(2)}) copy-start(f32[256,2048]{1,0:T(8,128)} %param.11) | copy-start | bytes 6291460
  28.4 14.6 %copy-start.8 = (f32[1,256,2048]{2,1,0:T(8,128)S(1)}, f32[1,256,2048]{2,1,0:T(8,128)}, u32[]{:S(2)}) copy-start(f32[1,256,2048]{2,1,0:T(8,128)} %copy-done.7) | copy-start | bytes 6291460
  36.8 7.2 %collective-permute-start.4 = (f32[1,2048]{1,0:T(1,128)S(1)}, f32[1,2048]{1,0:T(1,128)S(1)}, u32[]{:S(2)}, u32[]{:S(2)}) collective-permute-start(f32[1,2048]{1,0:T(1,128)S(1)} %get-tuple-element.42), channel_id=1, source_target_pairs={{0,4},{4,8},{8,12},{12,16},{16,20},{20,24},{24,28},{1,5},{5,9},{9,... | collective-permute-start | bytes 24584 | tf_op jit(solution)/shard_map/ppermute | solution.py:22
  41.7 6.4 %collective-permute-start.5 = (f32[1,2048]{1,0:T(1,128)S(1)}, f32[1,2048]{1,0:T(1,128)S(1)}, u32[]{:S(2)}, u32[]{:S(2)}) collective-permute-start(f32[1,2048]{1,0:T(1,128)S(1)} %get-tuple-element.43), channel_id=1, source_target_pairs={{4,0},{8,4},{12,8},{16,12},{20,16},{24,20},{28,24},{5,1},{9,5},{13... | collective-permute-start | bytes 24584 | tf_op jit(solution)/shard_map/ppermute | solution.py:24
  43.9 10.0 %copy-start = (f32[2,258,2048]{2,1,0:T(8,128)}, f32[2,258,2048]{2,1,0:T(8,128)S(1)}, u32[]{:S(2)}) copy-start(f32[2,258,2048]{2,1,0:T(8,128)S(1)} %pad_maximum_fusion) | copy-start | bytes 12681220
  43.9 17.0 %copy-start.9 = (f32[256,2048]{1,0:T(8,128)S(1)}, f32[256,2048]{1,0:T(8,128)}, u32[]{:S(2)}) copy-start(f32[256,2048]{1,0:T(8,128)} %param.10) | copy-start | bytes 6291460
  48.3 12.6 %collective-permute-start.6 = (f32[258,1]{1,0:T(8,128)S(1)}, f32[258,1]{1,0:T(8,128)S(1)}, u32[]{:S(2)}, u32[]{:S(2)}) collective-permute-start(f32[258,1]{1,0:T(8,128)S(1)} %get-tuple-element.38), channel_id=1, source_target_pairs={{0,1},{1,2},{2,3},{4,5},{5,6},{6,7},{8,9},{9,10},{10,11},{12,13},{... | collective-permute-start | bytes 3104 | tf_op jit(solution)/shard_map/ppermute | solution.py:22
  52.6 8.3 %collective-permute-start.7 = (f32[258,1]{1,0:T(8,128)S(1)}, f32[258,1]{1,0:T(8,128)S(1)}, u32[]{:S(2)}, u32[]{:S(2)}) collective-permute-start(f32[258,1]{1,0:T(8,128)S(1)} %get-tuple-element.39), channel_id=1, source_target_pairs={{1,0},{2,1},{3,2},{5,4},{6,5},{7,6},{9,8},{10,9},{11,10},{13,12},{... | collective-permute-start | bytes 3104 | tf_op jit(solution)/shard_map/ppermute | solution.py:24
  54.8 56.7 %collective-permute-start.11 = (f32[2,258,1]{2,1,0:T(8,128)}, f32[2,258,1]{2,1,0:T(8,128)}, u32[]{:S(2)}, u32[]{:S(2)}) collective-permute-start(f32[2,258,1]{2,1,0:T(8,128)} %get-tuple-element.28), channel_id=1, source_target_pairs={{1,0},{2,1},{3,2},{5,4},{6,5},{7,6},{9,8},{10,9},{11,10},{13,12},{... | collective-permute-start | bytes 6200 | tf_op jit(solution)/shard_map/ppermute | solution.py:24
  56.1 55.4 %collective-permute-start.10 = (f32[2,258,1]{2,1,0:T(8,128)}, f32[2,258,1]{2,1,0:T(8,128)}, u32[]{:S(2)}, u32[]{:S(2)}) collective-permute-start(f32[2,258,1]{2,1,0:T(8,128)} %get-tuple-element.29), channel_id=1, source_target_pairs={{0,1},{1,2},{2,3},{4,5},{5,6},{6,7},{8,9},{9,10},{10,11},{12,13},{... | collective-permute-start | bytes 6200 | tf_op jit(solution)/shard_map/ppermute | solution.py:22
  65.7 23.0 %copy-start.15 = (f32[4096]{0:T(1024)S(1)}, f32[4096]{0:T(1024)}, u32[]{:S(2)}) copy-start(f32[4096]{0:T(1024)} %param.16) | copy-start | bytes 49156
  65.7 23.0 %copy-start.16 = (f32[4096]{0:T(1024)S(1)}, f32[4096]{0:T(1024)}, u32[]{:S(2)}) copy-start(f32[4096]{0:T(1024)} %param.17) | copy-start | bytes 49156
  251.8 4.9 %collective-permute-start.12 = (f32[2,1,2048]{2,1,0:T(1,128)S(1)}, f32[2,1,2048]{2,1,0:T(1,128)S(1)}, u32[]{:S(2)}, u32[]{:S(2)}) collective-permute-start(f32[2,1,2048]{2,1,0:T(1,128)S(1)} %get-tuple-element.34), channel_id=1, source_target_pairs={{0,4},{4,8},{8,12},{12,16},{16,20},{20,24},{24,28},{1,5},{5,9},{9,... | collective-permute-start | bytes 49160 | tf_op jit(solution)/shard_map/ppermute | solution.py:22
  255.2 5.6 %collective-permute-start.13 = (f32[2,1,2048]{2,1,0:T(1,128)S(1)}, f32[2,1,2048]{2,1,0:T(1,128)S(1)}, u32[]{:S(2)}, u32[]{:S(2)}) collective-permute-start(f32[2,1,2048]{2,1,0:T(1,128)S(1)} %get-tuple-element.35), channel_id=1, source_target_pairs={{4,0},{8,4},{12,8},{16,12},{20,16},{24,20},{28,24},{5,1},{9,5},{13... | collective-permute-start | bytes 49160 | tf_op jit(solution)/shard_map/ppermute | solution.py:24
  263.5 4.4 collective-permute-start.15
  264.8 4.2 collective-permute-start.14
  283.0 5.7 %collective-permute-start.16 = (f32[2,1,2048]{2,1,0:T(1,128)S(1)}, f32[2,1,2048]{2,1,0:T(1,128)S(1)}, u32[]{:S(2)}, u32[]{:S(2)}) collective-permute-start(f32[2,1,2048]{2,1,0:T(1,128)S(1)} %get-tuple-element.32), channel_id=1, source_target_pairs={{0,4},{4,8},{8,12},{12,16},{16,20},{20,24},{24,28},{1,5},{5,9},{9,... | collective-permute-start | bytes 49160 | tf_op jit(solution)/shard_map/ppermute | solution.py:22
  287.3 5.6 %collective-permute-start.17 = (f32[2,1,2048]{2,1,0:T(1,128)S(1)}, f32[2,1,2048]{2,1,0:T(1,128)S(1)}, u32[]{:S(2)}, u32[]{:S(2)}) collective-permute-start(f32[2,1,2048]{2,1,0:T(1,128)S(1)} %get-tuple-element.33), channel_id=1, source_target_pairs={{4,0},{8,4},{12,8},{16,12},{20,16},{24,20},{28,24},{5,1},{9,5},{13... | collective-permute-start | bytes 49160 | tf_op jit(solution)/shard_map/ppermute | solution.py:24
  295.6 5.7 %collective-permute-start.19 = (f32[2,258,1]{2,1,0:T(8,128)S(1)}, f32[2,258,1]{2,1,0:T(8,128)S(1)}, u32[]{:S(2)}, u32[]{:S(2)}) collective-permute-start(f32[2,258,1]{2,1,0:T(8,128)S(1)} %get-tuple-element.24), channel_id=1, source_target_pairs={{1,0},{2,1},{3,2},{5,4},{6,5},{7,6},{9,8},{10,9},{11,10},{13,12},{... | collective-permute-start | bytes 6200 | tf_op jit(solution)/shard_map/ppermute | solution.py:24
  296.9 5.6 %collective-permute-start.18 = (f32[2,258,1]{2,1,0:T(8,128)S(1)}, f32[2,258,1]{2,1,0:T(8,128)S(1)}, u32[]{:S(2)}, u32[]{:S(2)}) collective-permute-start(f32[2,258,1]{2,1,0:T(8,128)S(1)} %get-tuple-element.25), channel_id=1, source_target_pairs={{0,1},{1,2},{2,3},{4,5},{5,6},{6,7},{8,9},{9,10},{10,11},{12,13},{... | collective-permute-start | bytes 6200 | tf_op jit(solution)/shard_map/ppermute | solution.py:22
  316.5 4.5 %collective-permute-start.20 = (f32[2,1,2048]{2,1,0:T(1,128)S(1)}, f32[2,1,2048]{2,1,0:T(1,128)S(1)}, u32[]{:S(2)}, u32[]{:S(2)}) collective-permute-start(f32[2,1,2048]{2,1,0:T(1,128)S(1)} %get-tuple-element.30), channel_id=1, source_target_pairs={{0,4},{4,8},{8,12},{12,16},{16,20},{20,24},{24,28},{1,5},{5,9},{9,... | collective-permute-start | bytes 49160 | tf_op jit(solution)/shard_map/ppermute | solution.py:22
  319.6 5.6 %collective-permute-start.21 = (f32[2,1,2048]{2,1,0:T(1,128)S(1)}, f32[2,1,2048]{2,1,0:T(1,128)S(1)}, u32[]{:S(2)}, u32[]{:S(2)}) collective-permute-start(f32[2,1,2048]{2,1,0:T(1,128)S(1)} %get-tuple-element.31), channel_id=1, source_target_pairs={{4,0},{8,4},{12,8},{16,12},{20,16},{24,20},{28,24},{5,1},{9,5},{13... | collective-permute-start | bytes 49160 | tf_op jit(solution)/shard_map/ppermute | solution.py:24
  327.9 8.5 %collective-permute-start.23 = (f32[2,258,1]{2,1,0:T(8,128)S(1)}, f32[2,258,1]{2,1,0:T(8,128)S(1)}, u32[]{:S(2)}, u32[]{:S(2)}) collective-permute-start(f32[2,258,1]{2,1,0:T(8,128)S(1)} %get-tuple-element.22), channel_id=1, source_target_pairs={{1,0},{2,1},{3,2},{5,4},{6,5},{7,6},{9,8},{10,9},{11,10},{13,12},{... | collective-permute-start | bytes 6200 | tf_op jit(solution)/shard_map/ppermute | solution.py:24
  329.2 8.1 %collective-permute-start.22 = (f32[2,258,1]{2,1,0:T(8,128)S(1)}, f32[2,258,1]{2,1,0:T(8,128)S(1)}, u32[]{:S(2)}, u32[]{:S(2)}) collective-permute-start(f32[2,258,1]{2,1,0:T(8,128)S(1)} %get-tuple-element.23), channel_id=1, source_target_pairs={{0,1},{1,2},{2,3},{4,5},{5,6},{6,7},{8,9},{9,10},{10,11},{12,13},{... | collective-permute-start | bytes 6200 | tf_op jit(solution)/shard_map/ppermute | solution.py:22
  351.3 86.9 %copy-start.11 = (f32[256,2048]{1,0:T(8,128)}, f32[256,2048]{1,0:T(8,128)S(1)}, u32[]{:S(2)}) copy-start(f32[256,2048]{1,0:T(8,128)S(1)} %fusion.7) | copy-start | bytes 6291460
  (10 other events, 44.9 us)
Sparse Core Ops, SparseCore 0:
  111.6 130.0 all-reduce.3
where the time goes:
time: 446 us; the launch traced here: 445 us
  waiting for transfers between devices  143 us (32%)
  local copies, waits for them, and re-layouts  114 us (26%)
  starting transfers between devices  66.1 us (15%)
  other arithmetic  60.9 us (14%)
  blocking collectives  46.3 us (10%)
  between operations  14.7 us (3%)
    unnamed x2, waiting for transfers between devices  119 us
    ppermute x12, starting transfers between devices, extended_2(): lax.ppermute(tail, axis, [(i, (i + 1) % count) for i in range(ends)])  50.3 us
    all_gather x1, blocking collectives, shards(): lax.all_gather(surface, ('passage', 'tile'), axis=0, tiled=True)  46.3 us
    gather x1, local copies, waits for them, and re-layouts, shards(): wall_temps = everywhere[owner * surface_size + face_surface]  40.5 us
    concatenate x4, local copies, waits for them, and re-layouts, extended_2(): jnp.concatenate([lax.ppermute(tail, axis, [(i, (i + 1) % count) for i in...  26.2 us
    gather x1, local copies, waits for them, and re-layouts, shards(): heat = film * (gas_next.reshape(-1)[face_cell] - wall_previous)  23 us
    scatter-add x1, other arithmetic, shards(): jnp.zeros((devices_all * surface_size,), jnp.float32).at[target].add(heat)  22.7 us
    another operation x4, other arithmetic, shards(): jnp.stack([temper, conduct])  22 us
  transfers between devices with their start and end apart: 25, of which 11 were waited for; matrix products, arithmetic and copies ran while one was open for 16% of the time, Pallas kernels for 0%

commit v1 on v0

v1 whole, which is shorter than its diff:
```python
import functools

import jax
import jax.numpy as jnp
from jax import lax
from jax.experimental import pallas as pl
from jax.experimental.pallas import tpu as pltpu
from jax.sharding import PartitionSpec as P

SUBSTEPS = 4
DIFFUSE = 0.05
SOLID_STEP = 0.1
SOFTEN = 0.08
LANES = 128
ROWS = 8
ROUTE_ROWS = 8
EDGE = SUBSTEPS - 1
F32 = jnp.float32
BF16 = jnp.bfloat16
VMEM = pltpu.VMEM
MIB = 2**20


def params(mib):
    return pltpu.CompilerParams(vmem_limit_bytes=mib * MIB)


def whole(space=pltpu.VMEM):
    return pl.BlockSpec(memory_space=space)


def iota(shape, dim):
    return lax.broadcasted_iota(jnp.int32, shape, dim)


def base_conductivity(material):
    return jnp.where(
        material == 0,
        jnp.float32(1.0),
        jnp.where(material == 1, jnp.float32(0.3), jnp.float32(0.08)),
    )


def even(axis):
    return lax.rem(lax.axis_index(axis), 2) == 0


def split3(x):
    one = x.astype(BF16).astype(F32)
    rest = x - one
    two = rest.astype(BF16).astype(F32)
    return one, two, (rest - two).astype(BF16).astype(F32)


def dot_lanes(a, b):
    return lax.dot_general(a, b, (((1,), (1,)), ((), ())), preferred_element_type=F32)


def dot(a, b):
    return lax.dot_general(a, b, (((1,), (0,)), ((), ())), preferred_element_type=F32)


def pair_swaps(axis, count):
    first = [(i, i + 1) for i in range(0, count - 1, 2)]
    second = [(i, i + 1) for i in range(1, count - 1, 2)]

    def both(pairs):
        return pairs + [(b, a) for a, b in pairs]

    def run(one, two):
        return lax.ppermute(one, axis, both(first)), lax.ppermute(two, axis, both(second))

    return run


def pack_columns(gl, gr, sl, sr, ul, ur, ml, mr, one_ref, two_ref):
    lane = iota(gl.shape, 1)
    head = jnp.where(
        lane < 4,
        ul[...],
        jnp.where(
            lane < 8,
            pltpu.roll(base_conductivity(ml[...]), 4, 1),
            jnp.where(lane < 10, pltpu.roll(gl[...], 8, 1), pltpu.roll(sl[...], 10, 1)),
        ),
    )
    tail = jnp.where(
        lane >= 124,
        ur[...],
        jnp.where(
            lane >= 120,
            pltpu.roll(base_conductivity(mr[...]), 124, 1),
            jnp.where(lane >= 118, pltpu.roll(gr[...], 120, 1), pltpu.roll(sr[...], 118, 1)),
        ),
    )
    head = head.T[0:16]
    tail = tail.T[112:128]
    is_even = even("tile")
    one_ref[...] = jnp.where(is_even, tail, head)
    two_ref[...] = jnp.where(is_even, head, tail)


def halo_tiles(w):
    lane = iota(w.shape, 1)
    zero = jnp.zeros_like(w)
    solid = jnp.where((lane < 4) | (lane >= 124), w, zero)
    conduct = jnp.where(
        lane < 4, pltpu.roll(w, 124, 1), jnp.where(lane >= 124, pltpu.roll(w, 4, 1), zero)
    )
    return solid, conduct


def gas_halo_tiles(w):
    lane = iota(w.shape, 1)
    zero = jnp.zeros_like(w)
    gas = jnp.where(
        lane < 2, pltpu.roll(w, 120, 1), jnp.where(lane >= 126, pltpu.roll(w, 8, 1), zero)
    )
    speed = jnp.where(
        lane < 1, pltpu.roll(w, 118, 1), jnp.where(lane >= 127, pltpu.roll(w, 10, 1), zero)
    )
    return gas, speed


def pack_rows(one, two, gt, gb, st, sb, ut, ub, mt, mb, w_ref, a_ref, b_ref, wt):
    is_even = even("tile")
    wt[...] = jnp.zeros_like(wt)
    wt[0:16, :] = jnp.where(is_even, one[...], two[...])
    wt[112:128, :] = jnp.where(is_even, two[...], one[...])
    w = wt[...].T
    w_ref[...] = w
    size = w.shape[0]
    wide = gt.shape[1] + LANES

    def rows(g, s, u, m, part, step, keep):
        uh, kh = halo_tiles(part)
        gh, sh = gas_halo_tiles(part)
        g = jnp.concatenate([g[...], gh], axis=1)
        s = jnp.concatenate([s[...], sh], axis=1)
        u = jnp.concatenate([u[...], uh], axis=1)
        k = jnp.concatenate([base_conductivity(m[...]), kh], axis=1)
        before = pltpu.roll(g, 1, 1)
        after = pltpu.roll(g, wide - 1, 1)
        inner = pltpu.roll(g, step, 0)
        partial = g - s * (g - before) + DIFFUSE * (inner + before + after - 4.0 * g)
        return g, partial, u, k

    row = iota((ROWS, wide), 0)
    zero = jnp.zeros((ROWS, wide), F32)
    g, partial, u, k = rows(gt, st, ut, mt, w[0:ROWS], ROWS - 1, 0)

    def first_two(x, y):
        return jnp.where(row == 0, x, jnp.where(row == 1, pltpu.roll(y, 1, 0), zero))

    up = (first_two(g, u), first_two(partial, k))
    g, partial, u, k = rows(gb, sb, ub, mb, w[size - ROWS : size], 1, 0)

    def last_rows(x, y):
        return jnp.where(row == 0, pltpu.roll(x, 1, 0), y)

    down = (last_rows(g, u), last_rows(partial, k))
    is_even = even("passage")
    for half in range(2):
        a_ref[half * ROWS : (half + 1) * ROWS, :] = jnp.where(is_even, down[half], up[half])
        b_ref[half * ROWS : (half + 1) * ROWS, :] = jnp.where(is_even, up[half], down[half])


def find_slots(devices, per_owner, rows, cols, owner, surface, cell, slot_ref, row_ref, idx_ref, held, lhs, rhs):
    blocks = owner.shape[0]
    owners = iota((devices, LANES), 0)
    for b in range(blocks):
        held[b * devices : (b + 1) * devices, :] = jnp.where(owner[b : b + 1, :] == owners, 1.0, 0.0).astype(BF16)
    r, c = iota((LANES, 2 * LANES), 0), iota((LANES, 2 * LANES), 1)
    before = jnp.where((r < c) | (c >= LANES), 1.0, 0.0).astype(BF16)
    counts = dot(held[...], before)
    high = slot_ref.shape[0]
    table = idx_ref.shape[0]
    start = jnp.zeros((devices, LANES), F32)
    highs, lows = iota((table, LANES), 0), iota((LANES, LANES), 0)
    for b in range(blocks):
        own = counts[b * devices : (b + 1) * devices]
        mine = owner[b : b + 1, :]
        rank = jnp.sum(
            jnp.where(mine == owners, own[:, :LANES] + start, 0.0), axis=0, keepdims=True
        ).astype(jnp.int32)
        start = start + own[:, LANES:]
        hi = mine * per_owner + lax.shift_right_logical(rank, 7)
        lo = rank & (LANES - 1)
        slot_ref[b : b + 1, :] = hi * LANES + lo
        value = surface[b : b + 1, :]
        coarse = (value & ~255).astype(F32)
        fine = (value & 255).astype(F32)
        at = slice(b * LANES, (b + 1) * LANES)
        lhs[0:table, at] = jnp.where(highs == hi, coarse, 0.0).astype(BF16)
        lhs[table : 2 * table, at] = jnp.where(highs == hi, fine, 0.0).astype(BF16)
        rhs[:, at] = jnp.where(lows == lo, 1.0, 0.0).astype(BF16)
    both = dot_lanes(lhs[...], rhs[...])
    idx_ref[...] = both[0:table] + both[table : 2 * table]
    place = cell[...]
    row_ref[...] = lax.div(lax.rem(place, cols), LANES) * rows + lax.div(place, cols)


def shifted(tiles, lane):
    count = len(tiles)
    left = [pltpu.roll(x, LANES - 1, 1) for x in tiles]
    right = [pltpu.roll(x, 1, 1) for x in tiles]
    after = [jnp.where(lane == LANES - 1, left[(i + 1) % count], left[i]) for i in range(count)]
    before = [jnp.where(lane == 0, right[i - 1], right[i]) for i in range(count)]
    return after, before


def gas_kernel(
    tiles_across, per_owner, gas, speed, w, ra, rb, rowidx, cell, owner, surface, slot, film, wall, idx,
    out, route, gx, sx, s1, tab, stage, lhs, rhs, sums, sem,
):
    rows, cols = gas.shape
    nt = cols // LANES
    devices = route.shape[0]
    blocks = owner.shape[0]
    table = idx.shape[0]
    copies = []
    for ct in range(nt):
        at = pl.ds(ct * LANES, LANES)
        copies.append(pltpu.make_async_copy(gas.at[:, at], gx.at[ct, pl.ds(ROWS, rows)], sem.at[0, ct]))
        copies.append(pltpu.make_async_copy(speed.at[:, at], sx.at[ct], sem.at[1, ct]))
    for copy in copies:
        copy.start()
    gh, sh = gas_halo_tiles(w[...])
    gx[nt, ROWS : ROWS + rows, :] = gh
    sx[nt] = sh
    is_even = even("passage")
    place = lax.axis_index("passage")
    in_top = jnp.where(place > 0, 1.0, 0.0)
    in_bottom = jnp.where(place < lax.axis_size("passage") - 1, 1.0, 0.0)

    def top(row, ct):
        at = slice(ct * LANES, (ct + 1) * LANES)
        return jnp.where(is_even, rb[row : row + 1, at], ra[row : row + 1, at])

    def bottom(row, ct):
        at = slice(ct * LANES, (ct + 1) * LANES)
        return jnp.where(is_even, ra[row : row + 1, at], rb[row : row + 1, at])

    for ct in range(nt + 1):
        gx[ct, ROWS - 1 : ROWS, :] = top(0, ct)
        gx[ct, ROWS + rows : ROWS + rows + 1, :] = bottom(0, ct)
    for copy in copies:
        copy.wait()
    for ct in range(nt):
        s1[ct, ROWS - 1 : ROWS, :] = in_top * (top(8, ct) + DIFFUSE * gx[ct, ROWS : ROWS + 1, :])
        s1[ct, ROWS + rows : ROWS + rows + 1, :] = in_bottom * (
            bottom(8, ct) + DIFFUSE * gx[ct, ROWS + rows - 1 : ROWS + rows, :]
        )
    lane = iota((ROWS, LANES), 1)

    def tendency(v, north, south, after, before, s):
        return DIFFUSE * (south + north + after + before - 4.0 * v) - s * (v - before)

    def first(i, carry):
        r0 = pl.multiple_of(i * ROWS, ROWS)
        v = [gx[ct, pl.ds(ROWS + r0, ROWS), :] for ct in range(nt + 1)]
        after, before = shifted(v, lane)
        for ct in range(nt + 1):
            north = gx[ct, pl.ds(ROWS - 1 + r0, ROWS), :]
            south = gx[ct, pl.ds(ROWS + 1 + r0, ROWS), :]
            s = sx[ct, pl.ds(r0, ROWS), :]
            new = v[ct] + tendency(v[ct], north, south, after[ct], before[ct], s)
            if ct == nt:
                new = jnp.where(s > 0, new, 0.0)
            s1[ct, pl.ds(ROWS + r0, ROWS), :] = new
        return carry

    lax.fori_loop(0, rows // ROWS, first, 0)

    def second(i, carry):
        r0 = pl.multiple_of(i * ROWS, ROWS)
        v = [s1[ct, pl.ds(ROWS + r0, ROWS), :] for ct in range(nt + 1)]
        after, before = shifted(v, lane)
        for ct in range(nt):
            north = s1[ct, pl.ds(ROWS - 1 + r0, ROWS), :]
            south = s1[ct, pl.ds(ROWS + 1 + r0, ROWS), :]
            s = sx[ct, pl.ds(r0, ROWS), :]
            g = gx[ct, pl.ds(ROWS + r0, ROWS), :]
            tab[pl.ds(ct * rows + r0, ROWS), :] = 0.5 * (
                g + v[ct] + tendency(v[ct], north, south, after[ct], before[ct], s)
            )
        return carry

    lax.fori_loop(0, rows // ROWS, second, 0)
    outs = [
        pltpu.make_async_copy(tab.at[pl.ds(ct * rows, rows)], out.at[:, pl.ds(ct * LANES, LANES)], sem.at[0, ct])
        for ct in range(nt)
    ]
    for copy in outs:
        copy.start()
    sub = iota((ROWS, LANES), 0)
    unroll = 8

    def gather(i, carry):
        base = pl.multiple_of(i * (ROWS * unroll), ROWS * unroll)
        for g in range(unroll):
            acc = jnp.broadcast_to(tab[pl.ds(rowidx[base + g * ROWS], 1), :], (ROWS, LANES))
            for j in range(1, ROWS):
                row = tab[pl.ds(rowidx[base + g * ROWS + j], 1), :]
                acc = jnp.where(sub == j, jnp.broadcast_to(row, (ROWS, LANES)), acc)
            stage[pl.ds(base + g * ROWS, ROWS), :] = acc
        return carry

    lax.fori_loop(0, stage.shape[0] // (ROWS * unroll), gather, 0)
    lanes_down = iota((LANES, LANES), 0)
    highs = iota((table, LANES), 0)
    owners = iota((devices, LANES), 0)
    part = table + devices
    for b in range(blocks):
        at = slice(b * LANES, (b + 1) * LANES)
        picked = jnp.where(lanes_down == (cell[b : b + 1, :] & (LANES - 1)), stage[at, :].T, 0.0)
        face = jnp.sum(picked, axis=0, keepdims=True)
        heat = split3(film[b : b + 1, :] * (face - wall[b : b + 1, :]))
        place_of = slot[b : b + 1, :]
        hi = lax.shift_right_logical(place_of, 7)
        lo = place_of & (LANES - 1)
        mine = owner[b : b + 1, :]
        voxel = surface[b : b + 1, :]
        line = lax.div(voxel, cols)
        col = lax.rem(voxel, cols)
        tile = lax.rem(mine, tiles_across)
        to_right = (col >= cols - EDGE) & (tile < tiles_across - 1)
        to_left = (col < EDGE) & (tile > 0)
        dest = jnp.where(to_right, mine + 1, jnp.where(to_left, mine - 1, -1))
        code = jnp.where(to_right, col - (cols - EDGE), 16 + col) + 8 * line
        for k in range(3):
            lhs[k * part : k * part + table, at] = jnp.where(highs == hi, heat[k], 0.0).astype(BF16)
            lhs[k * part + table : (k + 1) * part, at] = jnp.where(owners == dest, heat[k], 0.0).astype(BF16)
        rhs[0:LANES, at] = jnp.where(lanes_down == lo, 1.0, 0.0).astype(BF16)
        rhs[LANES : LANES + 32, at] = jnp.where(iota((32, LANES), 0) == code, 1.0, 0.0).astype(BF16)
    three = dot_lanes(lhs[...], rhs[...])
    sums[...] = three[0:part] + three[part : 2 * part] + three[2 * part : 3 * part]
    route[...] = jnp.zeros_like(route)
    for o in range(devices):
        own = slice(o * per_owner, (o + 1) * per_owner)
        route[o, 0:per_owner, :] = sums[own, 0:LANES]
        route[o, per_owner : 2 * per_owner, :] = idx[own, :]
        route[o, 2 * per_owner : 2 * per_owner + 1, 0:32] = sums[table + o : table + o + 1, LANES : LANES + 32]
    for copy in outs:
        copy.wait()


def strip_kernel(per_owner, recv, ra, rb, w, solid, material, top_ref, up_ref, ret_ref, lhs, rhs, dep, src, tabu):
    devices = recv.shape[0]
    cols = solid.shape[1]
    nt = cols // LANES
    wide = cols + LANES
    high = 2 * nt
    highs = iota((high, LANES), 0)
    lanes_down = iota((LANES, LANES), 0)
    for d in range(devices):
        for q in range(per_owner):
            at = slice((d * per_owner + q) * LANES, (d * per_owner + q + 1) * LANES)
            heat = split3(recv[d, q : q + 1, :])
            where = recv[d, per_owner + q : per_owner + q + 1, :].astype(jnp.int32)
            hi = lax.shift_right_logical(where, 7)
            for k in range(3):
                lhs[k * high : (k + 1) * high, at] = jnp.where(highs == hi, heat[k], 0.0).astype(BF16)
            rhs[:, at] = jnp.where(lanes_down == (where & (LANES - 1)), 1.0, 0.0).astype(BF16)
    three = dot_lanes(lhs[...], rhs[...])
    dep[...] = three[0:high] + three[high : 2 * high] + three[2 * high : 3 * high]
    edges = recv[0, 2 * per_owner : 2 * per_owner + 1, :]
    for d in range(1, devices):
        edges = edges + recv[d, 2 * per_owner : 2 * per_owner + 1, :]
    src[...] = jnp.zeros_like(src)
    lane = iota((1, LANES), 1)
    for line in range(2):
        for ct in range(nt):
            src[line : line + 1, ct * LANES : (ct + 1) * LANES] = dep[line * nt + ct : line * nt + ct + 1, :]
        left = pltpu.roll(edges, LANES - EDGE - 8 * line, 1)
        right = pltpu.roll(edges, LANES - 16 - 8 * line, 1)
        src[line : line + 1, cols:wide] = jnp.where(
            lane >= LANES - EDGE, left, jnp.where(lane < EDGE, right, 0.0)
        )
    is_even = even("passage")
    row8 = iota((ROWS, wide), 0)

    def above(at):
        return jnp.where(row8 > 0, jnp.where(is_even, rb[at : at + ROWS, :], ra[at : at + ROWS, :]), 0.0)

    uh, kh = halo_tiles(w[...])
    u = jnp.concatenate([above(0), jnp.concatenate([solid[...], uh], axis=1)], axis=0)
    k0 = jnp.concatenate([above(8), jnp.concatenate([base_conductivity(material[...]), kh], axis=1)], axis=0)
    inside = jnp.where(k0 > 0, 0.5 * SOLID_STEP, 0.0)
    source = jnp.concatenate(
        [jnp.zeros((ROWS, wide), F32), 2.0 * src[...], jnp.zeros((ROWS, wide), F32)], axis=0
    )
    high_rows = 3 * ROWS
    for _ in range(SUBSTEPS):
        k = k0 * jnp.exp(SOFTEN * u)
        across = (k + pltpu.roll(k, wide - 1, 1)) * (pltpu.roll(u, wide - 1, 1) - u)
        down = (k + pltpu.roll(k, high_rows - 1, 0)) * (pltpu.roll(u, high_rows - 1, 0) - u)
        flux = across - pltpu.roll(across, 1, 1) + down - pltpu.roll(down, 1, 0)
        u = u + inside * (flux + source)
    up_ref[...] = u[0:ROWS, 0:cols]
    top_ref[...] = u[ROWS : 2 * ROWS, 0:cols]
    for line in range(2):
        for ct in range(nt):
            tabu[line * nt + ct : line * nt + ct + 1, :] = top_ref[line : line + 1, ct * LANES : (ct + 1) * LANES]
    parts = jnp.concatenate(split3(tabu[...]), axis=0).astype(BF16)
    for d in range(devices):
        for q in range(per_owner):
            at = slice((d * per_owner + q) * LANES, (d * per_owner + q + 1) * LANES)
            x = dot(parts, rhs[:, at])
            x = x[0:high] + x[high : 2 * high] + x[2 * high : 3 * high]
            where = recv[d, per_owner + q : per_owner + q + 1, :].astype(jnp.int32)
            hi = lax.shift_right_logical(where, 7)
            ret_ref[d, q : q + 1, :] = jnp.sum(jnp.where(highs == hi, x, 0.0), axis=0, keepdims=True)


def bulk_kernel(solid, material, w, ra, rb, out, ua, ub, ka, kb, k0, mat, sem):
    rows, cols = solid.shape
    nt = cols // LANES
    copies = []
    for ct in range(nt):
        at = pl.ds(ct * LANES, LANES)
        copies.append(pltpu.make_async_copy(solid.at[:, at], ua.at[ct, pl.ds(ROWS, rows)], sem.at[0, ct]))
        copies.append(pltpu.make_async_copy(material.at[:, at], mat.at[ct], sem.at[1, ct]))
    for copy in copies:
        copy.start()
    uh, kh = halo_tiles(w[...])
    ua[nt, ROWS : ROWS + rows, :] = uh
    k0[nt] = kh
    ka[nt, ROWS : ROWS + rows, :] = kh * jnp.exp(SOFTEN * uh)
    is_even = even("passage")
    zero = jnp.zeros((ROWS, LANES), F32)
    for ct in range(nt + 1):
        at = slice(ct * LANES, (ct + 1) * LANES)
        below = jnp.where(is_even, ra[1:2, at], rb[1:2, at])
        below_k = jnp.where(is_even, ra[9:10, at], rb[9:10, at]) * jnp.exp(SOFTEN * below)
        for u, k in ((ua, ka), (ub, kb)):
            u[ct, 0:ROWS, :] = zero
            k[ct, 0:ROWS, :] = zero
            u[ct, ROWS + rows : ROWS + rows + 1, :] = below
            k[ct, ROWS + rows : ROWS + rows + 1, :] = below_k
    for copy in copies:
        copy.wait()

    def begin(i, carry):
        r0 = pl.multiple_of(i * ROWS, ROWS)
        for ct in range(nt):
            base = base_conductivity(mat[ct, pl.ds(r0, ROWS), :])
            k0[ct, pl.ds(r0, ROWS), :] = base
            ka[ct, pl.ds(ROWS + r0, ROWS), :] = base * jnp.exp(SOFTEN * ua[ct, pl.ds(ROWS + r0, ROWS), :])
        return carry

    lax.fori_loop(0, rows // ROWS, begin, 0)
    lane = iota((ROWS, LANES), 1)
    for step in range(SUBSTEPS):
        last = step == SUBSTEPS - 1
        u, k, nu, nk = (ua, ka, ub, kb) if step % 2 == 0 else (ub, kb, ua, ka)

        def body(i, carry, u=u, k=k, nu=nu, nk=nk, last=last):
            r0 = pl.multiple_of(i * ROWS, ROWS)
            at = pl.ds(ROWS + r0, ROWS)
            north, south = pl.ds(ROWS - 1 + r0, ROWS), pl.ds(ROWS + 1 + r0, ROWS)
            here = [u[ct, at, :] for ct in range(nt + 1)]
            cond = [k[ct, at, :] for ct in range(nt + 1)]
            turned = [pltpu.roll(x, LANES - 1, 1) for x in here]
            turned_k = [pltpu.roll(x, LANES - 1, 1) for x in cond]
            edge = lane == LANES - 1
            across = []
            for ct in range(nt + 1):
                after = jnp.where(edge, turned[(ct + 1) % (nt + 1)], turned[ct])
                after_k = jnp.where(edge, turned_k[(ct + 1) % (nt + 1)], turned_k[ct])
                across.append((cond[ct] + after_k) * (after - here[ct]))
            back = [pltpu.roll(x, 1, 1) for x in across]
            for ct in range(nt if last else nt + 1):
                flux = across[ct] - jnp.where(lane == 0, back[ct - 1], back[ct])
                flux = flux + (cond[ct] + k[ct, north, :]) * (u[ct, north, :] - here[ct])
                flux = flux + (cond[ct] + k[ct, south, :]) * (u[ct, south, :] - here[ct])
                base = k0[ct, pl.ds(r0, ROWS), :]
                if ct == nt:
                    flux = jnp.where(base > 0, flux, 0.0)
                new = here[ct] + 0.5 * SOLID_STEP * flux
                nu[ct, at, :] = new
                if not last:
                    nk[ct, at, :] = base * jnp.exp(SOFTEN * new)
            return carry

        lax.fori_loop(0, rows // ROWS, body, 0)
    final = ua if SUBSTEPS % 2 == 0 else ub
    outs = [
        pltpu.make_async_copy(final.at[ct, pl.ds(ROWS, rows)], out.at[:, pl.ds(ct * LANES, LANES)], sem.at[0, ct])
        for ct in range(nt)
    ]
    for copy in outs:
        copy.start()
    for copy in outs:
        copy.wait()


def finish_kernel(recv, slot, top, below, solid, wall_ref, out, tabl, edge, sem):
    devices, per_owner = recv.shape[0], recv.shape[1]
    rows = solid.shape[0]
    keep = rows - EDGE
    fetch = pltpu.make_async_copy(out.at[pl.ds(rows - ROWS, ROWS)], edge, sem.at[0])
    fetch.start()
    put = pltpu.make_async_copy(top, out.at[pl.ds(0, ROWS)], sem.at[1])
    put.start()
    for d in range(devices):
        tabl[d * per_owner : (d + 1) * per_owner, :] = recv[d]
    table = tabl.shape[0]
    parts = jnp.concatenate(split3(tabl[...]), axis=0).astype(BF16)
    highs, lanes_down = iota((table, LANES), 0), iota((LANES, LANES), 0)
    fetch.wait()
    last = lax.axis_index("passage") == lax.axis_size("passage") - 1
    row = iota(edge.shape, 0) + (rows - ROWS)
    edge[...] = jnp.where((row >= keep) & jnp.logical_not(last), below[...], edge[...])
    store = pltpu.make_async_copy(edge, out.at[pl.ds(rows - ROWS, ROWS)], sem.at[0])
    store.start()
    for b in range(slot.shape[0]):
        place = slot[b : b + 1, :]
        lows = jnp.where(lanes_down == (place & (LANES - 1)), 1.0, 0.0).astype(BF16)
        x = dot(parts, lows)
        x = x[0:table] + x[table : 2 * table] + x[2 * table : 3 * table]
        hi = lax.shift_right_logical(place, 7)
        wall_ref[b : b + 1, :] = jnp.sum(jnp.where(highs == hi, x, 0.0), axis=0, keepdims=True)
    put.wait()
    store.wait()


def shards(gas, gas_speed, solid, material, face_cell, face_owner, face_surface, film, wall_previous):
    passages = lax.axis_size("passage")
    tiles = lax.axis_size("tile")
    devices = passages * tiles
    rows, cols = solid.shape
    nt = cols // LANES
    faces = face_cell.shape[0]
    blocks = faces // LANES
    cap = 2 * faces // devices
    per_owner = max(1, cap // LANES)
    table = devices * per_owner
    wide = cols + LANES

    def shape(dims, kind=F32):
        return jax.ShapeDtypeStruct(dims, kind)

    def cost(flops, moved, hard=0):
        return pl.CostEstimate(flops=flops, bytes_accessed=moved, transcendentals=hard)

    fields = (gas, gas_speed, solid, material)
    left = pl.BlockSpec((rows, LANES), lambda i: (0, 0))
    right = pl.BlockSpec((rows, LANES), lambda i: (0, nt - 1))
    column = pl.BlockSpec((16, rows), lambda i: (0, 0))
    one, two = pl.pallas_call(
        pack_columns,
        grid=(1,),
        in_specs=[left, right] * 4,
        out_specs=[column, column],
        out_shape=[shape((16, rows))] * 2,
        name="pack_columns",
        cost_estimate=cost(1000000, 8 * rows * LANES * 4),
    )(*[x for field in fields for x in (field, field)])
    one, two = pair_swaps("tile", tiles)(one, two)

    def tall(count, row):
        return pl.BlockSpec((count, cols), lambda i: (row, 0))

    full = pl.BlockSpec((rows, LANES), lambda i: (0, 0))
    band = pl.BlockSpec((16, wide), lambda i: (0, 0))
    w, ra, rb = pl.pallas_call(
        pack_rows,
        grid=(1,),
        in_specs=[column, column] + [tall(ROWS, 0), tall(ROWS, rows // ROWS - 1)] * 4,
        out_specs=[full, band, band],
        out_shape=[shape((rows, LANES)), shape((16, wide)), shape((16, wide))],
        scratch_shapes=[VMEM((LANES, rows), F32)],
        name="pack_rows",
        cost_estimate=cost(1000000, 8 * ROWS * cols * 4),
    )(one, two, *[x for field in fields for x in (field, field)])
    ra, rb = pair_swaps("passage", passages)(ra, rb)

    def folded(x):
        return x.reshape(blocks, LANES)

    owner, surface, cell = folded(face_owner), folded(face_surface), folded(face_cell)
    slot, rowidx, idx = pl.pallas_call(
        functools.partial(find_slots, devices, per_owner, rows, cols),
        in_specs=[whole()] * 3,
        out_specs=[whole()] * 3,
        out_shape=[shape((blocks, LANES), jnp.int32), shape((blocks, LANES), jnp.int32), shape((table, LANES))],
        scratch_shapes=[
            VMEM((blocks * devices, LANES), BF16),
            VMEM((2 * table, faces), BF16),
            VMEM((LANES, faces), BF16),
        ],
        compiler_params=params(24),
        name="find_slots",
        cost_estimate=cost(20000000, 1000000),
    )(owner, surface, cell)

    part = table + devices
    gas_next, route = pl.pallas_call(
        functools.partial(gas_kernel, tiles, per_owner),
        in_specs=[whole(pl.ANY)] * 2 + [whole()] * 3 + [whole(pltpu.SMEM)] + [whole()] * 7,
        out_specs=[whole(pl.ANY), whole()],
        out_shape=[shape((rows, cols)), shape((devices, ROUTE_ROWS, LANES))],
        scratch_shapes=[
            VMEM((nt + 1, rows + 2 * ROWS, LANES), F32),
            VMEM((nt + 1, rows, LANES), F32),
            VMEM((nt + 1, rows + 2 * ROWS, LANES), F32),
            VMEM((nt * rows, LANES), F32),
            VMEM((faces, LANES), F32),
            VMEM((3 * part, faces), BF16),
            VMEM((LANES + 32, faces), BF16),
            VMEM((part, LANES + 32), F32),
            pltpu.SemaphoreType.DMA((2, nt)),
        ],
        compiler_params=params(40),
        name="gas_and_heat",
        cost_estimate=cost(60000000, 40000000),
    )(
        gas, gas_speed, w, ra, rb, rowidx.reshape(faces), cell, owner, surface, slot,
        folded(film), folded(wall_previous), idx,
    )
    recv = lax.all_to_all(route, ("passage", "tile"), 0, 0, tiled=True)

    bulk = pl.pallas_call(
        bulk_kernel,
        in_specs=[whole(pl.ANY)] * 2 + [whole()] * 3,
        out_specs=whole(pl.ANY),
        out_shape=shape((rows, cols)),
        scratch_shapes=[VMEM((nt + 1, rows + 2 * ROWS, LANES), F32)] * 4
        + [
            VMEM((nt + 1, rows, LANES), F32),
            VMEM((nt, rows, LANES), jnp.int32),
            pltpu.SemaphoreType.DMA((2, nt)),
        ],
        compiler_params=params(40),
        name="solid_bulk",
        cost_estimate=cost(60000000, 40000000),
    )(solid, material, w, ra, rb)

    slots = table * LANES
    top, up, ret = pl.pallas_call(
        functools.partial(strip_kernel, per_owner),
        grid=(1,),
        in_specs=[
            pl.BlockSpec((devices, ROUTE_ROWS, LANES), lambda i: (0, 0, 0)),
            band,
            band,
            pl.BlockSpec((16, LANES), lambda i: (0, 0)),
            tall(16, 0),
            tall(16, 0),
        ],
        out_specs=[
            pl.BlockSpec((ROWS, cols), lambda i: (0, 0)),
            pl.BlockSpec((ROWS, cols), lambda i: (0, 0)),
            pl.BlockSpec((devices, per_owner, LANES), lambda i: (0, 0, 0)),
        ],
        out_shape=[shape((ROWS, cols)), shape((ROWS, cols)), shape((devices, per_owner, LANES))],
        scratch_shapes=[
            VMEM((6 * nt, slots), BF16),
            VMEM((LANES, slots), BF16),
            VMEM((2 * nt, LANES), F32),
            VMEM((ROWS, wide), F32),
            VMEM((2 * nt, LANES), F32),
        ],
        compiler_params=params(32),
        name="solid_strip",
        cost_estimate=cost(20000000, 4000000),
    )(recv, ra, rb, w, solid, material)
    ret = lax.all_to_all(ret, ("passage", "tile"), 0, 0, tiled=True)
    below = lax.ppermute(up, "passage", [(i + 1, i) for i in range(passages - 1)])

    wall, solid_next = pl.pallas_call(
        finish_kernel,
        in_specs=[whole()] * 4 + [whole(pl.ANY)],
        out_specs=[whole(), whole(pl.ANY)],
        out_shape=[shape((blocks, LANES)), shape((rows, cols))],
        input_output_aliases={4: 1},
        scratch_shapes=[
            VMEM((table, LANES), F32),
            VMEM((ROWS, cols), F32),
            pltpu.SemaphoreType.DMA((2,)),
        ],
        compiler_params=params(24),
        name="wall_temperatures",
        cost_estimate=cost(20000000, 4000000),
    )(ret, slot, top, below, bulk)
    return gas_next, solid_next, wall.reshape(faces)


def solution(mesh):
    in_specs = (
        P("passage", "tile"),
        P("passage", "tile"),
        P("passage", "tile"),
        P("passage", "tile"),
        P(("passage", "tile")),
        P(("passage", "tile"), None),
        P(("passage", "tile")),
        P(("passage", "tile")),
        P(("passage", "tile")),
    )
    out_specs = (P("passage", "tile"), P("passage", "tile"), P(("passage", "tile")))
    return jax.shard_map(shards, mesh=mesh, in_specs=in_specs, out_specs=out_specs, check_vma=False)
```

time: 446 us -> 96.5 us (0.22)
  waiting for transfers between devices: 143 us -> 1.51 us
  local copies, waits for them, and re-layouts: 114 us -> 6.9 us
  other arithmetic: 60.9 us -> 0 us
  starting transfers between devices: 66.1 us -> 9.82 us
  Pallas kernels: 0 us -> 55.8 us
  blocking collectives: 46.3 us -> 21.2 us
  between operations: 14.7 us -> 0.78 us
    unnamed x2 -> x0, waiting for transfers between devices: 119 us -> none
    gather x2 -> x0, local copies, waits for them, and re-layouts: 63.6 us -> none  [the longest x1 40.5 us: shards(): wall_temps = everywhere[owner * surface_size + face_surface]]
    ppermute x24 -> x5, starting transfers between devices: 66.1 us -> 6.04 us  [the longest x2 3.31 us: run(): lax.ppermute(one, axis, both(first))]
    pallas_call x0 -> x7, Pallas kernels: none -> 55.8 us  [the longest x1 28 us: shards(): pl.pallas_call(bulk_kernel, in_specs=[whole(pl.ANY)] * 2 + [whole()] * 3,...]
    all_gather x1 -> x0, blocking collectives: 46.3 us -> none  [shards(): lax.all_gather(surface, ('passage', 'tile'), axis=0, tiled=True)]
    concatenate x4 -> x0, local copies, waits for them, and re-layouts: 26.2 us -> none  [extended_2(): jnp.concatenate([lax.ppermute(tail, axis, [(i, (i + 1) % count) for i in...]
    scatter-add x1 -> x0, other arithmetic: 22.7 us -> none  [shards(): jnp.zeros((devices_all * surface_size,), jnp.float32).at[target].add(heat)]
    ppermute x24 -> x5, waiting for transfers between devices: 24 us -> 1.51 us  [the longest x2 1.5 us: run(): lax.ppermute(one, axis, both(first))]
  transfers between devices with their start and end apart: 25 -> 6, of which waited for: 11 -> 2; matrix products, arithmetic and copies ran while one was open for 16% -> 0% of each run, Pallas kernels for 0% -> 30%
where the time goes in v1:
time: 96.5 us; the launch traced here: 96 us
  Pallas kernels  55.8 us (58%)
  blocking collectives  21.2 us (22%)
  starting transfers between devices  9.82 us (10%)
  local copies, waits for them, and re-layouts  6.9 us (7%)
  waiting for transfers between devices  1.51 us (2%)
    pallas_call x1, Pallas kernels, shards(): pl.pallas_call(bulk_kernel, in_specs=[whole(pl.ANY)] * 2 + [whole()] * 3,...  28 us
    all_to_all x1, blocking collectives, shards(): recv = lax.all_to_all(route, ('passage', 'tile'), 0, 0, tiled=True)  21.2 us
    pallas_call x1, Pallas kernels, shards(): pl.pallas_call(functools.partial(gas_kernel, tiles, per_owner), in_specs=...  15.1 us
    unnamed x28, local copies, waits for them, and re-layouts  6.9 us
    pallas_call x1, Pallas kernels, shards(): pl.pallas_call(functools.partial(strip_kernel, per_owner), grid=(1,), in_...  4.41 us
    all_to_all x1, starting transfers between devices, shards(): ret = lax.all_to_all(ret, ('passage', 'tile'), 0, 0, tiled=True)  3.78 us
    ppermute x2, starting transfers between devices, run(): lax.ppermute(one, axis, both(first))  3.31 us
    pallas_call x1, Pallas kernels, shards(): pl.pallas_call(finish_kernel, in_specs=[whole()] * 4 + [whole(pl.ANY)], o...  2.65 us
  transfers between devices with their start and end apart: 6, of which 2 were waited for; matrix products, arithmetic and copies ran while one was open for 0% of the time, Pallas kernels for 30%

profile of v1, /device:TPU:0, one launch (start us, length us, event | category | flops | bytes accessed | tf_op | source)
XLA Modules:
  0.0 96.0 jit_solution(12717034080126010129)
XLA Ops:
  0.6 2.3 %pack_columns.1 = (f32[16,256]{1,0:T(8,128)}, f32[16,256]{1,0:T(8,128)}) custom-call(f32[256,2048]{1,0:T(8,128)} %gas.1, f32[256,2048]{1,0:T(8,128)} %gas.1, f32[256,2048]{1,0:T(8,128)} %speed.1, f32[256,2048]{1,0:T(8,128)} %speed.1, f32[256,2048]{1,0:T(8,128)} %solid.3, f32[256,2048]{1,0:T(8,128)} %solid.3, s32[256,2048]{1,0:T(8,128)} %material.3, ...), custom_call_target="tpu_custom_call" | custom-call | flops 1000000 | bytes 1048576 | tf_op jit(solution)/shard_map/pack_columns/pallas_call | solution.py:551
  2.9 0.5 collective-permute-start
  3.4 0.0 copy-start.11
  3.4 0.8 collective-permute-start.1
  4.2 0.2 collective-permute-done.one
  4.4 0.0 collective-permute-done.1.two
  4.4 0.6 copy-done.12
  5.0 0.6 copy-done.13
  5.6 2.1 %pack_rows.1 = (f32[256,128]{1,0:T(8,128)}, f32[16,2176]{1,0:T(8,128)}, f32[16,2176]{1,0:T(8,128)}) custom-call(f32[16,256]{1,0:T(8,128)} %copy-done.12, f32[16,256]{1,0:T(8,128)} %copy-done.13, f32[256,2048]{1,0:T(8,128)} %gas.1, f32[256,2048]{1,0:T(8,128)} %gas.1, f32[256,2048]{1,0:T(8,128)} %speed.1, f32[256,2048]{1,0:T(8,128)} %speed.1, ...), custom_call_target="tpu_custom_call" | custom-call | flops 1000000 | bytes 524288 | tf_op jit(solution)/shard_map/pack_rows/pallas_call | solution.py:567
  7.7 2.9 %collective-permute-start.2 = (f32[16,2176]{1,0:T(8,128)}, f32[16,2176]{1,0:T(8,128)S(1)}, u32[]{:S(2)}, u32[]{:S(2)}) collective-permute-start(f32[16,2176]{1,0:T(8,128)} %get-tuple-element.21), channel_id=1, source_target_pairs={{0,4},{8,12},{16,20},{24,28},{4,0},{12,8},{20,16},{28,24},{1,5},{9... | collective-permute-start | bytes 417800 | tf_op jit(solution)/shard_map/ppermute | solution.py:71
  10.6 0.7 collective-permute-start.3
  11.2 0.0 copy-done.7
  11.2 0.0 copy-done.8
  11.3 1.3 %find_slots.1 = (s32[32,128]{1,0:T(8,128)S(1)}, s32[32,128]{1,0:T(8,128)S(1)}, f32[64,128]{1,0:T(8,128)S(1)}) custom-call(s32[32,128]{1,0:T(8,128)S(1)} %bitcast.7, s32[32,128]{1,0:T(8,128)S(1)} %bitcast.9, s32[32,128]{1,0:T(8,128)S(1)} %bitcast.11), custom_call_target="tpu_custom_call" | custom-call | flops 20000000 | bytes 1000000 | tf_op jit(solution)/shard_map/find_slots/pallas_call | solution.py:583
  12.5 1.3 %collective-permute-done.2.ra = f32[16,2176]{1,0:T(8,128)S(1)} collective-permute-done((f32[16,2176]{1,0:T(8,128)}, f32[16,2176]{1,0:T(8,128)S(1)}, u32[]{:S(2)}, u32[]{:S(2)}) %collective-permute-start.2) | collective-permute-done | bytes 139296 | tf_op jit(solution)/shard_map/ppermute | solution.py:71
  13.8 0.0 collective-permute-done.3.rb
  13.8 0.0 copy-done.10
  13.8 0.0 copy-start.3
  13.8 1.6 %copy-done.3 = f32[256,2048]{1,0:T(8,128)S(1)} copy-done((f32[256,2048]{1,0:T(8,128)S(1)}, f32[256,2048]{1,0:T(8,128)}, u32[]{:S(2)}) %copy-start.3) | copy-done | bytes 2097176
  15.4 1.6 %copy-done.4 = f32[256,2048]{1,0:T(8,128)S(1)} copy-done((f32[256,2048]{1,0:T(8,128)S(1)}, f32[256,2048]{1,0:T(8,128)}, u32[]{:S(2)}) %copy-start.4) | copy-done | bytes 2097176
  17.0 0.9 copy-done.5
  17.9 15.1 %gas_and_heat.1 = (f32[256,2048]{1,0:T(8,128)}, f32[32,8,128]{2,1,0:T(8,128)S(1)}) custom-call(f32[256,2048]{1,0:T(8,128)S(1)} %copy-done.3, f32[256,2048]{1,0:T(8,128)S(1)} %copy-done.4, f32[256,128]{1,0:T(8,128)S(1)} %copy-done.5, f32[16,2176]{1,0:T(8,128)S(1)} %collective-permute-done.2.ra, f32[16,2176]{1,0:T(8,128)S(1)} %collective-permute-done.3.rb, ...), custom_call_target="tpu_custom_call" | custom-call | flops 60000000 | bytes 40000000 | tf_op jit(solution)/shard_map/gas_and_heat/pallas_call | solution.py:599
  33.0 21.2 %all_to_all.10.recv = f32[32,8,128]{2,1,0:T(8,128)S(1)} all-to-all(f32[32,8,128]{2,1,0:T(8,128)S(1)} %get-tuple-element.27), channel_id=1, replica_groups=mesh['passage'=8,'tile'=4] {'passage','tile'}, dimensions={0} | all-to-all | bytes 262144 | tf_op jit(solution)/shard_map/all_to_all | solution.py:622
  54.2 4.4 %solid_strip.1 = (f32[8,2048]{1,0:T(8,128)S(1)}, f32[8,2048]{1,0:T(8,128)S(1)}, f32[32,2,128]{2,1,0:T(2,128)}) custom-call(f32[32,8,128]{2,1,0:T(8,128)S(1)} %all_to_all.10.recv, f32[16,2176]{1,0:T(8,128)S(1)} %collective-permute-done.2.ra, f32[16,2176]{1,0:T(8,128)S(1)} %collective-permute-done.3.rb, f32[256,128]{1,0:T(8,128)S(1)} %copy-done.5, ...), custom_call_target="tpu_custom_call" | custom-call | flops 20000000 | bytes 4000000 | tf_op jit(solution)/shard_map/solid_strip/pallas_call | solution.py:641
  58.6 1.3 %collective-permute-start.4 = (f32[8,2048]{1,0:T(8,128)S(1)}, f32[8,2048]{1,0:T(8,128)S(1)}, u32[]{:S(2)}, u32[]{:S(2)}) collective-permute-start(f32[8,2048]{1,0:T(8,128)S(1)} %get-tuple-element.30), channel_id=1, source_target_pairs={{4,0},{8,4},{12,8},{16,12},{20,16},{24,20},{28,24},{5,1},{9,5},{13... | collective-permute-start | bytes 196616 | tf_op jit(solution)/shard_map/ppermute | solution.py:670
  59.9 3.8 %all-to-all-start.1 = ((f32[32,2,128]{2,1,0:T(2,128)}), f32[32,2,128]{2,1,0:T(2,128)S(1)}, u32[]{:S(2)}, u32[]{:S(2)}) async-start(f32[32,2,128]{2,1,0:T(2,128)} %get-tuple-element.28), calls=%async_computation.1 | async-start | bytes 65536 | tf_op jit(solution)/shard_map/all_to_all | solution.py:669
  63.7 0.0 copy-start.2
  63.7 1.6 %copy-done.2 = s32[256,2048]{1,0:T(8,128)S(1)} copy-done((s32[256,2048]{1,0:T(8,128)S(1)}, s32[256,2048]{1,0:T(8,128)}, u32[]{:S(2)}) %copy-start.2) | copy-done | bytes 2097176
  65.3 28.0 %solid_bulk.1.solid = f32[256,2048]{1,0:T(8,128)} custom-call(f32[256,2048]{1,0:T(8,128)S(1)} %copy-done, s32[256,2048]{1,0:T(8,128)S(1)} %copy-done.2, f32[256,128]{1,0:T(8,128)S(1)} %copy-done.6, f32[16,2176]{1,0:T(8,128)S(1)} %collective-permute-done.2.ra, f32[16,2176]{1,0:T(8,128)S(1)} %collective-permute-done.3.rb), custom_call_target="tpu_custom_call" | custom-call | flops 60000000 | bytes 40000000 | tf_op jit(solution)/shard_map/solid_bulk/pallas_call | solution.py:624
  93.3 0.0 all-to-all-done.1.recv
  93.3 0.0 collective-permute-done.4.below
  93.3 2.7 %wall_temperatures.1 = (f32[32,128]{1,0:T(8,128)}, f32[256,2048]{1,0:T(8,128)}) custom-call(f32[32,2,128]{2,1,0:T(2,128)S(1)} %all-to-all-done.1.recv, s32[32,128]{1,0:T(8,128)S(1)} %get-tuple-element.24.slot, f32[8,2048]{1,0:T(8,128)S(1)} %get-tuple-element.29.top, f32[8,2048]{1,0:T(8,128)S(1)} %collective-permute-done.4.below, ...), custom_call_target="tpu_custom_call", output_to_operand_aliasing={{1}: (4, {})} | custom-call | flops 20000000 | bytes 4000000 | tf_op jit(solution)/shard_map/wall_temperatures/pallas_call | solution.py:672
  (16 shorter events, 0.0 us)
Async XLA Ops:
  2.9 1.5 %collective-permute-start = (f32[16,256]{1,0:T(8,128)}, f32[16,256]{1,0:T(8,128)S(1)}, u32[]{:S(2)}, u32[]{:S(2)}) collective-permute-start(f32[16,256]{1,0:T(8,128)} %get-tuple-element.18), channel_id=1, source_target_pairs={{0,1},{2,3},{1,0},{3,2},{4,5},{6,7},{5,4},{7,6},{8,9},{10,11},{9,8... | collective-permute-start | bytes 49160 | tf_op jit(solution)/shard_map/ppermute | solution.py:71
  3.4 7.9 %copy-start.7 = (s32[4096,1]{0,1:T(1,128)S(1)}, s32[4096,1]{0,1:T(1,128)}, u32[]{:S(2)}) copy-start(s32[4096,1]{0,1:T(1,128)} %param.14) | copy-start | bytes 49156
  3.4 7.9 %copy-start.8 = (s32[4096]{0:T(1024)S(1)}, s32[4096]{0:T(1024)}, u32[]{:S(2)}) copy-start(s32[4096]{0:T(1024)} %param.15) | copy-start | bytes 49156
  3.4 7.9 %copy-start.9 = (s32[4096]{0:T(1024)S(1)}, s32[4096]{0:T(1024)}, u32[]{:S(2)}) copy-start(s32[4096]{0:T(1024)} %param.13) | copy-start | bytes 49156
  3.4 10.4 %copy-start.10 = (f32[4096]{0:T(1024)S(1)}, f32[4096]{0:T(1024)}, u32[]{:S(2)}) copy-start(f32[4096]{0:T(1024)} %param.16) | copy-start | bytes 49156
  3.4 10.4 %copy-start.11 = (f32[4096]{0:T(1024)S(1)}, f32[4096]{0:T(1024)}, u32[]{:S(2)}) copy-start(f32[4096]{0:T(1024)} %param.17) | copy-start | bytes 49156
  3.4 1.0 %collective-permute-start.1 = (f32[16,256]{1,0:T(8,128)}, f32[16,256]{1,0:T(8,128)S(1)}, u32[]{:S(2)}, u32[]{:S(2)}) collective-permute-start(f32[16,256]{1,0:T(8,128)} %get-tuple-element.19), channel_id=1, source_target_pairs={{1,2},{2,1},{5,6},{6,5},{9,10},{10,9},{13,14},{14,13},{17,18},{18,... | collective-permute-start | bytes 49160 | tf_op jit(solution)/shard_map/ppermute | solution.py:71
  4.4 0.6 copy-start.12
  5.0 0.6 copy-start.13
  7.7 6.1 %collective-permute-start.2 = (f32[16,2176]{1,0:T(8,128)}, f32[16,2176]{1,0:T(8,128)S(1)}, u32[]{:S(2)}, u32[]{:S(2)}) collective-permute-start(f32[16,2176]{1,0:T(8,128)} %get-tuple-element.21), channel_id=1, source_target_pairs={{0,4},{8,12},{16,20},{24,28},{4,0},{12,8},{20,16},{28,24},{1,5},{9... | collective-permute-start | bytes 417800 | tf_op jit(solution)/shard_map/ppermute | solution.py:71
  10.6 3.2 %collective-permute-start.3 = (f32[16,2176]{1,0:T(8,128)}, f32[16,2176]{1,0:T(8,128)S(1)}, u32[]{:S(2)}, u32[]{:S(2)}) collective-permute-start(f32[16,2176]{1,0:T(8,128)} %get-tuple-element.22), channel_id=1, source_target_pairs={{4,8},{12,16},{20,24},{8,4},{16,12},{24,20},{5,9},{13,17},{21,25},... | collective-permute-start | bytes 417800 | tf_op jit(solution)/shard_map/ppermute | solution.py:71
  13.8 1.6 %copy-start.3 = (f32[256,2048]{1,0:T(8,128)S(1)}, f32[256,2048]{1,0:T(8,128)}, u32[]{:S(2)}) copy-start(f32[256,2048]{1,0:T(8,128)} %gas.1) | copy-start | bytes 6291460
  15.4 1.6 %copy-start.4 = (f32[256,2048]{1,0:T(8,128)S(1)}, f32[256,2048]{1,0:T(8,128)}, u32[]{:S(2)}) copy-start(f32[256,2048]{1,0:T(8,128)} %speed.1) | copy-start | bytes 6291460
  17.0 0.9 copy-start.5
  17.9 36.3 %copy-start = (f32[256,2048]{1,0:T(8,128)S(1)}, f32[256,2048]{1,0:T(8,128)}, u32[]{:S(2)}) copy-start(f32[256,2048]{1,0:T(8,128)} %solid.3) | copy-start | bytes 6291460
  17.9 36.3 %copy-start.1 = (s32[256,2048]{1,0:T(8,128)S(1)}, s32[256,2048]{1,0:T(8,128)}, u32[]{:S(2)}) copy-start(s32[256,2048]{1,0:T(8,128)} %material.3) | copy-start | bytes 6291460
  54.2 9.5 %copy-start.6 = (f32[256,128]{1,0:T(8,128)S(1)}, f32[256,128]{1,0:T(8,128)}, u32[]{:S(2)}) copy-start(f32[256,128]{1,0:T(8,128)} %get-tuple-element.20.w) | copy-start | bytes 393220
  58.6 34.7 %collective-permute-start.4 = (f32[8,2048]{1,0:T(8,128)S(1)}, f32[8,2048]{1,0:T(8,128)S(1)}, u32[]{:S(2)}, u32[]{:S(2)}) collective-permute-start(f32[8,2048]{1,0:T(8,128)S(1)} %get-tuple-element.30), channel_id=1, source_target_pairs={{4,0},{8,4},{12,8},{16,12},{20,16},{24,20},{28,24},{5,1},{9,5},{13... | collective-permute-start | bytes 196616 | tf_op jit(solution)/shard_map/ppermute | solution.py:670
  59.9 33.4 %all-to-all-start.1 = ((f32[32,2,128]{2,1,0:T(2,128)}), f32[32,2,128]{2,1,0:T(2,128)S(1)}, u32[]{:S(2)}, u32[]{:S(2)}) async-start(f32[32,2,128]{2,1,0:T(2,128)} %get-tuple-element.28), calls=%async_computation.1 | async-start | bytes 65536 | tf_op jit(solution)/shard_map/all_to_all | solution.py:669
  63.7 1.6 %copy-start.2 = (s32[256,2048]{1,0:T(8,128)S(1)}, s32[256,2048]{1,0:T(8,128)}, u32[]{:S(2)}) copy-start(s32[256,2048]{1,0:T(8,128)} %material.3) | copy-start | bytes 6291460

commit v2 on v1

--- a/solution.py
+++ b/solution.py
@@ -270,7 +270,7 @@
             s1[ct, pl.ds(ROWS + r0, ROWS), :] = new
         return carry
 
-    lax.fori_loop(0, rows // ROWS, first, 0)
+    lax.fori_loop(0, rows // ROWS, first, 0, unroll=4)
 
     def second(i, carry):
         r0 = pl.multiple_of(i * ROWS, ROWS)
@@ -286,7 +286,7 @@
             )
         return carry
 
-    lax.fori_loop(0, rows // ROWS, second, 0)
+    lax.fori_loop(0, rows // ROWS, second, 0, unroll=4)
     outs = [
         pltpu.make_async_copy(tab.at[pl.ds(ct * rows, rows)], out.at[:, pl.ds(ct * LANES, LANES)], sem.at[0, ct])
         for ct in range(nt)
@@ -345,7 +345,7 @@
         copy.wait()
 
 
-def strip_kernel(per_owner, recv, ra, rb, w, solid, material, top_ref, up_ref, ret_ref, lhs, rhs, dep, src, tabu):
+def strip_kernel(per_owner, recv, ra, rb, w, solid, material, token, top_ref, up_ref, ret_ref, lhs, rhs, dep, src, tabu):
     devices = recv.shape[0]
     cols = solid.shape[1]
     nt = cols // LANES
@@ -413,64 +413,80 @@
             ret_ref[d, q : q + 1, :] = jnp.sum(jnp.where(highs == hi, x, 0.0), axis=0, keepdims=True)
 
 
-def bulk_kernel(solid, material, w, ra, rb, out, ua, ub, ka, kb, k0, mat, sem):
+def bulk_kernel(first, last_half, solid, material, w, ra, rb, after, *rest):
+    out, ua, ub, ka, kb, k0, k1, mat, sem = rest[1:] if last_half else rest[:1] + rest[2:]
     rows, cols = solid.shape
+    half = mat.shape[1] - ROWS
+    top = first - ROWS if last_half else first
+    count = half + ROWS
     nt = cols // LANES
     copies = []
     for ct in range(nt):
         at = pl.ds(ct * LANES, LANES)
-        copies.append(pltpu.make_async_copy(solid.at[:, at], ua.at[ct, pl.ds(ROWS, rows)], sem.at[0, ct]))
-        copies.append(pltpu.make_async_copy(material.at[:, at], mat.at[ct], sem.at[1, ct]))
+        copies.append(
+            pltpu.make_async_copy(solid.at[pl.ds(top, count), at], ua.at[ct, pl.ds(ROWS, count)], sem.at[0, ct])
+        )
+        copies.append(pltpu.make_async_copy(material.at[pl.ds(top, count), at], mat.at[ct], sem.at[1, ct]))
     for copy in copies:
         copy.start()
-    uh, kh = halo_tiles(w[...])
-    ua[nt, ROWS : ROWS + rows, :] = uh
+    uh, kh = halo_tiles(w[top : top + count, :])
+    ua[nt, ROWS : ROWS + count, :] = uh
     k0[nt] = kh
-    ka[nt, ROWS : ROWS + rows, :] = kh * jnp.exp(SOFTEN * uh)
+    ka[nt, ROWS : ROWS + count, :] = kh * jnp.exp(SOFTEN * uh)
     is_even = even("passage")
     zero = jnp.zeros((ROWS, LANES), F32)
     for ct in range(nt + 1):
         at = slice(ct * LANES, (ct + 1) * LANES)
-        below = jnp.where(is_even, ra[1:2, at], rb[1:2, at])
-        below_k = jnp.where(is_even, ra[9:10, at], rb[9:10, at]) * jnp.exp(SOFTEN * below)
+        if last_half:
+            below = jnp.where(is_even, ra[1:2, at], rb[1:2, at])
+            below_k = jnp.where(is_even, ra[9:10, at], rb[9:10, at]) * jnp.exp(SOFTEN * below)
         for u, k in ((ua, ka), (ub, kb)):
             u[ct, 0:ROWS, :] = zero
             k[ct, 0:ROWS, :] = zero
-            u[ct, ROWS + rows : ROWS + rows + 1, :] = below
-            k[ct, ROWS + rows : ROWS + rows + 1, :] = below_k
+            if last_half:
+                u[ct, ROWS + count : ROWS + count + 1, :] = below
+                k[ct, ROWS + count : ROWS + count + 1, :] = below_k
+            else:
+                u[ct, ROWS + count : 2 * ROWS + count, :] = zero
+                k[ct, ROWS + count : 2 * ROWS + count, :] = zero
     for copy in copies:
         copy.wait()
+    lane = iota((ROWS, LANES), 1)
+    edge = lane == LANES - 1
 
     def begin(i, carry):
         r0 = pl.multiple_of(i * ROWS, ROWS)
+        bases = []
         for ct in range(nt):
             base = base_conductivity(mat[ct, pl.ds(r0, ROWS), :])
             k0[ct, pl.ds(r0, ROWS), :] = base
             ka[ct, pl.ds(ROWS + r0, ROWS), :] = base * jnp.exp(SOFTEN * ua[ct, pl.ds(ROWS + r0, ROWS), :])
+            bases.append(base)
+        bases.append(k0[nt, pl.ds(r0, ROWS), :])
+        turned = [pltpu.roll(x, LANES - 1, 1) for x in bases]
+        for ct in range(nt + 1):
+            k1[ct, pl.ds(r0, ROWS), :] = jnp.where(edge, turned[(ct + 1) % (nt + 1)], turned[ct])
         return carry
 
-    lax.fori_loop(0, rows // ROWS, begin, 0)
-    lane = iota((ROWS, LANES), 1)
+    lax.fori_loop(0, count // ROWS, begin, 0, unroll=2)
     for step in range(SUBSTEPS):
-        last = step == SUBSTEPS - 1
+        final = step == SUBSTEPS - 1
         u, k, nu, nk = (ua, ka, ub, kb) if step % 2 == 0 else (ub, kb, ua, ka)
 
-        def body(i, carry, u=u, k=k, nu=nu, nk=nk, last=last):
+        def body(i, carry, u=u, k=k, nu=nu, nk=nk, final=final):
             r0 = pl.multiple_of(i * ROWS, ROWS)
             at = pl.ds(ROWS + r0, ROWS)
             north, south = pl.ds(ROWS - 1 + r0, ROWS), pl.ds(ROWS + 1 + r0, ROWS)
             here = [u[ct, at, :] for ct in range(nt + 1)]
             cond = [k[ct, at, :] for ct in range(nt + 1)]
             turned = [pltpu.roll(x, LANES - 1, 1) for x in here]
-            turned_k = [pltpu.roll(x, LANES - 1, 1) for x in cond]
-            edge = lane == LANES - 1
             across = []
             for ct in range(nt + 1):
-                after = jnp.where(edge, turned[(ct + 1) % (nt + 1)], turned[ct])
-                after_k = jnp.where(edge, turned_k[(ct + 1) % (nt + 1)], turned_k[ct])
-                across.append((cond[ct] + after_k) * (after - here[ct]))
+                nearby = jnp.where(edge, turned[(ct + 1) % (nt + 1)], turned[ct])
+                nearby_k = k1[ct, pl.ds(r0, ROWS), :] * jnp.exp(SOFTEN * nearby)
+                across.append((cond[ct] + nearby_k) * (nearby - here[ct]))
             back = [pltpu.roll(x, 1, 1) for x in across]
-            for ct in range(nt if last else nt + 1):
+            for ct in range(nt if final else nt + 1):
                 flux = across[ct] - jnp.where(lane == 0, back[ct - 1], back[ct])
                 flux = flux + (cond[ct] + k[ct, north, :]) * (u[ct, north, :] - here[ct])
                 flux = flux + (cond[ct] + k[ct, south, :]) * (u[ct, south, :] - here[ct])
@@ -479,18 +495,25 @@
                     flux = jnp.where(base > 0, flux, 0.0)
                 new = here[ct] + 0.5 * SOLID_STEP * flux
                 nu[ct, at, :] = new
-                if not last:
+                if not final:
                     nk[ct, at, :] = base * jnp.exp(SOFTEN * new)
             return carry
 
-        lax.fori_loop(0, rows // ROWS, body, 0)
+        lax.fori_loop(0, count // ROWS, body, 0, unroll=4)
     final = ua if SUBSTEPS % 2 == 0 else ub
+    skip = ROWS if last_half else 0
     outs = [
-        pltpu.make_async_copy(final.at[ct, pl.ds(ROWS, rows)], out.at[:, pl.ds(ct * LANES, LANES)], sem.at[0, ct])
+        pltpu.make_async_copy(
+            final.at[ct, pl.ds(ROWS + skip, half)],
+            out.at[pl.ds(first, half), pl.ds(ct * LANES, LANES)],
+            sem.at[0, ct],
+        )
         for ct in range(nt)
     ]
     for copy in outs:
         copy.start()
+    if not last_half:
+        rest[1][...] = zero
     for copy in outs:
         copy.wait()
 
@@ -551,6 +574,7 @@
     one, two = pl.pallas_call(
         pack_columns,
         grid=(1,),
+        compiler_params=params(60),
         in_specs=[left, right] * 4,
         out_specs=[column, column],
         out_shape=[shape((16, rows))] * 2,
@@ -567,6 +591,7 @@
     w, ra, rb = pl.pallas_call(
         pack_rows,
         grid=(1,),
+        compiler_params=params(60),
         in_specs=[column, column] + [tall(ROWS, 0), tall(ROWS, rows // ROWS - 1)] * 4,
         out_specs=[full, band, band],
         out_shape=[shape((rows, LANES)), shape((16, wide)), shape((16, wide))],
@@ -590,7 +615,7 @@
             VMEM((2 * table, faces), BF16),
             VMEM((LANES, faces), BF16),
         ],
-        compiler_params=params(24),
+        compiler_params=params(60),
         name="find_slots",
         cost_estimate=cost(20000000, 1000000),
     )(owner, surface, cell)
@@ -612,7 +637,7 @@
             VMEM((part, LANES + 32), F32),
             pltpu.SemaphoreType.DMA((2, nt)),
         ],
-        compiler_params=params(40),
+        compiler_params=params(60),
         name="gas_and_heat",
         cost_estimate=cost(60000000, 40000000),
     )(
@@ -621,21 +646,28 @@
     )
     recv = lax.all_to_all(route, ("passage", "tile"), 0, 0, tiled=True)
 
-    bulk = pl.pallas_call(
-        bulk_kernel,
-        in_specs=[whole(pl.ANY)] * 2 + [whole()] * 3,
-        out_specs=whole(pl.ANY),
-        out_shape=shape((rows, cols)),
-        scratch_shapes=[VMEM((nt + 1, rows + 2 * ROWS, LANES), F32)] * 4
-        + [
-            VMEM((nt + 1, rows, LANES), F32),
-            VMEM((nt, rows, LANES), jnp.int32),
-            pltpu.SemaphoreType.DMA((2, nt)),
-        ],
-        compiler_params=params(40),
-        name="solid_bulk",
-        cost_estimate=cost(60000000, 40000000),
-    )(solid, material, w, ra, rb)
+    half = rows // 2 // ROWS * ROWS
+
+    def bulk_half(first, count, after, whole_so_far):
+        last_half = first > 0
+        return pl.pallas_call(
+            functools.partial(bulk_kernel, first, last_half),
+            in_specs=[whole(pl.ANY)] * 2 + [whole()] * 3 + [whole(pl.ANY)] * (2 if last_half else 1),
+            out_specs=[whole(pl.ANY)] + ([] if last_half else [whole()]),
+            out_shape=[shape((rows, cols))] + ([] if last_half else [shape((ROWS, LANES))]),
+            input_output_aliases={6: 0} if last_half else {},
+            scratch_shapes=[VMEM((nt + 1, count + 3 * ROWS, LANES), F32)] * 4
+            + [VMEM((nt + 1, count + ROWS, LANES), F32)] * 2
+            + [
+                VMEM((nt, count + ROWS, LANES), jnp.int32),
+                pltpu.SemaphoreType.DMA((2, nt)),
+            ],
+            compiler_params=params(60),
+            name="solid_bulk",
+            cost_estimate=cost(60000000, 30000000),
+        )(solid, material, w, ra, rb, after, *([whole_so_far] if last_half else []))
+
+    bulk, token = bulk_half(0, half, gas_next, None)
 
     slots = table * LANES
     top, up, ret = pl.pallas_call(
@@ -648,6 +680,7 @@
             pl.BlockSpec((16, LANES), lambda i: (0, 0)),
             tall(16, 0),
             tall(16, 0),
+            pl.BlockSpec((ROWS, LANES), lambda i: (0, 0)),
         ],
         out_specs=[
             pl.BlockSpec((ROWS, cols), lambda i: (0, 0)),
@@ -662,13 +695,14 @@
             VMEM((ROWS, wide), F32),
             VMEM((2 * nt, LANES), F32),
         ],
-        compiler_params=params(32),
+        compiler_params=params(60),
         name="solid_strip",
         cost_estimate=cost(20000000, 4000000),
-    )(recv, ra, rb, w, solid, material)
+    )(recv, ra, rb, w, solid, material, token)
     ret = lax.all_to_all(ret, ("passage", "tile"), 0, 0, tiled=True)
     below = lax.ppermute(up, "passage", [(i + 1, i) for i in range(passages - 1)])
 
+    (bulk,) = bulk_half(half, rows - half, top, bulk)
     wall, solid_next = pl.pallas_call(
         finish_kernel,
         in_specs=[whole()] * 4 + [whole(pl.ANY)],
@@ -680,7 +714,7 @@
             VMEM((ROWS, cols), F32),
             pltpu.SemaphoreType.DMA((2,)),
         ],
-        compiler_params=params(24),
+        compiler_params=params(60),
         name="wall_temperatures",
         cost_estimate=cost(20000000, 4000000),
     )(ret, slot, top, below, bulk)

time: 96.5 us -> 84.8 us (0.88)
  blocking collectives: 21.2 us -> 0 us
  starting transfers between devices: 9.82 us -> 25.7 us
  local copies, waits for them, and re-layouts: 6.9 us -> 3.76 us
  Pallas kernels: 55.8 us -> 53.4 us
  waiting for transfers between devices: 1.51 us -> 0.41 us
    all_to_all x1 -> x0, blocking collectives: 21.2 us -> none  [shards(): recv = lax.all_to_all(route, ('passage', 'tile'), 0, 0, tiled=True)]
    all_to_all x0 -> x1, starting transfers between devices: none -> 12.8 us  [shards(): recv = lax.all_to_all(route, ('passage', 'tile'), 0, 0, tiled=True)]
    pallas_call x3 -> x4, Pallas kernels: 32.4 us -> 27.7 us  [the longest x2 23.3 us: bulk_half(): pl.pallas_call(functools.partial(bulk_kernel, first, last_half), in_specs...]
    all_to_all x1, starting transfers between devices: 3.78 us -> 6.98 us  [shards(): ret = lax.all_to_all(ret, ('passage', 'tile'), 0, 0, tiled=True)]
    unnamed x28 -> x14, local copies, waits for them, and re-layouts: 6.9 us -> 3.76 us
    pallas_call x1, Pallas kernels: 1.27 us -> 2.64 us  [shards(): pl.pallas_call(functools.partial(find_slots, devices, per_owner, rows, co...]
    pallas_call x1, Pallas kernels: 15.1 us -> 13.9 us  [shards(): pl.pallas_call(functools.partial(gas_kernel, tiles, per_owner), in_specs=...]
    pallas_call x1, Pallas kernels: 4.41 us -> 5.58 us  [shards(): pl.pallas_call(functools.partial(strip_kernel, per_owner), grid=(1,), in_...]
  transfers between devices with their start and end apart: 6 -> 7, of which waited for: 2 -> 1; matrix products, arithmetic and copies ran while one was open for 0% -> 0% of each run, Pallas kernels for 30% -> 31%
where the time goes in v2:
time: 84.8 us; the launch traced here: 84 us
  Pallas kernels  53.4 us (63%)
  starting transfers between devices  25.7 us (30%)
  local copies, waits for them, and re-layouts  3.76 us (4%)
    pallas_call x2, Pallas kernels, bulk_half(): pl.pallas_call(functools.partial(bulk_kernel, first, last_half), in_specs...  23.3 us
    pallas_call x1, Pallas kernels, shards(): pl.pallas_call(functools.partial(gas_kernel, tiles, per_owner), in_specs=...  13.9 us
    all_to_all x1, starting transfers between devices, shards(): recv = lax.all_to_all(route, ('passage', 'tile'), 0, 0, tiled=True)  12.8 us
    all_to_all x1, starting transfers between devices, shards(): ret = lax.all_to_all(ret, ('passage', 'tile'), 0, 0, tiled=True)  6.98 us
    pallas_call x1, Pallas kernels, shards(): pl.pallas_call(functools.partial(strip_kernel, per_owner), grid=(1,), in_...  5.58 us
    unnamed x14, local copies, waits for them, and re-layouts  3.76 us
    pallas_call x1, Pallas kernels, shards(): pl.pallas_call(finish_kernel, in_specs=[whole()] * 4 + [whole(pl.ANY)], o...  3.56 us
    ppermute x2, starting transfers between devices, run(): lax.ppermute(one, axis, both(first))  3.31 us
  transfers between devices with their start and end apart: 7, of which 1 were waited for; matrix products, arithmetic and copies ran while one was open for 0% of the time, Pallas kernels for 31%

profile of v2, /device:TPU:0, one launch (start us, length us, event | category | flops | bytes accessed | tf_op | source)
XLA Modules:
  0.0 84.0 jit_solution(11738249024291900839)
XLA Ops:
  0.6 2.3 %pack_columns.1 = (f32[16,256]{1,0:T(8,128)}, f32[16,256]{1,0:T(8,128)}) custom-call(f32[256,2048]{1,0:T(8,128)} %gas.1, f32[256,2048]{1,0:T(8,128)} %gas.1, f32[256,2048]{1,0:T(8,128)} %speed.1, f32[256,2048]{1,0:T(8,128)} %speed.1, f32[256,2048]{1,0:T(8,128)} %solid.5, f32[256,2048]{1,0:T(8,128)} %solid.5, s32[256,2048]{1,0:T(8,128)} %material.5, ...), custom_call_target="tpu_custom_call" | custom-call | flops 1000000 | bytes 1048576 | tf_op jit(solution)/shard_map/pack_columns/pallas_call | solution.py:574
  2.9 0.5 collective-permute-start
  3.4 0.7 collective-permute-start.1
  4.0 0.4 collective-permute-done.one
  4.4 0.0 collective-permute-done.1.two
  4.4 0.6 copy-done.5
  5.0 0.6 copy-done.6
  5.6 2.1 %pack_rows.1 = (f32[256,128]{1,0:T(8,128)}, f32[16,2176]{1,0:T(8,128)}, f32[16,2176]{1,0:T(8,128)}) custom-call(f32[16,256]{1,0:T(8,128)} %copy-done.5, f32[16,256]{1,0:T(8,128)} %copy-done.6, f32[256,2048]{1,0:T(8,128)} %gas.1, f32[256,2048]{1,0:T(8,128)} %gas.1, f32[256,2048]{1,0:T(8,128)} %speed.1, f32[256,2048]{1,0:T(8,128)} %speed.1, ...), custom_call_target="tpu_custom_call" | custom-call | flops 1000000 | bytes 524288 | tf_op jit(solution)/shard_map/pack_rows/pallas_call | solution.py:591
  7.7 2.9 %collective-permute-start.2 = (f32[16,2176]{1,0:T(8,128)}, f32[16,2176]{1,0:T(8,128)S(1)}, u32[]{:S(2)}, u32[]{:S(2)}) collective-permute-start(f32[16,2176]{1,0:T(8,128)} %get-tuple-element.23), channel_id=1, source_target_pairs={{0,4},{8,12},{16,20},{24,28},{4,0},{12,8},{20,16},{28,24},{1,5},{9... | collective-permute-start | bytes 417800 | tf_op jit(solution)/shard_map/ppermute | solution.py:71
  10.6 0.7 collective-permute-start.3
  11.2 2.6 %find_slots.1 = (s32[32,128]{1,0:T(8,128)}, s32[32,128]{1,0:T(8,128)}, f32[64,128]{1,0:T(8,128)}) custom-call(s32[32,128]{1,0:T(8,128)} %bitcast.7, s32[32,128]{1,0:T(8,128)} %bitcast.9, s32[32,128]{1,0:T(8,128)} %bitcast.11), custom_call_target="tpu_custom_call" | custom-call | flops 20000000 | bytes 1000000 | tf_op jit(solution)/shard_map/find_slots/pallas_call | solution.py:608
  13.9 0.0 collective-permute-done.2.ra
  13.9 0.0 collective-permute-done.3.rb
  13.9 0.0 copy-start.1
  13.9 0.6 copy-done
  14.5 0.1 copy-done.1
  14.6 13.9 %gas_and_heat.1 = (f32[256,2048]{1,0:T(8,128)}, f32[32,8,128]{2,1,0:T(8,128)}) custom-call(f32[256,2048]{1,0:T(8,128)} %gas.1, f32[256,2048]{1,0:T(8,128)} %speed.1, f32[256,128]{1,0:T(8,128)} %get-tuple-element.22.w, f32[16,2176]{1,0:T(8,128)} %copy-done, f32[16,2176]{1,0:T(8,128)} %copy-done.1, s32[4096]{0:T(1024)} %bitcast.15, s32[32,128]{1,0:T(8,128)} %bitcast.12, ...), custom_call_target="tpu_custom_call" | custom-call | flops 60000000 | bytes 40000000 | tf_op jit(solution)/shard_map/gas_and_heat/pallas_call | solution.py:624
  28.5 12.8 %all-to-all-start = ((f32[32,8,128]{2,1,0:T(8,128)}), f32[32,8,128]{2,1,0:T(8,128)S(1)}, u32[]{:S(2)}, u32[]{:S(2)}) async-start(f32[32,8,128]{2,1,0:T(8,128)} %get-tuple-element.29), calls=%async_computation | async-start | bytes 262144 | tf_op jit(solution)/shard_map/all_to_all | solution.py:647
  41.3 12.0 %solid_bulk.2 = (f32[256,2048]{1,0:T(8,128)}, f32[8,128]{1,0:T(8,128)}) custom-call(f32[256,2048]{1,0:T(8,128)} %solid.5, s32[256,2048]{1,0:T(8,128)} %material.5, f32[256,128]{1,0:T(8,128)} %get-tuple-element.22.w, f32[16,2176]{1,0:T(8,128)} %copy-done, f32[16,2176]{1,0:T(8,128)} %copy-done.1, f32[256,2048]{1,0:T(8,128)} %get-tuple-element.17.after), custom_call_target="tpu_custom_call" | custom-call | flops 60000000 | bytes 30000000 | tf_op jit(solution)/shard_map/solid_bulk/pallas_call | solution.py:653
  53.3 0.0 all-to-all-done.recv
  53.3 0.0 copy-start.2
  53.3 0.7 copy-done.2
  54.0 5.6 %solid_strip.1 = (f32[8,2048]{1,0:T(8,128)}, f32[8,2048]{1,0:T(8,128)}, f32[32,2,128]{2,1,0:T(2,128)}) custom-call(f32[32,8,128]{2,1,0:T(8,128)} %copy-done.2, f32[16,2176]{1,0:T(8,128)} %copy-done, f32[16,2176]{1,0:T(8,128)} %copy-done.1, f32[256,128]{1,0:T(8,128)} %get-tuple-element.22.w, f32[256,2048]{1,0:T(8,128)} %solid.5, s32[256,2048]{1,0:T(8,128)} %material.5, ...), custom_call_target="tpu_custom_call" | custom-call | flops 20000000 | bytes 4000000 | tf_op jit(solution)/shard_map/solid_strip/pallas_call | solution.py:673
  59.6 1.3 %collective-permute-start.4 = (f32[8,2048]{1,0:T(8,128)}, f32[8,2048]{1,0:T(8,128)S(1)}, u32[]{:S(2)}, u32[]{:S(2)}) collective-permute-start(f32[8,2048]{1,0:T(8,128)} %get-tuple-element.33), channel_id=1, source_target_pairs={{4,0},{8,4},{12,8},{16,12},{20,16},{24,20},{28,24},{5,1},{9,5},{13... | collective-permute-start | bytes 196616 | tf_op jit(solution)/shard_map/ppermute | solution.py:703
  60.9 7.0 %all-to-all-start.1 = ((f32[32,2,128]{2,1,0:T(2,128)}), f32[32,2,128]{2,1,0:T(2,128)S(1)}, u32[]{:S(2)}, u32[]{:S(2)}) async-start(f32[32,2,128]{2,1,0:T(2,128)} %get-tuple-element.31), calls=%async_computation.1 | async-start | bytes 65536 | tf_op jit(solution)/shard_map/all_to_all | solution.py:702
  67.8 11.4 %solid_bulk.3.solid = f32[256,2048]{1,0:T(8,128)} custom-call(f32[256,2048]{1,0:T(8,128)} %solid.5, s32[256,2048]{1,0:T(8,128)} %material.5, f32[256,128]{1,0:T(8,128)} %get-tuple-element.22.w, f32[16,2176]{1,0:T(8,128)} %copy-done, f32[16,2176]{1,0:T(8,128)} %copy-done.1, f32[8,2048]{1,0:T(8,128)} %get-tuple-element.32.after.top, ...), custom_call_target="tpu_custom_call", output_to_operand_aliasing={{}: (6, {})} | custom-call | flops 60000000 | bytes 30000000 | tf_op jit(solution)/shard_map/solid_bulk/pallas_call | solution.py:653
  79.2 0.0 all-to-all-done.1.recv
  79.2 0.0 copy-start.3
  79.2 0.0 collective-permute-done.4.below
  79.3 0.6 copy-done.3
  79.9 0.6 copy-done.4
  80.5 3.6 %wall_temperatures.1 = (f32[32,128]{1,0:T(8,128)}, f32[256,2048]{1,0:T(8,128)}) custom-call(f32[32,2,128]{2,1,0:T(2,128)} %copy-done.3, s32[32,128]{1,0:T(8,128)} %get-tuple-element.26.slot, f32[8,2048]{1,0:T(8,128)} %get-tuple-element.32.after.top, f32[8,2048]{1,0:T(8,128)} %copy-done.4, f32[256,2048]{1,0:T(8,128)} %solid_bulk.3.solid), custom_call_target="tpu_custom_call", output_to_operand_aliasing={{1}: (4, {})} | custom-call | flops 20000000 | bytes 4000000 | tf_op jit(solution)/shard_map/wall_temperatures/pallas_call | solution.py:706
  (4 shorter events, 0.0 us)
Async XLA Ops:
  2.9 1.5 %collective-permute-start = (f32[16,256]{1,0:T(8,128)}, f32[16,256]{1,0:T(8,128)S(1)}, u32[]{:S(2)}, u32[]{:S(2)}) collective-permute-start(f32[16,256]{1,0:T(8,128)} %get-tuple-element.20), channel_id=1, source_target_pairs={{0,1},{2,3},{1,0},{3,2},{4,5},{6,7},{5,4},{7,6},{8,9},{10,11},{9,8... | collective-permute-start | bytes 49160 | tf_op jit(solution)/shard_map/ppermute | solution.py:71
  3.4 1.1 %collective-permute-start.1 = (f32[16,256]{1,0:T(8,128)}, f32[16,256]{1,0:T(8,128)S(1)}, u32[]{:S(2)}, u32[]{:S(2)}) collective-permute-start(f32[16,256]{1,0:T(8,128)} %get-tuple-element.21), channel_id=1, source_target_pairs={{1,2},{2,1},{5,6},{6,5},{9,10},{10,9},{13,14},{14,13},{17,18},{18,... | collective-permute-start | bytes 49160 | tf_op jit(solution)/shard_map/ppermute | solution.py:71
  4.4 0.6 copy-start.5
  5.0 0.6 copy-start.6
  7.7 6.2 %collective-permute-start.2 = (f32[16,2176]{1,0:T(8,128)}, f32[16,2176]{1,0:T(8,128)S(1)}, u32[]{:S(2)}, u32[]{:S(2)}) collective-permute-start(f32[16,2176]{1,0:T(8,128)} %get-tuple-element.23), channel_id=1, source_target_pairs={{0,4},{8,12},{16,20},{24,28},{4,0},{12,8},{20,16},{28,24},{1,5},{9... | collective-permute-start | bytes 417800 | tf_op jit(solution)/shard_map/ppermute | solution.py:71
  10.6 3.3 %collective-permute-start.3 = (f32[16,2176]{1,0:T(8,128)}, f32[16,2176]{1,0:T(8,128)S(1)}, u32[]{:S(2)}, u32[]{:S(2)}) collective-permute-start(f32[16,2176]{1,0:T(8,128)} %get-tuple-element.24), channel_id=1, source_target_pairs={{4,8},{12,16},{20,24},{8,4},{16,12},{24,20},{5,9},{13,17},{21,25},... | collective-permute-start | bytes 417800 | tf_op jit(solution)/shard_map/ppermute | solution.py:71
  13.9 0.7 copy-start
  13.9 0.7 copy-start.1
  28.5 24.8 %all-to-all-start = ((f32[32,8,128]{2,1,0:T(8,128)}), f32[32,8,128]{2,1,0:T(8,128)S(1)}, u32[]{:S(2)}, u32[]{:S(2)}) async-start(f32[32,8,128]{2,1,0:T(8,128)} %get-tuple-element.29), calls=%async_computation | async-start | bytes 262144 | tf_op jit(solution)/shard_map/all_to_all | solution.py:647
  53.3 0.7 copy-start.2
  59.6 19.7 %collective-permute-start.4 = (f32[8,2048]{1,0:T(8,128)}, f32[8,2048]{1,0:T(8,128)S(1)}, u32[]{:S(2)}, u32[]{:S(2)}) collective-permute-start(f32[8,2048]{1,0:T(8,128)} %get-tuple-element.33), channel_id=1, source_target_pairs={{4,0},{8,4},{12,8},{16,12},{20,16},{24,20},{28,24},{5,1},{9,5},{13... | collective-permute-start | bytes 196616 | tf_op jit(solution)/shard_map/ppermute | solution.py:703
  60.9 18.4 %all-to-all-start.1 = ((f32[32,2,128]{2,1,0:T(2,128)}), f32[32,2,128]{2,1,0:T(2,128)S(1)}, u32[]{:S(2)}, u32[]{:S(2)}) async-start(f32[32,2,128]{2,1,0:T(2,128)} %get-tuple-element.31), calls=%async_computation.1 | async-start | bytes 65536 | tf_op jit(solution)/shard_map/all_to_all | solution.py:702
  79.2 0.6 copy-start.3
  79.8 0.6 copy-start.4

commit v3 on v2

--- a/solution.py
+++ b/solution.py
@@ -11,6 +11,8 @@
 DIFFUSE = 0.05
 SOLID_STEP = 0.1
 SOFTEN = 0.08
+SCALE = SOFTEN * 1.4426950408889634
+SHARE = 0.5 * SOLID_STEP
 LANES = 128
 ROWS = 8
 ROUTE_ROWS = 8
@@ -22,7 +24,7 @@
 
 
 def params(mib):
-    return pltpu.CompilerParams(vmem_limit_bytes=mib * MIB)
+    return pltpu.CompilerParams(vmem_limit_bytes=int(mib * MIB))
 
 
 def whole(space=pltpu.VMEM):
@@ -33,11 +35,11 @@
     return lax.broadcasted_iota(jnp.int32, shape, dim)
 
 
-def base_conductivity(material):
+def base_conductivity(material, share=1.0):
     return jnp.where(
         material == 0,
-        jnp.float32(1.0),
-        jnp.where(material == 1, jnp.float32(0.3), jnp.float32(0.08)),
+        jnp.float32(share),
+        jnp.where(material == 1, jnp.float32(0.3 * share), jnp.float32(0.08 * share)),
     )
 
 
@@ -73,24 +75,41 @@
     return run
 
 
-def pack_columns(gl, gr, sl, sr, ul, ur, ml, mr, one_ref, two_ref):
-    lane = iota(gl.shape, 1)
+def pack_columns(gas, speed, solid, material, one_ref, two_ref, top_f, top_m, tiles, tile_m, sem):
+    size, cols = gas.shape
+    fields = (gas, speed, solid)
+    ends = (pl.ds(0, LANES), pl.ds(cols - LANES, LANES))
+    bands = (pl.ds(0, ROWS), pl.ds(size - ROWS, ROWS))
+    tall, flat = [], []
+    for e in range(2):
+        for f in range(3):
+            tall.append(pltpu.make_async_copy(fields[f].at[:, ends[e]], tiles.at[2 * f + e], sem.at[0, 4 * e + f]))
+        tall.append(pltpu.make_async_copy(material.at[:, ends[e]], tile_m.at[e], sem.at[0, 4 * e + 3]))
+    for e in range(2):
+        for f in range(3):
+            flat.append(pltpu.make_async_copy(fields[f].at[bands[e], :], top_f.at[2 * f + e], sem.at[1, 4 * e + f]))
+        flat.append(pltpu.make_async_copy(material.at[bands[e], :], top_m.at[e], sem.at[1, 4 * e + 3]))
+    for copy in tall + flat:
+        copy.start()
+    for copy in tall:
+        copy.wait()
+    lane = iota((size, LANES), 1)
     head = jnp.where(
         lane < 4,
-        ul[...],
+        tiles[4],
         jnp.where(
             lane < 8,
-            pltpu.roll(base_conductivity(ml[...]), 4, 1),
-            jnp.where(lane < 10, pltpu.roll(gl[...], 8, 1), pltpu.roll(sl[...], 10, 1)),
+            pltpu.roll(base_conductivity(tile_m[0]), 4, 1),
+            jnp.where(lane < 10, pltpu.roll(tiles[0], 8, 1), pltpu.roll(tiles[2], 10, 1)),
         ),
     )
     tail = jnp.where(
         lane >= 124,
-        ur[...],
+        tiles[5],
         jnp.where(
             lane >= 120,
-            pltpu.roll(base_conductivity(mr[...]), 124, 1),
-            jnp.where(lane >= 118, pltpu.roll(gr[...], 120, 1), pltpu.roll(sr[...], 118, 1)),
+            pltpu.roll(base_conductivity(tile_m[1]), 124, 1),
+            jnp.where(lane >= 118, pltpu.roll(tiles[1], 120, 1), pltpu.roll(tiles[3], 118, 1)),
         ),
     )
     head = head.T[0:16]
@@ -98,6 +117,8 @@
     is_even = even("tile")
     one_ref[...] = jnp.where(is_even, tail, head)
     two_ref[...] = jnp.where(is_even, head, tail)
+    for copy in flat:
+        copy.wait()
 
 
 def halo_tiles(w):
@@ -122,7 +143,7 @@
     return gas, speed
 
 
-def pack_rows(one, two, gt, gb, st, sb, ut, ub, mt, mb, w_ref, a_ref, b_ref, wt):
+def pack_rows(one, two, edges, edge_m, w_ref, a_ref, b_ref, wt):
     is_even = even("tile")
     wt[...] = jnp.zeros_like(wt)
     wt[0:16, :] = jnp.where(is_even, one[...], two[...])
@@ -130,9 +151,10 @@
     w = wt[...].T
     w_ref[...] = w
     size = w.shape[0]
-    wide = gt.shape[1] + LANES
-
-    def rows(g, s, u, m, part, step, keep):
+    wide = edges.shape[2] + LANES
+
+    def rows(e, part, step):
+        g, s, u, m = edges.at[e], edges.at[2 + e], edges.at[4 + e], edge_m.at[e]
         uh, kh = halo_tiles(part)
         gh, sh = gas_halo_tiles(part)
         g = jnp.concatenate([g[...], gh], axis=1)
@@ -147,13 +169,13 @@
 
     row = iota((ROWS, wide), 0)
     zero = jnp.zeros((ROWS, wide), F32)
-    g, partial, u, k = rows(gt, st, ut, mt, w[0:ROWS], ROWS - 1, 0)
+    g, partial, u, k = rows(0, w[0:ROWS], ROWS - 1)
 
     def first_two(x, y):
         return jnp.where(row == 0, x, jnp.where(row == 1, pltpu.roll(y, 1, 0), zero))
 
     up = (first_two(g, u), first_two(partial, k))
-    g, partial, u, k = rows(gb, sb, ub, mb, w[size - ROWS : size], 1, 0)
+    g, partial, u, k = rows(1, w[size - ROWS : size], 1)
 
     def last_rows(x, y):
         return jnp.where(row == 0, pltpu.roll(x, 1, 0), y)
@@ -211,23 +233,22 @@
 
 def gas_kernel(
     tiles_across, per_owner, gas, speed, w, ra, rb, rowidx, cell, owner, surface, slot, film, wall, idx,
-    out, route, gx, sx, s1, tab, stage, lhs, rhs, sums, sem,
+    out, route, gx, sx, sh, s1, tab, final, stage, lhs, rhs, sums, sem,
 ):
     rows, cols = gas.shape
     nt = cols // LANES
     devices = route.shape[0]
     blocks = owner.shape[0]
     table = idx.shape[0]
-    copies = []
+    copies = [pltpu.make_async_copy(speed, sx, sem.at[1, 0])]
     for ct in range(nt):
         at = pl.ds(ct * LANES, LANES)
         copies.append(pltpu.make_async_copy(gas.at[:, at], gx.at[ct, pl.ds(ROWS, rows)], sem.at[0, ct]))
-        copies.append(pltpu.make_async_copy(speed.at[:, at], sx.at[ct], sem.at[1, ct]))
     for copy in copies:
         copy.start()
-    gh, sh = gas_halo_tiles(w[...])
+    gh, speed_halo = gas_halo_tiles(w[...])
     gx[nt, ROWS : ROWS + rows, :] = gh
-    sx[nt] = sh
+    sh[...] = speed_halo
     is_even = even("passage")
     place = lax.axis_index("passage")
     in_top = jnp.where(place > 0, 1.0, 0.0)
@@ -263,7 +284,7 @@
         for ct in range(nt + 1):
             north = gx[ct, pl.ds(ROWS - 1 + r0, ROWS), :]
             south = gx[ct, pl.ds(ROWS + 1 + r0, ROWS), :]
-            s = sx[ct, pl.ds(r0, ROWS), :]
+            s = sh[pl.ds(r0, ROWS), :] if ct == nt else sx[pl.ds(r0, ROWS), ct * LANES : (ct + 1) * LANES]
             new = v[ct] + tendency(v[ct], north, south, after[ct], before[ct], s)
             if ct == nt:
                 new = jnp.where(s > 0, new, 0.0)
@@ -279,20 +300,17 @@
         for ct in range(nt):
             north = s1[ct, pl.ds(ROWS - 1 + r0, ROWS), :]
             south = s1[ct, pl.ds(ROWS + 1 + r0, ROWS), :]
-            s = sx[ct, pl.ds(r0, ROWS), :]
+            at = slice(ct * LANES, (ct + 1) * LANES)
+            s = sx[pl.ds(r0, ROWS), at]
             g = gx[ct, pl.ds(ROWS + r0, ROWS), :]
-            tab[pl.ds(ct * rows + r0, ROWS), :] = 0.5 * (
-                g + v[ct] + tendency(v[ct], north, south, after[ct], before[ct], s)
-            )
+            new = 0.5 * (g + v[ct] + tendency(v[ct], north, south, after[ct], before[ct], s))
+            tab[pl.ds(ct * rows + r0, ROWS), :] = new
+            final[pl.ds(r0, ROWS), at] = new
         return carry
 
     lax.fori_loop(0, rows // ROWS, second, 0, unroll=4)
-    outs = [
-        pltpu.make_async_copy(tab.at[pl.ds(ct * rows, rows)], out.at[:, pl.ds(ct * LANES, LANES)], sem.at[0, ct])
-        for ct in range(nt)
-    ]
-    for copy in outs:
-        copy.start()
+    put = pltpu.make_async_copy(final, out, sem.at[1, 0])
+    put.start()
     sub = iota((ROWS, LANES), 0)
     unroll = 8
 
@@ -341,16 +359,23 @@
         route[o, 0:per_owner, :] = sums[own, 0:LANES]
         route[o, per_owner : 2 * per_owner, :] = idx[own, :]
         route[o, 2 * per_owner : 2 * per_owner + 1, 0:32] = sums[table + o : table + o + 1, LANES : LANES + 32]
-    for copy in outs:
-        copy.wait()
-
-
-def strip_kernel(per_owner, recv, ra, rb, w, solid, material, token, top_ref, up_ref, ret_ref, lhs, rhs, dep, src, tabu):
+    put.wait()
+
+
+def strip_kernel(
+    per_owner, recv, ra, rb, w, solid, material, token, top_ref, up_ref, ret_ref, lhs, rhs, dep, src, tabu, su, sm, sem
+):
     devices = recv.shape[0]
     cols = solid.shape[1]
     nt = cols // LANES
     wide = cols + LANES
     high = 2 * nt
+    copies = [
+        pltpu.make_async_copy(solid.at[pl.ds(0, 2 * ROWS)], su, sem.at[0]),
+        pltpu.make_async_copy(material.at[pl.ds(0, 2 * ROWS)], sm, sem.at[1]),
+    ]
+    for copy in copies:
+        copy.start()
     highs = iota((high, LANES), 0)
     lanes_down = iota((LANES, LANES), 0)
     for d in range(devices):
@@ -383,9 +408,11 @@
     def above(at):
         return jnp.where(row8 > 0, jnp.where(is_even, rb[at : at + ROWS, :], ra[at : at + ROWS, :]), 0.0)
 
-    uh, kh = halo_tiles(w[...])
-    u = jnp.concatenate([above(0), jnp.concatenate([solid[...], uh], axis=1)], axis=0)
-    k0 = jnp.concatenate([above(8), jnp.concatenate([base_conductivity(material[...]), kh], axis=1)], axis=0)
+    uh, kh = halo_tiles(w[0 : 2 * ROWS, :])
+    for copy in copies:
+        copy.wait()
+    u = jnp.concatenate([above(0), jnp.concatenate([su[...], uh], axis=1)], axis=0)
+    k0 = jnp.concatenate([above(8), jnp.concatenate([base_conductivity(sm[...]), kh], axis=1)], axis=0)
     inside = jnp.where(k0 > 0, 0.5 * SOLID_STEP, 0.0)
     source = jnp.concatenate(
         [jnp.zeros((ROWS, wide), F32), 2.0 * src[...], jnp.zeros((ROWS, wide), F32)], axis=0
@@ -397,7 +424,10 @@
         down = (k + pltpu.roll(k, high_rows - 1, 0)) * (pltpu.roll(u, high_rows - 1, 0) - u)
         flux = across - pltpu.roll(across, 1, 1) + down - pltpu.roll(down, 1, 0)
         u = u + inside * (flux + source)
-    up_ref[...] = u[0:ROWS, 0:cols]
+    for j in range(EDGE):
+        for ct in range(nt):
+            row = ROWS - EDGE + j
+            up_ref[j, ct : ct + 1, :] = u[row : row + 1, ct * LANES : (ct + 1) * LANES]
     top_ref[...] = u[ROWS : 2 * ROWS, 0:cols]
     for line in range(2):
         for ct in range(nt):
@@ -413,33 +443,35 @@
             ret_ref[d, q : q + 1, :] = jnp.sum(jnp.where(highs == hi, x, 0.0), axis=0, keepdims=True)
 
 
-def bulk_kernel(first, last_half, solid, material, w, ra, rb, after, *rest):
-    out, ua, ub, ka, kb, k0, k1, mat, sem = rest[1:] if last_half else rest[:1] + rest[2:]
-    rows, cols = solid.shape
-    half = mat.shape[1] - ROWS
-    top = first - ROWS if last_half else first
-    count = half + ROWS
+def bulk_kernel(last_half, start, count, groups, solid, material, w, *refs):
+    if last_half:
+        ra, rb, top, so_far, out, low_ref, u0, m0, ua, ub, ka, kb, k0, k1, fin, sem = refs
+    else:
+        out, token, u0, m0, ua, ub, ka, kb, k0, k1, fin, sem = refs
+    cols = solid.shape[1]
     nt = cols // LANES
+    size = count // groups
+    blocks = size // ROWS
     copies = []
-    for ct in range(nt):
-        at = pl.ds(ct * LANES, LANES)
-        copies.append(
-            pltpu.make_async_copy(solid.at[pl.ds(top, count), at], ua.at[ct, pl.ds(ROWS, count)], sem.at[0, ct])
-        )
-        copies.append(pltpu.make_async_copy(material.at[pl.ds(top, count), at], mat.at[ct], sem.at[1, ct]))
+    for g in range(groups):
+        here, there = pl.ds(start + g * size, size), pl.ds(g * size, size)
+        copies.append(pltpu.make_async_copy(solid.at[here], u0.at[there], sem.at[0, g]))
+        copies.append(pltpu.make_async_copy(material.at[here], m0.at[there], sem.at[1, g]))
     for copy in copies:
         copy.start()
-    uh, kh = halo_tiles(w[top : top + count, :])
-    ua[nt, ROWS : ROWS + count, :] = uh
-    k0[nt] = kh
-    ka[nt, ROWS : ROWS + count, :] = kh * jnp.exp(SOFTEN * uh)
-    is_even = even("passage")
+    if last_half:
+        put = pltpu.make_async_copy(top, out.at[pl.ds(0, ROWS)], sem.at[2, 0])
+        put.start()
+    uh, kh = halo_tiles(w[start : start + count, :])
+    ua[nt, ROWS : ROWS + count, :] = SCALE * uh
+    k0[nt] = SHARE * kh
     zero = jnp.zeros((ROWS, LANES), F32)
     for ct in range(nt + 1):
         at = slice(ct * LANES, (ct + 1) * LANES)
         if last_half:
-            below = jnp.where(is_even, ra[1:2, at], rb[1:2, at])
-            below_k = jnp.where(is_even, ra[9:10, at], rb[9:10, at]) * jnp.exp(SOFTEN * below)
+            is_even = even("passage")
+            below = SCALE * jnp.where(is_even, ra[1:2, at], rb[1:2, at])
+            below_k = SHARE * jnp.where(is_even, ra[9:10, at], rb[9:10, at]) * jnp.exp2(below)
         for u, k in ((ua, ka), (ub, kb)):
             u[ct, 0:ROWS, :] = zero
             k[ct, 0:ROWS, :] = zero
@@ -449,31 +481,38 @@
             else:
                 u[ct, ROWS + count : 2 * ROWS + count, :] = zero
                 k[ct, ROWS + count : 2 * ROWS + count, :] = zero
-    for copy in copies:
-        copy.wait()
+    if not last_half:
+        token[...] = zero
     lane = iota((ROWS, LANES), 1)
     edge = lane == LANES - 1
 
     def begin(i, carry):
         r0 = pl.multiple_of(i * ROWS, ROWS)
         bases = []
-        for ct in range(nt):
-            base = base_conductivity(mat[ct, pl.ds(r0, ROWS), :])
-            k0[ct, pl.ds(r0, ROWS), :] = base
-            ka[ct, pl.ds(ROWS + r0, ROWS), :] = base * jnp.exp(SOFTEN * ua[ct, pl.ds(ROWS + r0, ROWS), :])
+        for ct in range(nt + 1):
+            if ct < nt:
+                at = slice(ct * LANES, (ct + 1) * LANES)
+                here = SCALE * u0[pl.ds(r0, ROWS), at]
+                base = base_conductivity(m0[pl.ds(r0, ROWS), at], SHARE)
+                ua[ct, pl.ds(ROWS + r0, ROWS), :] = here
+                k0[ct, pl.ds(r0, ROWS), :] = base
+            else:
+                here = ua[ct, pl.ds(ROWS + r0, ROWS), :]
+                base = k0[ct, pl.ds(r0, ROWS), :]
+            ka[ct, pl.ds(ROWS + r0, ROWS), :] = base * jnp.exp2(here)
             bases.append(base)
-        bases.append(k0[nt, pl.ds(r0, ROWS), :])
         turned = [pltpu.roll(x, LANES - 1, 1) for x in bases]
         for ct in range(nt + 1):
             k1[ct, pl.ds(r0, ROWS), :] = jnp.where(edge, turned[(ct + 1) % (nt + 1)], turned[ct])
         return carry
 
-    lax.fori_loop(0, count // ROWS, begin, 0, unroll=2)
-    for step in range(SUBSTEPS):
-        final = step == SUBSTEPS - 1
-        u, k, nu, nk = (ua, ka, ub, kb) if step % 2 == 0 else (ub, kb, ua, ka)
-
-        def body(i, carry, u=u, k=k, nu=nu, nk=nk, final=final):
+    for g in range(groups):
+        copies[2 * g].wait()
+        copies[2 * g + 1].wait()
+        lax.fori_loop(g * blocks, (g + 1) * blocks, begin, 0, unroll=True)
+
+    def substep(u, k, nu, nk, final):
+        def body(i, carry):
             r0 = pl.multiple_of(i * ROWS, ROWS)
             at = pl.ds(ROWS + r0, ROWS)
             north, south = pl.ds(ROWS - 1 + r0, ROWS), pl.ds(ROWS + 1 + r0, ROWS)
@@ -483,60 +522,65 @@
             across = []
             for ct in range(nt + 1):
                 nearby = jnp.where(edge, turned[(ct + 1) % (nt + 1)], turned[ct])
-                nearby_k = k1[ct, pl.ds(r0, ROWS), :] * jnp.exp(SOFTEN * nearby)
+                nearby_k = k1[ct, pl.ds(r0, ROWS), :] * jnp.exp2(nearby)
                 across.append((cond[ct] + nearby_k) * (nearby - here[ct]))
             back = [pltpu.roll(x, 1, 1) for x in across]
             for ct in range(nt if final else nt + 1):
                 flux = across[ct] - jnp.where(lane == 0, back[ct - 1], back[ct])
                 flux = flux + (cond[ct] + k[ct, north, :]) * (u[ct, north, :] - here[ct])
                 flux = flux + (cond[ct] + k[ct, south, :]) * (u[ct, south, :] - here[ct])
-                base = k0[ct, pl.ds(r0, ROWS), :]
                 if ct == nt:
-                    flux = jnp.where(base > 0, flux, 0.0)
-                new = here[ct] + 0.5 * SOLID_STEP * flux
-                nu[ct, at, :] = new
-                if not final:
-                    nk[ct, at, :] = base * jnp.exp(SOFTEN * new)
+                    flux = jnp.where(k0[ct, pl.ds(r0, ROWS), :] > 0, flux, 0.0)
+                new = here[ct] + flux
+                if final:
+                    fin[pl.ds(r0, ROWS), ct * LANES : (ct + 1) * LANES] = new * (1.0 / SCALE)
+                else:
+                    nu[ct, at, :] = new
+                    nk[ct, at, :] = k0[ct, pl.ds(r0, ROWS), :] * jnp.exp2(new)
             return carry
 
-        lax.fori_loop(0, count // ROWS, body, 0, unroll=4)
-    final = ua if SUBSTEPS % 2 == 0 else ub
-    skip = ROWS if last_half else 0
-    outs = [
-        pltpu.make_async_copy(
-            final.at[ct, pl.ds(ROWS + skip, half)],
-            out.at[pl.ds(first, half), pl.ds(ct * LANES, LANES)],
-            sem.at[0, ct],
+        return body
+
+    for step in range(SUBSTEPS - 1):
+        u, k, nu, nk = (ua, ka, ub, kb) if step % 2 == 0 else (ub, kb, ua, ka)
+        lax.fori_loop(0, count // ROWS, substep(u, k, nu, nk, False), 0, unroll=blocks)
+    last = (ua, ka, ub, kb) if SUBSTEPS % 2 == 1 else (ub, kb, ua, ka)
+    outs = []
+    for g in range(groups):
+        lax.fori_loop(g * blocks, (g + 1) * blocks, substep(*last, True), 0, unroll=True)
+        first = g * size + (ROWS if last_half and g == 0 else 0)
+        end = (g + 1) * size - (ROWS if not last_half and g == groups - 1 else 0)
+        outs.append(
+            pltpu.make_async_copy(
+                fin.at[pl.ds(first, end - first)], out.at[pl.ds(start + first, end - first)], sem.at[0, g]
+            )
         )
-        for ct in range(nt)
-    ]
-    for copy in outs:
-        copy.start()
-    if not last_half:
-        rest[1][...] = zero
+        outs[-1].start()
+    if last_half:
+        low_ref[...] = fin[count - ROWS : count, :]
+        put.wait()
     for copy in outs:
         copy.wait()
 
 
-def finish_kernel(recv, slot, top, below, solid, wall_ref, out, tabl, edge, sem):
+def finish_kernel(recv, slot, below, low, solid, wall_ref, out, tabl, edge, sem):
     devices, per_owner = recv.shape[0], recv.shape[1]
     rows = solid.shape[0]
-    keep = rows - EDGE
-    fetch = pltpu.make_async_copy(out.at[pl.ds(rows - ROWS, ROWS)], edge, sem.at[0])
-    fetch.start()
-    put = pltpu.make_async_copy(top, out.at[pl.ds(0, ROWS)], sem.at[1])
-    put.start()
+    nt = below.shape[1]
+    last = lax.axis_index("passage") == lax.axis_size("passage") - 1
+    edge[...] = low[...]
+    for j in range(EDGE):
+        row = ROWS - EDGE + j
+        for ct in range(nt):
+            at = slice(ct * LANES, (ct + 1) * LANES)
+            edge[row : row + 1, at] = jnp.where(last, low[row : row + 1, at], below[j, ct : ct + 1, :])
+    store = pltpu.make_async_copy(edge, out.at[pl.ds(rows - ROWS, ROWS)], sem.at[0])
+    store.start()
     for d in range(devices):
         tabl[d * per_owner : (d + 1) * per_owner, :] = recv[d]
     table = tabl.shape[0]
     parts = jnp.concatenate(split3(tabl[...]), axis=0).astype(BF16)
     highs, lanes_down = iota((table, LANES), 0), iota((LANES, LANES), 0)
-    fetch.wait()
-    last = lax.axis_index("passage") == lax.axis_size("passage") - 1
-    row = iota(edge.shape, 0) + (rows - ROWS)
-    edge[...] = jnp.where((row >= keep) & jnp.logical_not(last), below[...], edge[...])
-    store = pltpu.make_async_copy(edge, out.at[pl.ds(rows - ROWS, ROWS)], sem.at[0])
-    store.start()
     for b in range(slot.shape[0]):
         place = slot[b : b + 1, :]
         lows = jnp.where(lanes_down == (place & (LANES - 1)), 1.0, 0.0).astype(BF16)
@@ -544,7 +588,6 @@
         x = x[0:table] + x[table : 2 * table] + x[2 * table : 3 * table]
         hi = lax.shift_right_logical(place, 7)
         wall_ref[b : b + 1, :] = jnp.sum(jnp.where(highs == hi, x, 0.0), axis=0, keepdims=True)
-    put.wait()
     store.wait()
 
 
@@ -567,38 +610,32 @@
     def cost(flops, moved, hard=0):
         return pl.CostEstimate(flops=flops, bytes_accessed=moved, transcendentals=hard)
 
-    fields = (gas, gas_speed, solid, material)
-    left = pl.BlockSpec((rows, LANES), lambda i: (0, 0))
-    right = pl.BlockSpec((rows, LANES), lambda i: (0, nt - 1))
-    column = pl.BlockSpec((16, rows), lambda i: (0, 0))
-    one, two = pl.pallas_call(
+    one, two, edges, edge_m = pl.pallas_call(
         pack_columns,
-        grid=(1,),
-        compiler_params=params(60),
-        in_specs=[left, right] * 4,
-        out_specs=[column, column],
-        out_shape=[shape((16, rows))] * 2,
+        in_specs=[whole(pltpu.HBM)] * 4,
+        out_specs=[whole()] * 4,
+        out_shape=[shape((16, rows))] * 2 + [shape((6, ROWS, cols)), shape((2, ROWS, cols), jnp.int32)],
+        scratch_shapes=[
+            VMEM((6, rows, LANES), F32),
+            VMEM((2, rows, LANES), jnp.int32),
+            pltpu.SemaphoreType.DMA((2, 8)),
+        ],
+        compiler_params=params(52),
         name="pack_columns",
         cost_estimate=cost(1000000, 8 * rows * LANES * 4),
-    )(*[x for field in fields for x in (field, field)])
+    )(gas, gas_speed, solid, material)
     one, two = pair_swaps("tile", tiles)(one, two)
 
-    def tall(count, row):
-        return pl.BlockSpec((count, cols), lambda i: (row, 0))
-
-    full = pl.BlockSpec((rows, LANES), lambda i: (0, 0))
-    band = pl.BlockSpec((16, wide), lambda i: (0, 0))
     w, ra, rb = pl.pallas_call(
         pack_rows,
-        grid=(1,),
-        compiler_params=params(60),
-        in_specs=[column, column] + [tall(ROWS, 0), tall(ROWS, rows // ROWS - 1)] * 4,
-        out_specs=[full, band, band],
+        in_specs=[whole()] * 4,
+        out_specs=[whole()] * 3,
         out_shape=[shape((rows, LANES)), shape((16, wide)), shape((16, wide))],
         scratch_shapes=[VMEM((LANES, rows), F32)],
+        compiler_params=params(8),
         name="pack_rows",
         cost_estimate=cost(1000000, 8 * ROWS * cols * 4),
-    )(one, two, *[x for field in fields for x in (field, field)])
+    )(one, two, edges, edge_m)
     ra, rb = pair_swaps("passage", passages)(ra, rb)
 
     def folded(x):
@@ -615,7 +652,7 @@
             VMEM((2 * table, faces), BF16),
             VMEM((LANES, faces), BF16),
         ],
-        compiler_params=params(60),
+        compiler_params=params(24),
         name="find_slots",
         cost_estimate=cost(20000000, 1000000),
     )(owner, surface, cell)
@@ -623,21 +660,23 @@
     part = table + devices
     gas_next, route = pl.pallas_call(
         functools.partial(gas_kernel, tiles, per_owner),
-        in_specs=[whole(pl.ANY)] * 2 + [whole()] * 3 + [whole(pltpu.SMEM)] + [whole()] * 7,
-        out_specs=[whole(pl.ANY), whole()],
+        in_specs=[whole(pltpu.HBM)] * 2 + [whole()] * 3 + [whole(pltpu.SMEM)] + [whole()] * 7,
+        out_specs=[whole(pltpu.HBM), whole()],
         out_shape=[shape((rows, cols)), shape((devices, ROUTE_ROWS, LANES))],
         scratch_shapes=[
             VMEM((nt + 1, rows + 2 * ROWS, LANES), F32),
-            VMEM((nt + 1, rows, LANES), F32),
+            VMEM((rows, cols), F32),
+            VMEM((rows, LANES), F32),
             VMEM((nt + 1, rows + 2 * ROWS, LANES), F32),
             VMEM((nt * rows, LANES), F32),
+            VMEM((rows, cols), F32),
             VMEM((faces, LANES), F32),
             VMEM((3 * part, faces), BF16),
             VMEM((LANES + 32, faces), BF16),
             VMEM((part, LANES + 32), F32),
             pltpu.SemaphoreType.DMA((2, nt)),
         ],
-        compiler_params=params(60),
+        compiler_params=params(24),
         name="gas_and_heat",
         cost_estimate=cost(60000000, 40000000),
     )(
@@ -646,78 +685,67 @@
     )
     recv = lax.all_to_all(route, ("passage", "tile"), 0, 0, tiled=True)
 
-    half = rows // 2 // ROWS * ROWS
-
-    def bulk_half(first, count, after, whole_so_far):
-        last_half = first > 0
+    blocks_here = rows // ROWS
+    ahead = blocks_here // 2 // 4 * 4
+
+    def bulk_half(last_half, start, count, groups, *more):
         return pl.pallas_call(
-            functools.partial(bulk_kernel, first, last_half),
-            in_specs=[whole(pl.ANY)] * 2 + [whole()] * 3 + [whole(pl.ANY)] * (2 if last_half else 1),
-            out_specs=[whole(pl.ANY)] + ([] if last_half else [whole()]),
-            out_shape=[shape((rows, cols))] + ([] if last_half else [shape((ROWS, LANES))]),
+            functools.partial(bulk_kernel, last_half, start, count, groups),
+            in_specs=[whole(pltpu.HBM)] * 2 + [whole()] + ([whole()] * 3 + [whole(pltpu.HBM)] if last_half else []),
+            out_specs=[whole(pltpu.HBM), whole()],
+            out_shape=[shape((rows, cols)), shape((ROWS, cols if last_half else LANES))],
             input_output_aliases={6: 0} if last_half else {},
-            scratch_shapes=[VMEM((nt + 1, count + 3 * ROWS, LANES), F32)] * 4
-            + [VMEM((nt + 1, count + ROWS, LANES), F32)] * 2
-            + [
-                VMEM((nt, count + ROWS, LANES), jnp.int32),
-                pltpu.SemaphoreType.DMA((2, nt)),
-            ],
-            compiler_params=params(60),
+            scratch_shapes=[VMEM((count, cols), F32), VMEM((count, cols), jnp.int32)]
+            + [VMEM((nt + 1, count + 2 * ROWS, LANES), F32)] * 4
+            + [VMEM((nt + 1, count, LANES), F32)] * 2
+            + [VMEM((count, cols), F32), pltpu.SemaphoreType.DMA((3, groups))],
+            compiler_params=params(52),
             name="solid_bulk",
             cost_estimate=cost(60000000, 30000000),
-        )(solid, material, w, ra, rb, after, *([whole_so_far] if last_half else []))
-
-    bulk, token = bulk_half(0, half, gas_next, None)
+        )(solid, material, w, *more)
+
+    bulk, token = bulk_half(False, 0, ahead * ROWS, 4)
 
     slots = table * LANES
     top, up, ret = pl.pallas_call(
         functools.partial(strip_kernel, per_owner),
-        grid=(1,),
-        in_specs=[
-            pl.BlockSpec((devices, ROUTE_ROWS, LANES), lambda i: (0, 0, 0)),
-            band,
-            band,
-            pl.BlockSpec((16, LANES), lambda i: (0, 0)),
-            tall(16, 0),
-            tall(16, 0),
-            pl.BlockSpec((ROWS, LANES), lambda i: (0, 0)),
-        ],
-        out_specs=[
-            pl.BlockSpec((ROWS, cols), lambda i: (0, 0)),
-            pl.BlockSpec((ROWS, cols), lambda i: (0, 0)),
-            pl.BlockSpec((devices, per_owner, LANES), lambda i: (0, 0, 0)),
-        ],
-        out_shape=[shape((ROWS, cols)), shape((ROWS, cols)), shape((devices, per_owner, LANES))],
+        in_specs=[whole()] * 4 + [whole(pltpu.HBM)] * 2 + [whole()],
+        out_specs=[whole()] * 3,
+        out_shape=[shape((ROWS, cols)), shape((EDGE, nt, LANES)), shape((devices, per_owner, LANES))],
         scratch_shapes=[
             VMEM((6 * nt, slots), BF16),
             VMEM((LANES, slots), BF16),
             VMEM((2 * nt, LANES), F32),
             VMEM((ROWS, wide), F32),
             VMEM((2 * nt, LANES), F32),
+            VMEM((2 * ROWS, cols), F32),
+            VMEM((2 * ROWS, cols), jnp.int32),
+            pltpu.SemaphoreType.DMA((2,)),
         ],
-        compiler_params=params(60),
+        compiler_params=params(52),
         name="solid_strip",
         cost_estimate=cost(20000000, 4000000),
     )(recv, ra, rb, w, solid, material, token)
     ret = lax.all_to_all(ret, ("passage", "tile"), 0, 0, tiled=True)
     below = lax.ppermute(up, "passage", [(i + 1, i) for i in range(passages - 1)])
 
-    (bulk,) = bulk_half(half, rows - half, top, bulk)
+    behind = (ahead - 2) * ROWS
+    bulk, low = bulk_half(True, behind, rows - behind, 3, ra, rb, top, bulk)
     wall, solid_next = pl.pallas_call(
         finish_kernel,
-        in_specs=[whole()] * 4 + [whole(pl.ANY)],
-        out_specs=[whole(), whole(pl.ANY)],
+        in_specs=[whole()] * 4 + [whole(pltpu.HBM)],
+        out_specs=[whole(), whole(pltpu.HBM)],
         out_shape=[shape((blocks, LANES)), shape((rows, cols))],
         input_output_aliases={4: 1},
         scratch_shapes=[
             VMEM((table, LANES), F32),
             VMEM((ROWS, cols), F32),
-            pltpu.SemaphoreType.DMA((2,)),
+            pltpu.SemaphoreType.DMA((1,)),
         ],
-        compiler_params=params(60),
+        compiler_params=params(24),
         name="wall_temperatures",
         cost_estimate=cost(20000000, 4000000),
-    )(ret, slot, top, below, bulk)
+    )(ret, slot, below, low, bulk)
     return gas_next, solid_next, wall.reshape(faces)
 
 

time: 84.8 us -> 67.7 us (0.80)
  Pallas kernels: 53.4 us -> 38.6 us
  local copies, waits for them, and re-layouts: 3.76 us -> 0.03 us
  waiting for transfers between devices: 0.41 us -> 1.93 us
    pallas_call x6, Pallas kernels: 36.8 us -> 25.4 us  [the longest x2 17.1 us: bulk_half(): pl.pallas_call(functools.partial(bulk_kernel, last_half, start, count, gr...]
    unnamed x14, local copies, waits for them, and re-layouts: 3.76 us -> 0.03 us
    pallas_call x1, Pallas kernels: 13.9 us -> 11.9 us  [shards(): pl.pallas_call(functools.partial(gas_kernel, tiles, per_owner), in_specs=...]
    all_to_all x1, starting transfers between devices: 6.98 us -> 5.19 us  [shards(): ret = lax.all_to_all(ret, ('passage', 'tile'), 0, 0, tiled=True)]
    pallas_call x1, Pallas kernels: 2.64 us -> 1.26 us  [shards(): pl.pallas_call(functools.partial(find_slots, devices, per_owner, rows, co...]
    ppermute x2, waiting for transfers between devices: 0.39 us -> 1.25 us  [run(): lax.ppermute(one, axis, both(first))]
  transfers between devices with their start and end apart: 7 -> 7, of which waited for: 1 -> 3; matrix products, arithmetic and copies ran while one was open for 0% -> 0% of each run, Pallas kernels for 31% -> 28%
where the time goes in v3:
time: 67.7 us; the launch traced here: 66.6 us
  Pallas kernels  38.6 us (57%)
  starting transfers between devices  25 us (37%)
  waiting for transfers between devices  1.93 us (3%)
  between operations  1.01 us (1%)
    pallas_call x2, Pallas kernels, bulk_half(): pl.pallas_call(functools.partial(bulk_kernel, last_half, start, count, gr...  17.1 us
    all_to_all x1, starting transfers between devices, shards(): recv = lax.all_to_all(route, ('passage', 'tile'), 0, 0, tiled=True)  13.6 us
    pallas_call x1, Pallas kernels, shards(): pl.pallas_call(functools.partial(gas_kernel, tiles, per_owner), in_specs=...  11.9 us
    all_to_all x1, starting transfers between devices, shards(): ret = lax.all_to_all(ret, ('passage', 'tile'), 0, 0, tiled=True)  5.19 us
    pallas_call x1, Pallas kernels, shards(): pl.pallas_call(functools.partial(strip_kernel, per_owner), in_specs=[whol...  4.26 us
    ppermute x2, starting transfers between devices, run(): lax.ppermute(one, axis, both(first))  3.44 us
    pallas_call x1, Pallas kernels, shards(): pl.pallas_call(pack_columns, in_specs=[whole(pltpu.HBM)] * 4, out_specs=[...  1.95 us
    pallas_call x1, Pallas kernels, shards(): pl.pallas_call(finish_kernel, in_specs=[whole()] * 4 + [whole(pltpu.HBM)]...  1.81 us
  transfers between devices with their start and end apart: 7, of which 3 were waited for; matrix products, arithmetic and copies ran while one was open for 0% of the time, Pallas kernels for 28%

profile of v3, /device:TPU:0, one launch (start us, length us, event | category | flops | bytes accessed | tf_op | source)
XLA Modules:
  0.0 66.6 jit_solution(11692146277149261604)
XLA Ops:
  0.6 0.0 copy-start.2
  0.6 0.0 copy-start.3
  0.7 0.0 copy-start.4
  0.7 0.0 copy-start.5
  0.7 0.0 copy-start
  0.7 0.0 copy-start.1
  0.7 0.0 copy-start.6
  0.7 2.0 %pack_columns.1 = (f32[16,256]{1,0:T(8,128)S(1)}, f32[16,256]{1,0:T(8,128)S(1)}, f32[6,8,2048]{2,1,0:T(8,128)S(1)}, s32[2,8,2048]{2,1,0:T(8,128)S(1)}) custom-call(f32[256,2048]{1,0:T(8,128)} %gas.3, f32[256,2048]{1,0:T(8,128)} %speed.3, f32[256,2048]{1,0:T(8,128)} %solid.7, s32[256,2048]{1,0:T(8,128)} %material.7), custom_call_target="tpu_custom_call" | custom-call | flops 1000000 | bytes 1048576 | tf_op jit(solution)/shard_map/pack_columns/pallas_call | solution.py:613
  2.7 0.5 collective-permute-start
  3.2 0.7 collective-permute-start.1
  3.8 0.2 collective-permute-done.one
  4.0 0.0 collective-permute-done.1.two
  4.0 0.3 pack_rows.1
  4.3 2.9 %collective-permute-start.2 = (f32[16,2176]{1,0:T(8,128)S(1)}, f32[16,2176]{1,0:T(8,128)S(1)}, u32[]{:S(2)}, u32[]{:S(2)}) collective-permute-start(f32[16,2176]{1,0:T(8,128)S(1)} %get-tuple-element.29), channel_id=1, source_target_pairs={{0,4},{8,12},{16,20},{24,28},{4,0},{12,8},{20,16},{28,24},{1,5},{9... | collective-permute-start | bytes 417800 | tf_op jit(solution)/shard_map/ppermute | solution.py:73
  7.2 0.7 collective-permute-start.3
  7.9 0.0 copy-done.2
  7.9 0.0 copy-done.3
  7.9 1.3 %find_slots.1 = (s32[32,128]{1,0:T(8,128)S(1)}, s32[32,128]{1,0:T(8,128)S(1)}, f32[64,128]{1,0:T(8,128)S(1)}) custom-call(s32[32,128]{1,0:T(8,128)S(1)} %bitcast.7, s32[32,128]{1,0:T(8,128)S(1)} %bitcast.9, s32[32,128]{1,0:T(8,128)S(1)} %bitcast.11), custom_call_target="tpu_custom_call" | custom-call | flops 20000000 | bytes 1000000 | tf_op jit(solution)/shard_map/find_slots/pallas_call | solution.py:645
  9.2 1.1 %collective-permute-done.2.ra.refs_0_ = f32[16,2176]{1,0:T(8,128)S(1)} collective-permute-done((f32[16,2176]{1,0:T(8,128)S(1)}, f32[16,2176]{1,0:T(8,128)S(1)}, u32[]{:S(2)}, u32[]{:S(2)}) %collective-permute-start.2) | collective-permute-done | bytes 139296 | tf_op jit(solution)/shard_map/ppermute | solution.py:73
  10.3 0.0 collective-permute-done.3.rb.refs_1_
  10.3 0.0 copy-done
  10.3 11.9 %gas_and_heat.1 = (f32[256,2048]{1,0:T(8,128)}, f32[32,8,128]{2,1,0:T(8,128)}) custom-call(f32[256,2048]{1,0:T(8,128)S(1)} %copy-done, f32[256,2048]{1,0:T(8,128)S(1)} %copy-done.1, f32[256,128]{1,0:T(8,128)S(1)} %get-tuple-element.28.w, f32[16,2176]{1,0:T(8,128)S(1)} %collective-permute-done.2.ra.refs_0_, f32[16,2176]{1,0:T(8,128)S(1)} %collective-permute-done.3.rb.refs_1_, ...), custom_call_target="tpu_custom_call" | custom-call | flops 60000000 | bytes 40000000 | tf_op jit(solution)/shard_map/gas_and_heat/pallas_call | solution.py:661
  22.2 13.6 %all-to-all-start = ((f32[32,8,128]{2,1,0:T(8,128)}), f32[32,8,128]{2,1,0:T(8,128)S(1)}, u32[]{:S(2)}, u32[]{:S(2)}) async-start(f32[32,8,128]{2,1,0:T(8,128)} %get-tuple-element.35), calls=%async_computation | async-start | bytes 262144 | tf_op jit(solution)/shard_map/all_to_all | solution.py:686
  35.8 7.6 %solid_bulk.2 = (f32[256,2048]{1,0:T(8,128)}, f32[8,128]{1,0:T(8,128)S(1)}) custom-call(f32[256,2048]{1,0:T(8,128)} %solid.7, s32[256,2048]{1,0:T(8,128)} %material.7, f32[256,128]{1,0:T(8,128)S(1)} %get-tuple-element.28.w), custom_call_target="tpu_custom_call" | custom-call | flops 60000000 | bytes 30000000 | tf_op jit(solution)/shard_map/solid_bulk/pallas_call | solution.py:692
  43.4 0.7 all-to-all-done.recv
  44.1 4.3 %solid_strip.1 = (f32[8,2048]{1,0:T(8,128)S(1)}, f32[3,16,128]{2,1,0:T(8,128)S(1)}, f32[32,2,128]{2,1,0:T(2,128)}) custom-call(f32[32,8,128]{2,1,0:T(8,128)S(1)} %all-to-all-done.recv, f32[16,2176]{1,0:T(8,128)S(1)} %collective-permute-done.2.ra.refs_0_, f32[16,2176]{1,0:T(8,128)S(1)} %collective-permute-done.3.rb.refs_1_, ...), custom_call_target="tpu_custom_call" | custom-call | flops 20000000 | bytes 4000000 | tf_op jit(solution)/shard_map/solid_strip/pallas_call | solution.py:710
  48.3 5.2 %all-to-all-start.1 = ((f32[32,2,128]{2,1,0:T(2,128)}), f32[32,2,128]{2,1,0:T(2,128)S(1)}, u32[]{:S(2)}, u32[]{:S(2)}) async-start(f32[32,2,128]{2,1,0:T(2,128)} %get-tuple-element.37), calls=%async_computation.1 | async-start | bytes 65536 | tf_op jit(solution)/shard_map/all_to_all | solution.py:729
  53.5 1.5 %collective-permute-start.4 = (f32[3,16,128]{2,1,0:T(8,128)S(1)}, f32[3,16,128]{2,1,0:T(8,128)S(1)}, u32[]{:S(2)}, u32[]{:S(2)}) collective-permute-start(f32[3,16,128]{2,1,0:T(8,128)S(1)} %get-tuple-element.38), channel_id=1, source_target_pairs={{4,0},{8,4},{12,8},{16,12},{20,16},{24,20},{28,24},{5,1},{9,5},{13... | collective-permute-start | bytes 73736 | tf_op jit(solution)/shard_map/ppermute | solution.py:730
  55.0 9.6 %solid_bulk.3 = (f32[256,2048]{1,0:T(8,128)}, f32[8,2048]{1,0:T(8,128)S(1)}) custom-call(f32[256,2048]{1,0:T(8,128)} %solid.7, s32[256,2048]{1,0:T(8,128)} %material.7, f32[256,128]{1,0:T(8,128)S(1)} %get-tuple-element.28.w, f32[16,2176]{1,0:T(8,128)S(1)} %collective-permute-done.2.ra.refs_0_, ...), custom_call_target="tpu_custom_call", output_to_operand_aliasing={{0}: (6, {})} | custom-call | flops 60000000 | bytes 30000000 | tf_op jit(solution)/shard_map/solid_bulk/pallas_call | solution.py:692
  64.6 0.0 collective-permute-done.4.below
  64.6 0.0 all-to-all-done.1.recv
  64.6 1.8 %wall_temperatures.1 = (f32[32,128]{1,0:T(8,128)}, f32[256,2048]{1,0:T(8,128)}) custom-call(f32[32,2,128]{2,1,0:T(2,128)S(1)} %all-to-all-done.1.recv, s32[32,128]{1,0:T(8,128)S(1)} %get-tuple-element.32.slot, f32[3,16,128]{2,1,0:T(8,128)S(1)} %collective-permute-done.4.below, f32[8,2048]{1,0:T(8,128)S(1)} %get-tuple-element.41.low, ...), custom_call_target="tpu_custom_call", output_to_operand_aliasing={{1}: (4, {})} | custom-call | flops 20000000 | bytes 4000000 | tf_op jit(solution)/shard_map/wall_temperatures/pallas_call | solution.py:734
  (4 shorter events, 0.0 us)
Async XLA Ops:
  0.6 7.3 %copy-start.2 = (s32[4096,1]{0,1:T(1,128)S(1)}, s32[4096,1]{0,1:T(1,128)}, u32[]{:S(2)}) copy-start(s32[4096,1]{0,1:T(1,128)} %param.14) | copy-start | bytes 49156
  0.6 7.3 %copy-start.3 = (s32[4096]{0:T(1024)S(1)}, s32[4096]{0:T(1024)}, u32[]{:S(2)}) copy-start(s32[4096]{0:T(1024)} %param.15) | copy-start | bytes 49156
  0.7 7.3 %copy-start.4 = (s32[4096]{0:T(1024)S(1)}, s32[4096]{0:T(1024)}, u32[]{:S(2)}) copy-start(s32[4096]{0:T(1024)} %param.13) | copy-start | bytes 49156
  0.7 9.6 %copy-start.5 = (f32[4096]{0:T(1024)S(1)}, f32[4096]{0:T(1024)}, u32[]{:S(2)}) copy-start(f32[4096]{0:T(1024)} %param.16) | copy-start | bytes 49156
  0.7 9.6 %copy-start = (f32[256,2048]{1,0:T(8,128)S(1)}, f32[256,2048]{1,0:T(8,128)}, u32[]{:S(2)}) copy-start(f32[256,2048]{1,0:T(8,128)} %gas.3) | copy-start | bytes 6291460
  0.7 9.6 %copy-start.1 = (f32[256,2048]{1,0:T(8,128)S(1)}, f32[256,2048]{1,0:T(8,128)}, u32[]{:S(2)}) copy-start(f32[256,2048]{1,0:T(8,128)} %speed.3) | copy-start | bytes 6291460
  0.7 9.6 %copy-start.6 = (f32[4096]{0:T(1024)S(1)}, f32[4096]{0:T(1024)}, u32[]{:S(2)}) copy-start(f32[4096]{0:T(1024)} %param.17) | copy-start | bytes 49156
  2.7 1.4 %collective-permute-start = (f32[16,256]{1,0:T(8,128)S(1)}, f32[16,256]{1,0:T(8,128)S(1)}, u32[]{:S(2)}, u32[]{:S(2)}) collective-permute-start(f32[16,256]{1,0:T(8,128)S(1)} %get-tuple-element.24), channel_id=1, source_target_pairs={{0,1},{2,3},{1,0},{3,2},{4,5},{6,7},{5,4},{7,6},{8,9},{10,11},{9,8... | collective-permute-start | bytes 49160 | tf_op jit(solution)/shard_map/ppermute | solution.py:73
  3.2 0.8 %collective-permute-start.1 = (f32[16,256]{1,0:T(8,128)S(1)}, f32[16,256]{1,0:T(8,128)S(1)}, u32[]{:S(2)}, u32[]{:S(2)}) collective-permute-start(f32[16,256]{1,0:T(8,128)S(1)} %get-tuple-element.25), channel_id=1, source_target_pairs={{1,2},{2,1},{5,6},{6,5},{9,10},{10,9},{13,14},{14,13},{17,18},{18,... | collective-permute-start | bytes 49160 | tf_op jit(solution)/shard_map/ppermute | solution.py:73
  4.3 6.0 %collective-permute-start.2 = (f32[16,2176]{1,0:T(8,128)S(1)}, f32[16,2176]{1,0:T(8,128)S(1)}, u32[]{:S(2)}, u32[]{:S(2)}) collective-permute-start(f32[16,2176]{1,0:T(8,128)S(1)} %get-tuple-element.29), channel_id=1, source_target_pairs={{0,4},{8,12},{16,20},{24,28},{4,0},{12,8},{20,16},{28,24},{1,5},{9... | collective-permute-start | bytes 417800 | tf_op jit(solution)/shard_map/ppermute | solution.py:73
  7.2 3.0 %collective-permute-start.3 = (f32[16,2176]{1,0:T(8,128)S(1)}, f32[16,2176]{1,0:T(8,128)S(1)}, u32[]{:S(2)}, u32[]{:S(2)}) collective-permute-start(f32[16,2176]{1,0:T(8,128)S(1)} %get-tuple-element.30), channel_id=1, source_target_pairs={{4,8},{12,16},{20,24},{8,4},{16,12},{24,20},{5,9},{13,17},{21,25},... | collective-permute-start | bytes 417800 | tf_op jit(solution)/shard_map/ppermute | solution.py:73
  22.2 21.8 %all-to-all-start = ((f32[32,8,128]{2,1,0:T(8,128)}), f32[32,8,128]{2,1,0:T(8,128)S(1)}, u32[]{:S(2)}, u32[]{:S(2)}) async-start(f32[32,8,128]{2,1,0:T(8,128)} %get-tuple-element.35), calls=%async_computation | async-start | bytes 262144 | tf_op jit(solution)/shard_map/all_to_all | solution.py:686
  48.3 16.3 %all-to-all-start.1 = ((f32[32,2,128]{2,1,0:T(2,128)}), f32[32,2,128]{2,1,0:T(2,128)S(1)}, u32[]{:S(2)}, u32[]{:S(2)}) async-start(f32[32,2,128]{2,1,0:T(2,128)} %get-tuple-element.37), calls=%async_computation.1 | async-start | bytes 65536 | tf_op jit(solution)/shard_map/all_to_all | solution.py:729
  53.5 11.1 %collective-permute-start.4 = (f32[3,16,128]{2,1,0:T(8,128)S(1)}, f32[3,16,128]{2,1,0:T(8,128)S(1)}, u32[]{:S(2)}, u32[]{:S(2)}) collective-permute-start(f32[3,16,128]{2,1,0:T(8,128)S(1)} %get-tuple-element.38), channel_id=1, source_target_pairs={{4,0},{8,4},{12,8},{16,12},{20,16},{24,20},{28,24},{5,1},{9,5},{13... | collective-permute-start | bytes 73736 | tf_op jit(solution)/shard_map/ppermute | solution.py:730

commit v4 on v3

--- a/solution.py
+++ b/solution.py
@@ -15,6 +15,7 @@
 SHARE = 0.5 * SOLID_STEP
 LANES = 128
 ROWS = 8
+TALL = 64
 ROUTE_ROWS = 8
 EDGE = SUBSTEPS - 1
 F32 = jnp.float32
@@ -143,7 +144,7 @@
     return gas, speed
 
 
-def pack_rows(one, two, edges, edge_m, w_ref, a_ref, b_ref, wt):
+def pack_rows(one, two, edges, edge_m, token, w_ref, a_ref, b_ref, wt):
     is_even = even("tile")
     wt[...] = jnp.zeros_like(wt)
     wt[0:16, :] = jnp.where(is_even, one[...], two[...])
@@ -231,24 +232,69 @@
     return after, before
 
 
+def fetch(gas, speed, g0, s0, token, sem):
+    copies = [pltpu.make_async_copy(gas, g0, sem.at[0]), pltpu.make_async_copy(speed, s0, sem.at[1])]
+    for copy in copies:
+        copy.start()
+    token[...] = jnp.zeros_like(token)
+    for copy in copies:
+        copy.wait()
+
+
+def tendency(v, north, south, after, before, s):
+    return DIFFUSE * (south + north + after + before - 4.0 * v) - s * (v - before)
+
+
+def first_section(gas, speed, w, s1, gx, sh):
+    rows, cols = gas.shape
+    nt = cols // LANES
+    gh, speed_halo = gas_halo_tiles(w[...])
+    gx[nt, ROWS : ROWS + rows, :] = gh
+    sh[...] = speed_halo
+    zero = jnp.zeros((ROWS, LANES), F32)
+    for ct in range(nt + 1):
+        gx[ct, 0:ROWS, :] = zero
+        gx[ct, ROWS + rows : 2 * ROWS + rows, :] = zero
+        s1[ct, 0:ROWS, :] = zero
+        s1[ct, ROWS + rows : 2 * ROWS + rows, :] = zero
+
+    def spread(i, carry):
+        r0 = i * rows
+        for ct in range(nt):
+            gx[ct, pl.ds(ROWS + r0, rows), :] = gas[pl.ds(r0, rows), ct * LANES : (ct + 1) * LANES]
+        return carry
+
+    spread(0, 0)
+    lane = iota((rows, LANES), 1)
+
+    def body(i, carry):
+        r0 = i * rows
+        v = [gx[ct, pl.ds(ROWS + r0, rows), :] for ct in range(nt + 1)]
+        after, before = shifted(v, lane)
+        for ct in range(nt + 1):
+            north = gx[ct, pl.ds(ROWS - 1 + r0, rows), :]
+            south = gx[ct, pl.ds(ROWS + 1 + r0, rows), :]
+            s = sh[pl.ds(r0, rows), :] if ct == nt else speed[pl.ds(r0, rows), ct * LANES : (ct + 1) * LANES]
+            new = v[ct] + tendency(v[ct], north, south, after[ct], before[ct], s)
+            if ct == nt:
+                new = jnp.where(s > 0, new, 0.0)
+            s1[ct, pl.ds(ROWS + r0, rows), :] = new
+        return carry
+
+    body(0, 0)
+
+
 def gas_kernel(
-    tiles_across, per_owner, gas, speed, w, ra, rb, rowidx, cell, owner, surface, slot, film, wall, idx,
-    out, route, gx, sx, sh, s1, tab, final, stage, lhs, rhs, sums, sem,
+    tiles_across, per_owner, gas, speed, sone, w, ra, rb, where_at, cell, owner, surface, slot, film, wall, idx,
+    out, route, s1, tab, final, stage, lhs, rhs, sums, rowidx, sem,
 ):
     rows, cols = gas.shape
     nt = cols // LANES
     devices = route.shape[0]
     blocks = owner.shape[0]
     table = idx.shape[0]
-    copies = [pltpu.make_async_copy(speed, sx, sem.at[1, 0])]
-    for ct in range(nt):
-        at = pl.ds(ct * LANES, LANES)
-        copies.append(pltpu.make_async_copy(gas.at[:, at], gx.at[ct, pl.ds(ROWS, rows)], sem.at[0, ct]))
-    for copy in copies:
-        copy.start()
-    gh, speed_halo = gas_halo_tiles(w[...])
-    gx[nt, ROWS : ROWS + rows, :] = gh
-    sh[...] = speed_halo
+    rows_in = pltpu.make_async_copy(where_at, rowidx, sem.at[1])
+    rows_in.start()
     is_even = even("passage")
     place = lax.axis_index("passage")
     in_top = jnp.where(place > 0, 1.0, 0.0)
@@ -262,55 +308,39 @@
         at = slice(ct * LANES, (ct + 1) * LANES)
         return jnp.where(is_even, ra[row : row + 1, at], rb[row : row + 1, at])
 
+    speed_halo = gas_halo_tiles(w[...])[1]
     for ct in range(nt + 1):
-        gx[ct, ROWS - 1 : ROWS, :] = top(0, ct)
-        gx[ct, ROWS + rows : ROWS + rows + 1, :] = bottom(0, ct)
-    for copy in copies:
-        copy.wait()
+        up, down = DIFFUSE * top(0, ct), DIFFUSE * bottom(0, ct)
+        if ct == nt:
+            up = jnp.where(speed_halo[0:1] > 0, up, 0.0)
+            down = jnp.where(speed_halo[rows - 1 : rows] > 0, down, 0.0)
+        s1[ct, ROWS : ROWS + 1, :] = s1[ct, ROWS : ROWS + 1, :] + up
+        s1[ct, ROWS + rows - 1 : ROWS + rows, :] = s1[ct, ROWS + rows - 1 : ROWS + rows, :] + down
     for ct in range(nt):
-        s1[ct, ROWS - 1 : ROWS, :] = in_top * (top(8, ct) + DIFFUSE * gx[ct, ROWS : ROWS + 1, :])
-        s1[ct, ROWS + rows : ROWS + rows + 1, :] = in_bottom * (
-            bottom(8, ct) + DIFFUSE * gx[ct, ROWS + rows - 1 : ROWS + rows, :]
-        )
-    lane = iota((ROWS, LANES), 1)
-
-    def tendency(v, north, south, after, before, s):
-        return DIFFUSE * (south + north + after + before - 4.0 * v) - s * (v - before)
-
-    def first(i, carry):
-        r0 = pl.multiple_of(i * ROWS, ROWS)
-        v = [gx[ct, pl.ds(ROWS + r0, ROWS), :] for ct in range(nt + 1)]
-        after, before = shifted(v, lane)
-        for ct in range(nt + 1):
-            north = gx[ct, pl.ds(ROWS - 1 + r0, ROWS), :]
-            south = gx[ct, pl.ds(ROWS + 1 + r0, ROWS), :]
-            s = sh[pl.ds(r0, ROWS), :] if ct == nt else sx[pl.ds(r0, ROWS), ct * LANES : (ct + 1) * LANES]
-            new = v[ct] + tendency(v[ct], north, south, after[ct], before[ct], s)
-            if ct == nt:
-                new = jnp.where(s > 0, new, 0.0)
-            s1[ct, pl.ds(ROWS + r0, ROWS), :] = new
-        return carry
-
-    lax.fori_loop(0, rows // ROWS, first, 0, unroll=4)
+        at = slice(ct * LANES, (ct + 1) * LANES)
+        s1[ct, ROWS - 1 : ROWS, :] = in_top * (top(8, ct) + DIFFUSE * gas[0:1, at])
+        s1[ct, ROWS + rows : ROWS + rows + 1, :] = in_bottom * (bottom(8, ct) + DIFFUSE * gas[rows - 1 : rows, at])
+    lane = iota((rows, LANES), 1)
 
     def second(i, carry):
-        r0 = pl.multiple_of(i * ROWS, ROWS)
-        v = [s1[ct, pl.ds(ROWS + r0, ROWS), :] for ct in range(nt + 1)]
+        r0 = i * rows
+        v = [s1[ct, pl.ds(ROWS + r0, rows), :] for ct in range(nt + 1)]
         after, before = shifted(v, lane)
         for ct in range(nt):
-            north = s1[ct, pl.ds(ROWS - 1 + r0, ROWS), :]
-            south = s1[ct, pl.ds(ROWS + 1 + r0, ROWS), :]
+            north = s1[ct, pl.ds(ROWS - 1 + r0, rows), :]
+            south = s1[ct, pl.ds(ROWS + 1 + r0, rows), :]
             at = slice(ct * LANES, (ct + 1) * LANES)
-            s = sx[pl.ds(r0, ROWS), at]
-            g = gx[ct, pl.ds(ROWS + r0, ROWS), :]
+            g = gas[pl.ds(r0, rows), at]
+            s = speed[pl.ds(r0, rows), at]
             new = 0.5 * (g + v[ct] + tendency(v[ct], north, south, after[ct], before[ct], s))
-            tab[pl.ds(ct * rows + r0, ROWS), :] = new
-            final[pl.ds(r0, ROWS), at] = new
+            tab[pl.ds(ct * rows + r0, rows), :] = new
+            final[pl.ds(r0, rows), at] = new
         return carry
 
-    lax.fori_loop(0, rows // ROWS, second, 0, unroll=4)
-    put = pltpu.make_async_copy(final, out, sem.at[1, 0])
+    second(0, 0)
+    put = pltpu.make_async_copy(final, out, sem.at[0])
     put.start()
+    rows_in.wait()
     sub = iota((ROWS, LANES), 0)
     unroll = 8
 
@@ -443,86 +473,78 @@
             ret_ref[d, q : q + 1, :] = jnp.sum(jnp.where(highs == hi, x, 0.0), axis=0, keepdims=True)
 
 
-def bulk_kernel(last_half, start, count, groups, solid, material, w, *refs):
-    if last_half:
-        ra, rb, top, so_far, out, low_ref, u0, m0, ua, ub, ka, kb, k0, k1, fin, sem = refs
-    else:
-        out, token, u0, m0, ua, ub, ka, kb, k0, k1, fin, sem = refs
-    cols = solid.shape[1]
+def bulk_kernel(solid, material, w, ra, rb, out, low_ref, u0, m0, ua, ub, ka, kb, k0, k1, fin, sem):
+    count, cols = solid.shape
     nt = cols // LANES
+    groups = sem.shape[1]
     size = count // groups
-    blocks = size // ROWS
+    blocks = size // TALL
     copies = []
     for g in range(groups):
-        here, there = pl.ds(start + g * size, size), pl.ds(g * size, size)
-        copies.append(pltpu.make_async_copy(solid.at[here], u0.at[there], sem.at[0, g]))
-        copies.append(pltpu.make_async_copy(material.at[here], m0.at[there], sem.at[1, g]))
+        at = pl.ds(g * size, size)
+        copies.append(pltpu.make_async_copy(solid.at[at], u0.at[at], sem.at[0, g]))
+        copies.append(pltpu.make_async_copy(material.at[at], m0.at[at], sem.at[1, g]))
     for copy in copies:
         copy.start()
-    if last_half:
-        put = pltpu.make_async_copy(top, out.at[pl.ds(0, ROWS)], sem.at[2, 0])
-        put.start()
-    uh, kh = halo_tiles(w[start : start + count, :])
+    uh, kh = halo_tiles(w[...])
     ua[nt, ROWS : ROWS + count, :] = SCALE * uh
     k0[nt] = SHARE * kh
     zero = jnp.zeros((ROWS, LANES), F32)
     for ct in range(nt + 1):
         at = slice(ct * LANES, (ct + 1) * LANES)
-        if last_half:
-            is_even = even("passage")
-            below = SCALE * jnp.where(is_even, ra[1:2, at], rb[1:2, at])
-            below_k = SHARE * jnp.where(is_even, ra[9:10, at], rb[9:10, at]) * jnp.exp2(below)
+        is_even = even("passage")
+        below = SCALE * jnp.where(is_even, ra[1:2, at], rb[1:2, at])
+        below_k = SHARE * jnp.where(is_even, ra[9:10, at], rb[9:10, at]) * jnp.exp2(below)
         for u, k in ((ua, ka), (ub, kb)):
             u[ct, 0:ROWS, :] = zero
             k[ct, 0:ROWS, :] = zero
-            if last_half:
-                u[ct, ROWS + count : ROWS + count + 1, :] = below
-                k[ct, ROWS + count : ROWS + count + 1, :] = below_k
-            else:
-                u[ct, ROWS + count : 2 * ROWS + count, :] = zero
-                k[ct, ROWS + count : 2 * ROWS + count, :] = zero
-    if not last_half:
-        token[...] = zero
-    lane = iota((ROWS, LANES), 1)
+            u[ct, ROWS + count : ROWS + count + 1, :] = below
+            k[ct, ROWS + count : ROWS + count + 1, :] = below_k
+    lane = iota((TALL, LANES), 1)
     edge = lane == LANES - 1
 
     def begin(i, carry):
-        r0 = pl.multiple_of(i * ROWS, ROWS)
+        r0 = i * TALL
         bases = []
         for ct in range(nt + 1):
             if ct < nt:
                 at = slice(ct * LANES, (ct + 1) * LANES)
-                here = SCALE * u0[pl.ds(r0, ROWS), at]
-                base = base_conductivity(m0[pl.ds(r0, ROWS), at], SHARE)
-                ua[ct, pl.ds(ROWS + r0, ROWS), :] = here
-                k0[ct, pl.ds(r0, ROWS), :] = base
+                here = SCALE * u0[pl.ds(r0, TALL), at]
+                base = base_conductivity(m0[pl.ds(r0, TALL), at], SHARE)
+                ua[ct, pl.ds(ROWS + r0, TALL), :] = here
+                k0[ct, pl.ds(r0, TALL), :] = base
             else:
-                here = ua[ct, pl.ds(ROWS + r0, ROWS), :]
-                base = k0[ct, pl.ds(r0, ROWS), :]
-            ka[ct, pl.ds(ROWS + r0, ROWS), :] = base * jnp.exp2(here)
+                here = ua[ct, pl.ds(ROWS + r0, TALL), :]
+                base = k0[ct, pl.ds(r0, TALL), :]
+            ka[ct, pl.ds(ROWS + r0, TALL), :] = base * jnp.exp2(here)
             bases.append(base)
         turned = [pltpu.roll(x, LANES - 1, 1) for x in bases]
         for ct in range(nt + 1):
-            k1[ct, pl.ds(r0, ROWS), :] = jnp.where(edge, turned[(ct + 1) % (nt + 1)], turned[ct])
+            k1[ct, pl.ds(r0, TALL), :] = jnp.where(edge, turned[(ct + 1) % (nt + 1)], turned[ct])
         return carry
 
     for g in range(groups):
         copies[2 * g].wait()
         copies[2 * g + 1].wait()
-        lax.fori_loop(g * blocks, (g + 1) * blocks, begin, 0, unroll=True)
+        for i in range(g * blocks, (g + 1) * blocks):
+            begin(i, 0)
 
     def substep(u, k, nu, nk, final):
+        tall = TALL if final else count
+        lane = iota((tall, LANES), 1)
+        edge = lane == LANES - 1
+
         def body(i, carry):
-            r0 = pl.multiple_of(i * ROWS, ROWS)
-            at = pl.ds(ROWS + r0, ROWS)
-            north, south = pl.ds(ROWS - 1 + r0, ROWS), pl.ds(ROWS + 1 + r0, ROWS)
+            r0 = i * tall
+            at = pl.ds(ROWS + r0, tall)
+            north, south = pl.ds(ROWS - 1 + r0, tall), pl.ds(ROWS + 1 + r0, tall)
             here = [u[ct, at, :] for ct in range(nt + 1)]
             cond = [k[ct, at, :] for ct in range(nt + 1)]
             turned = [pltpu.roll(x, LANES - 1, 1) for x in here]
             across = []
             for ct in range(nt + 1):
                 nearby = jnp.where(edge, turned[(ct + 1) % (nt + 1)], turned[ct])
-                nearby_k = k1[ct, pl.ds(r0, ROWS), :] * jnp.exp2(nearby)
+                nearby_k = k1[ct, pl.ds(r0, tall), :] * jnp.exp2(nearby)
                 across.append((cond[ct] + nearby_k) * (nearby - here[ct]))
             back = [pltpu.roll(x, 1, 1) for x in across]
             for ct in range(nt if final else nt + 1):
@@ -530,44 +552,40 @@
                 flux = flux + (cond[ct] + k[ct, north, :]) * (u[ct, north, :] - here[ct])
                 flux = flux + (cond[ct] + k[ct, south, :]) * (u[ct, south, :] - here[ct])
                 if ct == nt:
-                    flux = jnp.where(k0[ct, pl.ds(r0, ROWS), :] > 0, flux, 0.0)
+                    flux = jnp.where(k0[ct, pl.ds(r0, tall), :] > 0, flux, 0.0)
                 new = here[ct] + flux
                 if final:
-                    fin[pl.ds(r0, ROWS), ct * LANES : (ct + 1) * LANES] = new * (1.0 / SCALE)
+                    fin[pl.ds(r0, tall), ct * LANES : (ct + 1) * LANES] = new * (1.0 / SCALE)
                 else:
                     nu[ct, at, :] = new
-                    nk[ct, at, :] = k0[ct, pl.ds(r0, ROWS), :] * jnp.exp2(new)
+                    nk[ct, at, :] = k0[ct, pl.ds(r0, tall), :] * jnp.exp2(new)
             return carry
 
         return body
 
     for step in range(SUBSTEPS - 1):
         u, k, nu, nk = (ua, ka, ub, kb) if step % 2 == 0 else (ub, kb, ua, ka)
-        lax.fori_loop(0, count // ROWS, substep(u, k, nu, nk, False), 0, unroll=blocks)
+        substep(u, k, nu, nk, False)(0, 0)
     last = (ua, ka, ub, kb) if SUBSTEPS % 2 == 1 else (ub, kb, ua, ka)
     outs = []
     for g in range(groups):
-        lax.fori_loop(g * blocks, (g + 1) * blocks, substep(*last, True), 0, unroll=True)
-        first = g * size + (ROWS if last_half and g == 0 else 0)
-        end = (g + 1) * size - (ROWS if not last_half and g == groups - 1 else 0)
-        outs.append(
-            pltpu.make_async_copy(
-                fin.at[pl.ds(first, end - first)], out.at[pl.ds(start + first, end - first)], sem.at[0, g]
-            )
-        )
+        for i in range(g * blocks, (g + 1) * blocks):
+            substep(*last, True)(i, 0)
+        at = pl.ds(g * size, size)
+        outs.append(pltpu.make_async_copy(fin.at[at], out.at[at], sem.at[0, g]))
         outs[-1].start()
-    if last_half:
-        low_ref[...] = fin[count - ROWS : count, :]
-        put.wait()
+    low_ref[...] = fin[count - ROWS : count, :]
     for copy in outs:
         copy.wait()
 
 
-def finish_kernel(recv, slot, below, low, solid, wall_ref, out, tabl, edge, sem):
+def finish_kernel(recv, slot, below, low, top, solid, wall_ref, out, tabl, edge, sem):
     devices, per_owner = recv.shape[0], recv.shape[1]
     rows = solid.shape[0]
     nt = below.shape[1]
     last = lax.axis_index("passage") == lax.axis_size("passage") - 1
+    put = pltpu.make_async_copy(top, out.at[pl.ds(0, ROWS)], sem.at[1])
+    put.start()
     edge[...] = low[...]
     for j in range(EDGE):
         row = ROWS - EDGE + j
@@ -588,6 +606,7 @@
         x = x[0:table] + x[table : 2 * table] + x[2 * table : 3 * table]
         hi = lax.shift_right_logical(place, 7)
         wall_ref[b : b + 1, :] = jnp.sum(jnp.where(highs == hi, x, 0.0), axis=0, keepdims=True)
+    put.wait()
     store.wait()
 
 
@@ -626,16 +645,26 @@
     )(gas, gas_speed, solid, material)
     one, two = pair_swaps("tile", tiles)(one, two)
 
+    g0, s0, token = pl.pallas_call(
+        fetch,
+        in_specs=[whole(pltpu.HBM)] * 2,
+        out_specs=[whole()] * 3,
+        out_shape=[shape((rows, cols))] * 2 + [shape((ROWS, LANES))],
+        scratch_shapes=[pltpu.SemaphoreType.DMA((2,))],
+        compiler_params=params(48),
+        name="fetch",
+        cost_estimate=cost(0, 16 * rows * cols),
+    )(gas, gas_speed)
     w, ra, rb = pl.pallas_call(
         pack_rows,
-        in_specs=[whole()] * 4,
+        in_specs=[whole()] * 5,
         out_specs=[whole()] * 3,
         out_shape=[shape((rows, LANES)), shape((16, wide)), shape((16, wide))],
         scratch_shapes=[VMEM((LANES, rows), F32)],
         compiler_params=params(8),
         name="pack_rows",
         cost_estimate=cost(1000000, 8 * ROWS * cols * 4),
-    )(one, two, edges, edge_m)
+    )(one, two, edges, edge_m, token)
     ra, rb = pair_swaps("passage", passages)(ra, rb)
 
     def folded(x):
@@ -658,53 +687,55 @@
     )(owner, surface, cell)
 
     part = table + devices
-    gas_next, route = pl.pallas_call(
+    ringed = (nt + 1, rows + 2 * ROWS, LANES)
+    sone = pl.pallas_call(
+        first_section,
+        in_specs=[whole()] * 3,
+        out_specs=whole(),
+        out_shape=shape(ringed),
+        scratch_shapes=[VMEM(ringed, F32), VMEM((rows, LANES), F32)],
+        compiler_params=params(12),
+        name="first_section",
+        cost_estimate=cost(8000000, 6000000),
+    )(g0, s0, w)
+    gas_next, route, _ = pl.pallas_call(
         functools.partial(gas_kernel, tiles, per_owner),
-        in_specs=[whole(pltpu.HBM)] * 2 + [whole()] * 3 + [whole(pltpu.SMEM)] + [whole()] * 7,
-        out_specs=[whole(pltpu.HBM), whole()],
-        out_shape=[shape((rows, cols)), shape((devices, ROUTE_ROWS, LANES))],
+        in_specs=[whole()] * 6 + [whole(pl.ANY)] + [whole()] * 7,
+        out_specs=[whole(pltpu.HBM), whole(), whole()],
+        out_shape=[shape((rows, cols)), shape((devices, ROUTE_ROWS, LANES)), shape(ringed)],
+        input_output_aliases={2: 2},
         scratch_shapes=[
-            VMEM((nt + 1, rows + 2 * ROWS, LANES), F32),
-            VMEM((rows, cols), F32),
-            VMEM((rows, LANES), F32),
-            VMEM((nt + 1, rows + 2 * ROWS, LANES), F32),
             VMEM((nt * rows, LANES), F32),
             VMEM((rows, cols), F32),
             VMEM((faces, LANES), F32),
             VMEM((3 * part, faces), BF16),
             VMEM((LANES + 32, faces), BF16),
             VMEM((part, LANES + 32), F32),
-            pltpu.SemaphoreType.DMA((2, nt)),
+            pltpu.SMEM((faces,), jnp.int32),
+            pltpu.SemaphoreType.DMA((2,)),
         ],
-        compiler_params=params(24),
+        compiler_params=params(20),
         name="gas_and_heat",
         cost_estimate=cost(60000000, 40000000),
     )(
-        gas, gas_speed, w, ra, rb, rowidx.reshape(faces), cell, owner, surface, slot,
+        g0, s0, sone, w, ra, rb, rowidx.reshape(faces), cell, owner, surface, slot,
         folded(film), folded(wall_previous), idx,
     )
     recv = lax.all_to_all(route, ("passage", "tile"), 0, 0, tiled=True)
 
-    blocks_here = rows // ROWS
-    ahead = blocks_here // 2 // 4 * 4
-
-    def bulk_half(last_half, start, count, groups, *more):
-        return pl.pallas_call(
-            functools.partial(bulk_kernel, last_half, start, count, groups),
-            in_specs=[whole(pltpu.HBM)] * 2 + [whole()] + ([whole()] * 3 + [whole(pltpu.HBM)] if last_half else []),
-            out_specs=[whole(pltpu.HBM), whole()],
-            out_shape=[shape((rows, cols)), shape((ROWS, cols if last_half else LANES))],
-            input_output_aliases={6: 0} if last_half else {},
-            scratch_shapes=[VMEM((count, cols), F32), VMEM((count, cols), jnp.int32)]
-            + [VMEM((nt + 1, count + 2 * ROWS, LANES), F32)] * 4
-            + [VMEM((nt + 1, count, LANES), F32)] * 2
-            + [VMEM((count, cols), F32), pltpu.SemaphoreType.DMA((3, groups))],
-            compiler_params=params(52),
-            name="solid_bulk",
-            cost_estimate=cost(60000000, 30000000),
-        )(solid, material, w, *more)
-
-    bulk, token = bulk_half(False, 0, ahead * ROWS, 4)
+    bulk, low = pl.pallas_call(
+        bulk_kernel,
+        in_specs=[whole(pltpu.HBM)] * 2 + [whole()] * 3,
+        out_specs=[whole(pltpu.HBM), whole()],
+        out_shape=[shape((rows, cols)), shape((ROWS, cols))],
+        scratch_shapes=[VMEM((rows, cols), F32), VMEM((rows, cols), jnp.int32)]
+        + [VMEM(ringed, F32)] * 4
+        + [VMEM((nt + 1, rows, LANES), F32)] * 2
+        + [VMEM((rows, cols), F32), pltpu.SemaphoreType.DMA((2, 4))],
+        compiler_params=params(52),
+        name="solid_bulk",
+        cost_estimate=cost(60000000, 30000000),
+    )(solid, material, w, ra, rb)
 
     slots = table * LANES
     top, up, ret = pl.pallas_call(
@@ -725,27 +756,25 @@
         compiler_params=params(52),
         name="solid_strip",
         cost_estimate=cost(20000000, 4000000),
-    )(recv, ra, rb, w, solid, material, token)
+    )(recv, ra, rb, w, solid, material, low)
     ret = lax.all_to_all(ret, ("passage", "tile"), 0, 0, tiled=True)
     below = lax.ppermute(up, "passage", [(i + 1, i) for i in range(passages - 1)])
 
-    behind = (ahead - 2) * ROWS
-    bulk, low = bulk_half(True, behind, rows - behind, 3, ra, rb, top, bulk)
     wall, solid_next = pl.pallas_call(
         finish_kernel,
-        in_specs=[whole()] * 4 + [whole(pltpu.HBM)],
+        in_specs=[whole()] * 5 + [whole(pltpu.HBM)],
         out_specs=[whole(), whole(pltpu.HBM)],
         out_shape=[shape((blocks, LANES)), shape((rows, cols))],
-        input_output_aliases={4: 1},
+        input_output_aliases={5: 1},
         scratch_shapes=[
             VMEM((table, LANES), F32),
             VMEM((ROWS, cols), F32),
-            pltpu.SemaphoreType.DMA((1,)),
+            pltpu.SemaphoreType.DMA((2,)),
         ],
         compiler_params=params(24),
         name="wall_temperatures",
         cost_estimate=cost(20000000, 4000000),
-    )(ret, slot, below, low, bulk)
+    )(ret, slot, below, low, top, bulk)
     return gas_next, solid_next, wall.reshape(faces)
 
 

time: 67.7 us -> 62.2 us (0.919); the launches traced: 66.6 us -> 61.9 us
  Pallas kernels: 38.6 us -> 32.1 us
  waiting for transfers between devices: 1.93 us -> 5.96 us
  starting transfers between devices: 25 us -> 22.8 us
    ppermute x1, waiting for transfers between devices: 0.01 us -> 4.43 us  [shards(): lax.ppermute(up, 'passage', [(i + 1, i) for i in range(passages - 1)])]
    pallas_call x1, Pallas kernels: 11.9 us -> 8.2 us  [shards(): pl.pallas_call(functools.partial(gas_kernel, tiles, per_owner), in_specs=...]
    pallas_call x4 -> x5, Pallas kernels: 19.2 us -> 16.6 us  [the longest x1 10.5 us: shards(): pl.pallas_call(bulk_kernel, in_specs=[whole(pltpu.HBM)] * 2 + [whole()] *...]
    all_to_all x1, starting transfers between devices: 13.6 us -> 11.2 us  [shards(): recv = lax.all_to_all(route, ('passage', 'tile'), 0, 0, tiled=True)]
    all_to_all x1, waiting for transfers between devices: 0.01 us -> 1.52 us  [shards(): ret = lax.all_to_all(ret, ('passage', 'tile'), 0, 0, tiled=True)]
    ppermute x2, waiting for transfers between devices: 1.25 us -> 0.01 us  [run(): lax.ppermute(one, axis, both(first))]
  transfers between devices with their start and end apart: 7 -> 7, of which waited for: 3 -> 2; matrix products, arithmetic and copies ran while one was open for 0% -> 0% of each run, Pallas kernels for 28% -> 25%
where the time goes in v4:
time: 62.2 us; the launch traced here: 61.9 us
  Pallas kernels  32.1 us (52%)
  starting transfers between devices  22.8 us (37%)
  waiting for transfers between devices  5.96 us (10%)
  between operations  0.99 us (2%)
    all_to_all x1, starting transfers between devices, shards(): recv = lax.all_to_all(route, ('passage', 'tile'), 0, 0, tiled=True)  11.2 us
    pallas_call x1, Pallas kernels, shards(): pl.pallas_call(bulk_kernel, in_specs=[whole(pltpu.HBM)] * 2 + [whole()] *...  10.5 us
    pallas_call x1, Pallas kernels, shards(): pl.pallas_call(functools.partial(gas_kernel, tiles, per_owner), in_specs=...  8.2 us
    all_to_all x1, starting transfers between devices, shards(): ret = lax.all_to_all(ret, ('passage', 'tile'), 0, 0, tiled=True)  5.67 us
    ppermute x1, waiting for transfers between devices, shards(): lax.ppermute(up, 'passage', [(i + 1, i) for i in range(passages - 1)])  4.43 us
    pallas_call x1, Pallas kernels, shards(): pl.pallas_call(functools.partial(strip_kernel, per_owner), in_specs=[whol...  4.27 us
    ppermute x2, starting transfers between devices, run(): lax.ppermute(one, axis, both(first))  3.15 us
    pallas_call x1, Pallas kernels, shards(): pl.pallas_call(fetch, in_specs=[whole(pltpu.HBM)] * 2, out_specs=[whole()...  2.24 us
  transfers between devices with their start and end apart: 7, of which 2 were waited for; matrix products, arithmetic and copies ran while one was open for 0% of the time, Pallas kernels for 25%

profile of v4, /device:TPU:0, one launch (start us, length us, event | category | flops | bytes accessed | tf_op | source)
XLA Modules:
  0.0 61.9 jit_solution(15302553802906650845)
XLA Ops:
  0.6 1.8 %pack_columns.1 = (f32[16,256]{1,0:T(8,128)S(1)}, f32[16,256]{1,0:T(8,128)S(1)}, f32[6,8,2048]{2,1,0:T(8,128)S(1)}, s32[2,8,2048]{2,1,0:T(8,128)S(1)}) custom-call(f32[256,2048]{1,0:T(8,128)} %gas.3, f32[256,2048]{1,0:T(8,128)} %speed.3, f32[256,2048]{1,0:T(8,128)} %solid.5, s32[256,2048]{1,0:T(8,128)} %material.5), custom_call_target="tpu_custom_call" | custom-call | flops 1000000 | bytes 1048576 | tf_op jit(solution)/shard_map/pack_columns/pallas_call | solution.py:632
  2.4 0.5 collective-permute-start
  3.0 0.0 copy-start
  3.0 0.0 copy-start.1
  3.0 0.8 %collective-permute-start.1 = (f32[16,256]{1,0:T(8,128)S(1)}, f32[16,256]{1,0:T(8,128)S(1)}, u32[]{:S(2)}, u32[]{:S(2)}) collective-permute-start(f32[16,256]{1,0:T(8,128)S(1)} %get-tuple-element.28), channel_id=1, source_target_pairs={{1,2},{2,1},{5,6},{6,5},{9,10},{10,9},{13,14},{14,13},{17,18},{18,... | collective-permute-start | bytes 49160 | tf_op jit(solution)/shard_map/ppermute | solution.py:74
  3.8 2.2 %fetch.1 = (f32[256,2048]{1,0:T(8,128)S(1)}, f32[256,2048]{1,0:T(8,128)S(1)}, f32[8,128]{1,0:T(8,128)S(1)}) custom-call(f32[256,2048]{1,0:T(8,128)} %gas.3, f32[256,2048]{1,0:T(8,128)} %speed.3), custom_call_target="tpu_custom_call" | custom-call | bytes 8388608 | tf_op jit(solution)/shard_map/fetch/pallas_call | solution.py:648
  6.0 0.0 collective-permute-done.one
  6.0 0.0 collective-permute-done.1.two
  6.0 0.3 pack_rows.1
  6.3 2.6 %collective-permute-start.2 = (f32[16,2176]{1,0:T(8,128)S(1)}, f32[16,2176]{1,0:T(8,128)S(1)}, u32[]{:S(2)}, u32[]{:S(2)}) collective-permute-start(f32[16,2176]{1,0:T(8,128)S(1)} %get-tuple-element.33), channel_id=1, source_target_pairs={{0,4},{8,12},{16,20},{24,28},{4,0},{12,8},{20,16},{28,24},{1,5},{9... | collective-permute-start | bytes 417800 | tf_op jit(solution)/shard_map/ppermute | solution.py:74
  9.0 0.7 %collective-permute-start.3 = (f32[16,2176]{1,0:T(8,128)S(1)}, f32[16,2176]{1,0:T(8,128)S(1)}, u32[]{:S(2)}, u32[]{:S(2)}) collective-permute-start(f32[16,2176]{1,0:T(8,128)S(1)} %get-tuple-element.34), channel_id=1, source_target_pairs={{4,8},{12,16},{20,24},{8,4},{16,12},{24,20},{5,9},{13,17},{21,25},... | collective-permute-start | bytes 417800 | tf_op jit(solution)/shard_map/ppermute | solution.py:74
  9.6 0.0 copy-done
  9.6 0.0 copy-done.1
  9.6 0.0 copy-done.2
  9.6 1.3 %find_slots.1 = (s32[32,128]{1,0:T(8,128)S(1)}, s32[32,128]{1,0:T(8,128)S(1)}, f32[64,128]{1,0:T(8,128)S(1)}) custom-call(s32[32,128]{1,0:T(8,128)S(1)} %bitcast.7, s32[32,128]{1,0:T(8,128)S(1)} %bitcast.9, s32[32,128]{1,0:T(8,128)S(1)} %bitcast.11), custom_call_target="tpu_custom_call" | custom-call | flops 20000000 | bytes 1000000 | tf_op jit(solution)/shard_map/find_slots/pallas_call | solution.py:674
  10.9 0.0 copy-start.3
  10.9 0.0 copy-start.4
  10.9 1.8 %first_section.1.sone = f32[17,272,128]{2,1,0:T(8,128)S(1)} custom-call(f32[256,2048]{1,0:T(8,128)S(1)} %get-tuple-element.25.gas, f32[256,2048]{1,0:T(8,128)S(1)} %get-tuple-element.26.speed, f32[256,128]{1,0:T(8,128)S(1)} %get-tuple-element.32.w), custom_call_target="tpu_custom_call" | custom-call | flops 8000000 | bytes 6000000 | tf_op jit(solution)/shard_map/first_section/pallas_call | solution.py:691
  12.7 0.0 collective-permute-done.2.ra
  12.7 0.0 collective-permute-done.3.rb
  12.7 0.0 copy-done.3
  12.8 0.0 copy-done.4
  12.8 8.2 %gas_and_heat.1 = (f32[256,2048]{1,0:T(8,128)}, f32[32,8,128]{2,1,0:T(8,128)}, f32[17,272,128]{2,1,0:T(8,128)S(1)}) custom-call(f32[256,2048]{1,0:T(8,128)S(1)} %get-tuple-element.25.gas, f32[256,2048]{1,0:T(8,128)S(1)} %get-tuple-element.26.speed, f32[17,272,128]{2,1,0:T(8,128)S(1)} %first_section.1.sone, ...), custom_call_target="tpu_custom_call", output_to_operand_aliasing={{2}: (2, {})} | custom-call | flops 60000000 | bytes 40000000 | tf_op jit(solution)/shard_map/gas_and_heat/pallas_call | solution.py:701
  21.0 11.2 %all-to-all-start = ((f32[32,8,128]{2,1,0:T(8,128)}), f32[32,8,128]{2,1,0:T(8,128)S(1)}, u32[]{:S(2)}, u32[]{:S(2)}) async-start(f32[32,8,128]{2,1,0:T(8,128)} %get-tuple-element.39), calls=%async_computation | async-start | bytes 262144 | tf_op jit(solution)/shard_map/all_to_all | solution.py:724
  32.2 10.5 %solid_bulk.1 = (f32[256,2048]{1,0:T(8,128)}, f32[8,2048]{1,0:T(8,128)S(1)}) custom-call(f32[256,2048]{1,0:T(8,128)} %solid.5, s32[256,2048]{1,0:T(8,128)} %material.5, f32[256,128]{1,0:T(8,128)S(1)} %get-tuple-element.32.w, f32[16,2176]{1,0:T(8,128)S(1)} %collective-permute-done.2.ra, f32[16,2176]{1,0:T(8,128)S(1)} %collective-permute-done.3.rb), custom_call_target="tpu_custom_call" | custom-call | flops 60000000 | bytes 30000000 | tf_op jit(solution)/shard_map/solid_bulk/pallas_call | solution.py:726
  42.7 0.0 all-to-all-done.recv
  42.7 4.3 %solid_strip.1 = (f32[8,2048]{1,0:T(8,128)S(1)}, f32[3,16,128]{2,1,0:T(8,128)S(1)}, f32[32,2,128]{2,1,0:T(2,128)}) custom-call(f32[32,8,128]{2,1,0:T(8,128)S(1)} %all-to-all-done.recv, f32[16,2176]{1,0:T(8,128)S(1)} %collective-permute-done.2.ra, f32[16,2176]{1,0:T(8,128)S(1)} %collective-permute-done.3.rb, f32[256,128]{1,0:T(8,128)S(1)} %get-tuple-element.32.w, ...), custom_call_target="tpu_custom_call" | custom-call | flops 20000000 | bytes 4000000 | tf_op jit(solution)/shard_map/solid_strip/pallas_call | solution.py:741
  47.0 5.7 %all-to-all-start.1 = ((f32[32,2,128]{2,1,0:T(2,128)}), f32[32,2,128]{2,1,0:T(2,128)S(1)}, u32[]{:S(2)}, u32[]{:S(2)}) async-start(f32[32,2,128]{2,1,0:T(2,128)} %get-tuple-element.41), calls=%async_computation.1 | async-start | bytes 65536 | tf_op jit(solution)/shard_map/all_to_all | solution.py:760
  52.7 1.3 %collective-permute-start.4 = (f32[3,16,128]{2,1,0:T(8,128)S(1)}, f32[3,16,128]{2,1,0:T(8,128)S(1)}, u32[]{:S(2)}, u32[]{:S(2)}) collective-permute-start(f32[3,16,128]{2,1,0:T(8,128)S(1)} %get-tuple-element.42), channel_id=1, source_target_pairs={{4,0},{8,4},{12,8},{16,12},{20,16},{24,20},{28,24},{5,1},{9,5},{13... | collective-permute-start | bytes 73736 | tf_op jit(solution)/shard_map/ppermute | solution.py:761
  54.0 4.4 %collective-permute-done.4.below = f32[3,16,128]{2,1,0:T(8,128)S(1)} collective-permute-done((f32[3,16,128]{2,1,0:T(8,128)S(1)}, f32[3,16,128]{2,1,0:T(8,128)S(1)}, u32[]{:S(2)}, u32[]{:S(2)}) %collective-permute-start.4) | collective-permute-done | bytes 24608 | tf_op jit(solution)/shard_map/ppermute | solution.py:761
  58.4 1.5 %all-to-all-done.1.recv = f32[32,2,128]{2,1,0:T(2,128)S(1)} async-done(((f32[32,2,128]{2,1,0:T(2,128)}), f32[32,2,128]{2,1,0:T(2,128)S(1)}, u32[]{:S(2)}, u32[]{:S(2)}) %all-to-all-start.1) | async-done | bytes 32800 | tf_op jit(solution)/shard_map/all_to_all | solution.py:760
  59.9 1.8 %wall_temperatures.1 = (f32[32,128]{1,0:T(8,128)}, f32[256,2048]{1,0:T(8,128)}) custom-call(f32[32,2,128]{2,1,0:T(2,128)S(1)} %all-to-all-done.1.recv, s32[32,128]{1,0:T(8,128)S(1)} %get-tuple-element.36.slot, f32[3,16,128]{2,1,0:T(8,128)S(1)} %collective-permute-done.4.below, ...), custom_call_target="tpu_custom_call", output_to_operand_aliasing={{1}: (5, {})} | custom-call | flops 20000000 | bytes 4000000 | tf_op jit(solution)/shard_map/wall_temperatures/pallas_call | solution.py:763
  (1 shorter events, 0.0 us)
Async XLA Ops:
  2.4 3.6 %collective-permute-start = (f32[16,256]{1,0:T(8,128)S(1)}, f32[16,256]{1,0:T(8,128)S(1)}, u32[]{:S(2)}, u32[]{:S(2)}) collective-permute-start(f32[16,256]{1,0:T(8,128)S(1)} %get-tuple-element.27), channel_id=1, source_target_pairs={{0,1},{2,3},{1,0},{3,2},{4,5},{6,7},{5,4},{7,6},{8,9},{10,11},{9,8... | collective-permute-start | bytes 49160 | tf_op jit(solution)/shard_map/ppermute | solution.py:74
  3.0 6.7 %copy-start = (s32[4096,1]{0,1:T(1,128)S(1)}, s32[4096,1]{0,1:T(1,128)}, u32[]{:S(2)}) copy-start(s32[4096,1]{0,1:T(1,128)} %param.14) | copy-start | bytes 49156
  3.0 6.7 %copy-start.1 = (s32[4096]{0:T(1024)S(1)}, s32[4096]{0:T(1024)}, u32[]{:S(2)}) copy-start(s32[4096]{0:T(1024)} %param.15) | copy-start | bytes 49156
  3.0 6.7 %copy-start.2 = (s32[4096]{0:T(1024)S(1)}, s32[4096]{0:T(1024)}, u32[]{:S(2)}) copy-start(s32[4096]{0:T(1024)} %param.13) | copy-start | bytes 49156
  3.0 3.1 %collective-permute-start.1 = (f32[16,256]{1,0:T(8,128)S(1)}, f32[16,256]{1,0:T(8,128)S(1)}, u32[]{:S(2)}, u32[]{:S(2)}) collective-permute-start(f32[16,256]{1,0:T(8,128)S(1)} %get-tuple-element.28), channel_id=1, source_target_pairs={{1,2},{2,1},{5,6},{6,5},{9,10},{10,9},{13,14},{14,13},{17,18},{18,... | collective-permute-start | bytes 49160 | tf_op jit(solution)/shard_map/ppermute | solution.py:74
  6.3 6.4 %collective-permute-start.2 = (f32[16,2176]{1,0:T(8,128)S(1)}, f32[16,2176]{1,0:T(8,128)S(1)}, u32[]{:S(2)}, u32[]{:S(2)}) collective-permute-start(f32[16,2176]{1,0:T(8,128)S(1)} %get-tuple-element.33), channel_id=1, source_target_pairs={{0,4},{8,12},{16,20},{24,28},{4,0},{12,8},{20,16},{28,24},{1,5},{9... | collective-permute-start | bytes 417800 | tf_op jit(solution)/shard_map/ppermute | solution.py:74
  9.0 3.8 %collective-permute-start.3 = (f32[16,2176]{1,0:T(8,128)S(1)}, f32[16,2176]{1,0:T(8,128)S(1)}, u32[]{:S(2)}, u32[]{:S(2)}) collective-permute-start(f32[16,2176]{1,0:T(8,128)S(1)} %get-tuple-element.34), channel_id=1, source_target_pairs={{4,8},{12,16},{20,24},{8,4},{16,12},{24,20},{5,9},{13,17},{21,25},... | collective-permute-start | bytes 417800 | tf_op jit(solution)/shard_map/ppermute | solution.py:74
  10.9 1.8 %copy-start.3 = (f32[4096]{0:T(1024)S(1)}, f32[4096]{0:T(1024)}, u32[]{:S(2)}) copy-start(f32[4096]{0:T(1024)} %param.16) | copy-start | bytes 49156
  10.9 1.8 %copy-start.4 = (f32[4096]{0:T(1024)S(1)}, f32[4096]{0:T(1024)}, u32[]{:S(2)}) copy-start(f32[4096]{0:T(1024)} %param.17) | copy-start | bytes 49156
  21.0 21.7 %all-to-all-start = ((f32[32,8,128]{2,1,0:T(8,128)}), f32[32,8,128]{2,1,0:T(8,128)S(1)}, u32[]{:S(2)}, u32[]{:S(2)}) async-start(f32[32,8,128]{2,1,0:T(8,128)} %get-tuple-element.39), calls=%async_computation | async-start | bytes 262144 | tf_op jit(solution)/shard_map/all_to_all | solution.py:724
  47.0 12.9 %all-to-all-start.1 = ((f32[32,2,128]{2,1,0:T(2,128)}), f32[32,2,128]{2,1,0:T(2,128)S(1)}, u32[]{:S(2)}, u32[]{:S(2)}) async-start(f32[32,2,128]{2,1,0:T(2,128)} %get-tuple-element.41), calls=%async_computation.1 | async-start | bytes 65536 | tf_op jit(solution)/shard_map/all_to_all | solution.py:760
  52.7 5.7 %collective-permute-start.4 = (f32[3,16,128]{2,1,0:T(8,128)S(1)}, f32[3,16,128]{2,1,0:T(8,128)S(1)}, u32[]{:S(2)}, u32[]{:S(2)}) collective-permute-start(f32[3,16,128]{2,1,0:T(8,128)S(1)} %get-tuple-element.42), channel_id=1, source_target_pairs={{4,0},{8,4},{12,8},{16,12},{20,16},{24,20},{28,24},{5,1},{9,5},{13... | collective-permute-start | bytes 73736 | tf_op jit(solution)/shard_map/ppermute | solution.py:761

commit v5 on v4

--- a/solution.py
+++ b/solution.py
@@ -15,7 +15,6 @@
 SHARE = 0.5 * SOLID_STEP
 LANES = 128
 ROWS = 8
-TALL = 64
 ROUTE_ROWS = 8
 EDGE = SUBSTEPS - 1
 F32 = jnp.float32
@@ -342,33 +341,31 @@
     put.start()
     rows_in.wait()
     sub = iota((ROWS, LANES), 0)
-    unroll = 8
-
-    def gather(i, carry):
-        base = pl.multiple_of(i * (ROWS * unroll), ROWS * unroll)
-        for g in range(unroll):
+    lanes_down = iota((LANES, LANES), 0)
+    highs = iota((table, LANES), 0)
+    owners = iota((devices, LANES), 0)
+    part = table + devices
+
+    def gather(b):
+        base = pl.multiple_of(b * LANES, LANES)
+        for g in range(LANES // ROWS):
             acc = jnp.broadcast_to(tab[pl.ds(rowidx[base + g * ROWS], 1), :], (ROWS, LANES))
             for j in range(1, ROWS):
                 row = tab[pl.ds(rowidx[base + g * ROWS + j], 1), :]
                 acc = jnp.where(sub == j, jnp.broadcast_to(row, (ROWS, LANES)), acc)
             stage[pl.ds(base + g * ROWS, ROWS), :] = acc
-        return carry
-
-    lax.fori_loop(0, stage.shape[0] // (ROWS * unroll), gather, 0)
-    lanes_down = iota((LANES, LANES), 0)
-    highs = iota((table, LANES), 0)
-    owners = iota((devices, LANES), 0)
-    part = table + devices
-    for b in range(blocks):
-        at = slice(b * LANES, (b + 1) * LANES)
-        picked = jnp.where(lanes_down == (cell[b : b + 1, :] & (LANES - 1)), stage[at, :].T, 0.0)
+
+    def place_heat(b):
+        at = pl.ds(pl.multiple_of(b * LANES, LANES), LANES)
+        one = pl.ds(b, 1)
+        picked = jnp.where(lanes_down == (cell[one, :] & (LANES - 1)), stage[at, :].T, 0.0)
         face = jnp.sum(picked, axis=0, keepdims=True)
-        heat = split3(film[b : b + 1, :] * (face - wall[b : b + 1, :]))
-        place_of = slot[b : b + 1, :]
+        heat = split3(film[one, :] * (face - wall[one, :]))
+        place_of = slot[one, :]
         hi = lax.shift_right_logical(place_of, 7)
         lo = place_of & (LANES - 1)
-        mine = owner[b : b + 1, :]
-        voxel = surface[b : b + 1, :]
+        mine = owner[one, :]
+        voxel = surface[one, :]
         line = lax.div(voxel, cols)
         col = lax.rem(voxel, cols)
         tile = lax.rem(mine, tiles_across)
@@ -381,6 +378,15 @@
             lhs[k * part + table : (k + 1) * part, at] = jnp.where(owners == dest, heat[k], 0.0).astype(BF16)
         rhs[0:LANES, at] = jnp.where(lanes_down == lo, 1.0, 0.0).astype(BF16)
         rhs[LANES : LANES + 32, at] = jnp.where(iota((32, LANES), 0) == code, 1.0, 0.0).astype(BF16)
+
+    def both(b, carry):
+        place_heat(b - 1)
+        gather(b)
+        return carry
+
+    gather(0)
+    lax.fori_loop(1, blocks, both, 0)
+    place_heat(blocks - 1)
     three = dot_lanes(lhs[...], rhs[...])
     sums[...] = three[0:part] + three[part : 2 * part] + three[2 * part : 3 * part]
     route[...] = jnp.zeros_like(route)
@@ -473,127 +479,131 @@
             ret_ref[d, q : q + 1, :] = jnp.sum(jnp.where(highs == hi, x, 0.0), axis=0, keepdims=True)
 
 
-def bulk_kernel(solid, material, w, ra, rb, out, low_ref, u0, m0, ua, ub, ka, kb, k0, k1, fin, sem):
-    count, cols = solid.shape
+def bulk_kernel(is_back, start, chunk, solid, material, w, *refs):
+    if is_back:
+        ra, rb, _, fin, u0, m0, ua, ub, ka, kb, k0, k1, sem = refs
+    else:
+        out, token, u0, m0, ua, ub, ka, kb, k0, k1, fin, sem = refs
+    count, cols = u0.shape
     nt = cols // LANES
-    groups = sem.shape[1]
-    size = count // groups
-    blocks = size // TALL
+    skip = ROWS if is_back else 0
     copies = []
-    for g in range(groups):
-        at = pl.ds(g * size, size)
-        copies.append(pltpu.make_async_copy(solid.at[at], u0.at[at], sem.at[0, g]))
-        copies.append(pltpu.make_async_copy(material.at[at], m0.at[at], sem.at[1, g]))
+    for g in range(count // chunk):
+        here, there = pl.ds(start + g * chunk, chunk), pl.ds(g * chunk, chunk)
+        copies.append(pltpu.make_async_copy(solid.at[here], u0.at[there], sem.at[0, g]))
+        copies.append(pltpu.make_async_copy(material.at[here], m0.at[there], sem.at[1, g]))
     for copy in copies:
         copy.start()
-    uh, kh = halo_tiles(w[...])
+    uh, kh = halo_tiles(w[start : start + count, :])
     ua[nt, ROWS : ROWS + count, :] = SCALE * uh
     k0[nt] = SHARE * kh
     zero = jnp.zeros((ROWS, LANES), F32)
     for ct in range(nt + 1):
         at = slice(ct * LANES, (ct + 1) * LANES)
-        is_even = even("passage")
-        below = SCALE * jnp.where(is_even, ra[1:2, at], rb[1:2, at])
-        below_k = SHARE * jnp.where(is_even, ra[9:10, at], rb[9:10, at]) * jnp.exp2(below)
+        if is_back:
+            is_even = even("passage")
+            below = SCALE * jnp.where(is_even, ra[1:2, at], rb[1:2, at])
+            below_k = SHARE * jnp.where(is_even, ra[9:10, at], rb[9:10, at]) * jnp.exp2(below)
         for u, k in ((ua, ka), (ub, kb)):
             u[ct, 0:ROWS, :] = zero
             k[ct, 0:ROWS, :] = zero
-            u[ct, ROWS + count : ROWS + count + 1, :] = below
-            k[ct, ROWS + count : ROWS + count + 1, :] = below_k
-    lane = iota((TALL, LANES), 1)
-    edge = lane == LANES - 1
-
-    def begin(i, carry):
-        r0 = i * TALL
+            u[ct, ROWS + count : 2 * ROWS + count, :] = zero
+            k[ct, ROWS + count : 2 * ROWS + count, :] = zero
+            if is_back:
+                u[ct, ROWS + count : ROWS + count + 1, :] = below
+                k[ct, ROWS + count : ROWS + count + 1, :] = below_k
+    if not is_back:
+        token[...] = zero
+    edge = iota((chunk, LANES), 1) == LANES - 1
+
+    def begin(r0):
         bases = []
         for ct in range(nt + 1):
             if ct < nt:
                 at = slice(ct * LANES, (ct + 1) * LANES)
-                here = SCALE * u0[pl.ds(r0, TALL), at]
-                base = base_conductivity(m0[pl.ds(r0, TALL), at], SHARE)
-                ua[ct, pl.ds(ROWS + r0, TALL), :] = here
-                k0[ct, pl.ds(r0, TALL), :] = base
+                here = SCALE * u0[pl.ds(r0, chunk), at]
+                base = base_conductivity(m0[pl.ds(r0, chunk), at], SHARE)
+                ua[ct, pl.ds(ROWS + r0, chunk), :] = here
+                k0[ct, pl.ds(r0, chunk), :] = base
             else:
-                here = ua[ct, pl.ds(ROWS + r0, TALL), :]
-                base = k0[ct, pl.ds(r0, TALL), :]
-            ka[ct, pl.ds(ROWS + r0, TALL), :] = base * jnp.exp2(here)
+                here = ua[ct, pl.ds(ROWS + r0, chunk), :]
+                base = k0[ct, pl.ds(r0, chunk), :]
+            ka[ct, pl.ds(ROWS + r0, chunk), :] = base * jnp.exp2(here)
             bases.append(base)
         turned = [pltpu.roll(x, LANES - 1, 1) for x in bases]
         for ct in range(nt + 1):
-            k1[ct, pl.ds(r0, TALL), :] = jnp.where(edge, turned[(ct + 1) % (nt + 1)], turned[ct])
-        return carry
-
-    for g in range(groups):
+            k1[ct, pl.ds(r0, chunk), :] = jnp.where(edge, turned[(ct + 1) % (nt + 1)], turned[ct])
+
+    for g in range(count // chunk):
         copies[2 * g].wait()
         copies[2 * g + 1].wait()
-        for i in range(g * blocks, (g + 1) * blocks):
-            begin(i, 0)
-
-    def substep(u, k, nu, nk, final):
-        tall = TALL if final else count
+        begin(g * chunk)
+
+    def substep(u, k, nu, nk, r0, tall, final):
         lane = iota((tall, LANES), 1)
         edge = lane == LANES - 1
-
-        def body(i, carry):
-            r0 = i * tall
-            at = pl.ds(ROWS + r0, tall)
-            north, south = pl.ds(ROWS - 1 + r0, tall), pl.ds(ROWS + 1 + r0, tall)
-            here = [u[ct, at, :] for ct in range(nt + 1)]
-            cond = [k[ct, at, :] for ct in range(nt + 1)]
-            turned = [pltpu.roll(x, LANES - 1, 1) for x in here]
-            across = []
-            for ct in range(nt + 1):
-                nearby = jnp.where(edge, turned[(ct + 1) % (nt + 1)], turned[ct])
-                nearby_k = k1[ct, pl.ds(r0, tall), :] * jnp.exp2(nearby)
-                across.append((cond[ct] + nearby_k) * (nearby - here[ct]))
-            back = [pltpu.roll(x, 1, 1) for x in across]
-            for ct in range(nt if final else nt + 1):
-                flux = across[ct] - jnp.where(lane == 0, back[ct - 1], back[ct])
-                flux = flux + (cond[ct] + k[ct, north, :]) * (u[ct, north, :] - here[ct])
-                flux = flux + (cond[ct] + k[ct, south, :]) * (u[ct, south, :] - here[ct])
-                if ct == nt:
-                    flux = jnp.where(k0[ct, pl.ds(r0, tall), :] > 0, flux, 0.0)
-                new = here[ct] + flux
-                if final:
-                    fin[pl.ds(r0, tall), ct * LANES : (ct + 1) * LANES] = new * (1.0 / SCALE)
-                else:
-                    nu[ct, at, :] = new
-                    nk[ct, at, :] = k0[ct, pl.ds(r0, tall), :] * jnp.exp2(new)
-            return carry
-
-        return body
+        at = pl.ds(ROWS + r0, tall)
+        north, south = pl.ds(ROWS - 1 + r0, tall), pl.ds(ROWS + 1 + r0, tall)
+        here = [u[ct, at, :] for ct in range(nt + 1)]
+        cond = [k[ct, at, :] for ct in range(nt + 1)]
+        turned = [pltpu.roll(x, LANES - 1, 1) for x in here]
+        across = []
+        for ct in range(nt + 1):
+            nearby = jnp.where(edge, turned[(ct + 1) % (nt + 1)], turned[ct])
+            nearby_k = k1[ct, pl.ds(r0, tall), :] * jnp.exp2(nearby)
+            across.append((cond[ct] + nearby_k) * (nearby - here[ct]))
+        back = [pltpu.roll(x, 1, 1) for x in across]
+        for ct in range(nt if final else nt + 1):
+            flux = across[ct] - jnp.where(lane == 0, back[ct - 1], back[ct])
+            flux = flux + (cond[ct] + k[ct, north, :]) * (u[ct, north, :] - here[ct])
+            flux = flux + (cond[ct] + k[ct, south, :]) * (u[ct, south, :] - here[ct])
+            if ct == nt:
+                flux = jnp.where(k0[ct, pl.ds(r0, tall), :] > 0, flux, 0.0)
+            new = here[ct] + flux
+            if final:
+                fin[pl.ds(r0 - skip, tall), ct * LANES : (ct + 1) * LANES] = new * (1.0 / SCALE)
+            else:
+                nu[ct, at, :] = new
+                nk[ct, at, :] = k0[ct, pl.ds(r0, tall), :] * jnp.exp2(new)
 
     for step in range(SUBSTEPS - 1):
         u, k, nu, nk = (ua, ka, ub, kb) if step % 2 == 0 else (ub, kb, ua, ka)
-        substep(u, k, nu, nk, False)(0, 0)
+        substep(u, k, nu, nk, 0, count, False)
     last = (ua, ka, ub, kb) if SUBSTEPS % 2 == 1 else (ub, kb, ua, ka)
+    if is_back:
+        substep(*last, skip, count - skip, True)
+        return
     outs = []
-    for g in range(groups):
-        for i in range(g * blocks, (g + 1) * blocks):
-            substep(*last, True)(i, 0)
-        at = pl.ds(g * size, size)
+    for g in range(count // chunk):
+        tall = chunk - (ROWS if (g + 1) * chunk == count else 0)
+        substep(*last, g * chunk, tall, True)
+        at = pl.ds(g * chunk, tall)
         outs.append(pltpu.make_async_copy(fin.at[at], out.at[at], sem.at[0, g]))
         outs[-1].start()
-    low_ref[...] = fin[count - ROWS : count, :]
     for copy in outs:
         copy.wait()
 
 
-def finish_kernel(recv, slot, below, low, top, solid, wall_ref, out, tabl, edge, sem):
+def finish_kernel(recv, slot, below, back, top, solid, wall_ref, out, tabl, edge, sem):
     devices, per_owner = recv.shape[0], recv.shape[1]
     rows = solid.shape[0]
     nt = below.shape[1]
+    most = back.shape[0] - ROWS
+    stores = [
+        pltpu.make_async_copy(top, out.at[pl.ds(0, ROWS)], sem.at[0]),
+        pltpu.make_async_copy(back.at[pl.ds(0, most)], out.at[pl.ds(rows - ROWS - most, most)], sem.at[1]),
+        pltpu.make_async_copy(edge, out.at[pl.ds(rows - ROWS, ROWS)], sem.at[2]),
+    ]
+    for store in stores[:2]:
+        store.start()
     last = lax.axis_index("passage") == lax.axis_size("passage") - 1
-    put = pltpu.make_async_copy(top, out.at[pl.ds(0, ROWS)], sem.at[1])
-    put.start()
-    edge[...] = low[...]
+    edge[...] = back[most : most + ROWS, :]
     for j in range(EDGE):
         row = ROWS - EDGE + j
         for ct in range(nt):
             at = slice(ct * LANES, (ct + 1) * LANES)
-            edge[row : row + 1, at] = jnp.where(last, low[row : row + 1, at], below[j, ct : ct + 1, :])
-    store = pltpu.make_async_copy(edge, out.at[pl.ds(rows - ROWS, ROWS)], sem.at[0])
-    store.start()
+            edge[row : row + 1, at] = jnp.where(last, edge[row : row + 1, at], below[j, ct : ct + 1, :])
+    stores[2].start()
     for d in range(devices):
         tabl[d * per_owner : (d + 1) * per_owner, :] = recv[d]
     table = tabl.shape[0]
@@ -606,8 +616,8 @@
         x = x[0:table] + x[table : 2 * table] + x[2 * table : 3 * table]
         hi = lax.shift_right_logical(place, 7)
         wall_ref[b : b + 1, :] = jnp.sum(jnp.where(highs == hi, x, 0.0), axis=0, keepdims=True)
-    put.wait()
-    store.wait()
+    for store in stores:
+        store.wait()
 
 
 def shards(gas, gas_speed, solid, material, face_cell, face_owner, face_surface, film, wall_previous):
@@ -723,19 +733,30 @@
     )
     recv = lax.all_to_all(route, ("passage", "tile"), 0, 0, tiled=True)
 
-    bulk, low = pl.pallas_call(
-        bulk_kernel,
-        in_specs=[whole(pltpu.HBM)] * 2 + [whole()] * 3,
-        out_specs=[whole(pltpu.HBM), whole()],
-        out_shape=[shape((rows, cols)), shape((ROWS, cols))],
-        scratch_shapes=[VMEM((rows, cols), F32), VMEM((rows, cols), jnp.int32)]
-        + [VMEM(ringed, F32)] * 4
-        + [VMEM((nt + 1, rows, LANES), F32)] * 2
-        + [VMEM((rows, cols), F32), pltpu.SemaphoreType.DMA((2, 4))],
-        compiler_params=params(52),
-        name="solid_bulk",
-        cost_estimate=cost(60000000, 30000000),
-    )(solid, material, w, ra, rb)
+    behind = rows * 3 // 8 // ROWS * ROWS
+    front = rows - behind + ROWS
+    chunk = front // 3 if front % (3 * ROWS) == 0 else ROWS
+
+    def bulk_part(is_back, start, count, chunk, outs, specs, *more):
+        kept = [] if is_back else [VMEM((count, cols), F32)]
+        return pl.pallas_call(
+            functools.partial(bulk_kernel, is_back, start, chunk),
+            in_specs=[whole(pltpu.HBM)] * 2 + [whole()] * (1 + len(more)),
+            out_specs=specs,
+            out_shape=outs,
+            scratch_shapes=[VMEM((count, cols), F32), VMEM((count, cols), jnp.int32)]
+            + [VMEM((nt + 1, count + 2 * ROWS, LANES), F32)] * 4
+            + [VMEM((nt + 1, count, LANES), F32)] * 2
+            + kept
+            + [pltpu.SemaphoreType.DMA((2, count // chunk))],
+            compiler_params=params(52),
+            name="solid_bulk",
+            cost_estimate=cost(60000000, 30000000),
+        )(solid, material, w, *more)
+
+    bulk, token = bulk_part(
+        False, 0, front, chunk, [shape((rows, cols)), shape((ROWS, LANES))], [whole(pltpu.HBM), whole()]
+    )
 
     slots = table * LANES
     top, up, ret = pl.pallas_call(
@@ -756,10 +777,13 @@
         compiler_params=params(52),
         name="solid_strip",
         cost_estimate=cost(20000000, 4000000),
-    )(recv, ra, rb, w, solid, material, low)
+    )(recv, ra, rb, w, solid, material, token)
     ret = lax.all_to_all(ret, ("passage", "tile"), 0, 0, tiled=True)
     below = lax.ppermute(up, "passage", [(i + 1, i) for i in range(passages - 1)])
 
+    (back,) = bulk_part(
+        True, rows - behind - ROWS, behind + ROWS, behind + ROWS, [shape((behind, cols))], [whole()], ra, rb, top
+    )
     wall, solid_next = pl.pallas_call(
         finish_kernel,
         in_specs=[whole()] * 5 + [whole(pltpu.HBM)],
@@ -769,12 +793,12 @@
         scratch_shapes=[
             VMEM((table, LANES), F32),
             VMEM((ROWS, cols), F32),
-            pltpu.SemaphoreType.DMA((2,)),
+            pltpu.SemaphoreType.DMA((3,)),
         ],
         compiler_params=params(24),
         name="wall_temperatures",
         cost_estimate=cost(20000000, 4000000),
-    )(ret, slot, below, low, top, bulk)
+    )(ret, slot, below, back, top, bulk)
     return gas_next, solid_next, wall.reshape(faces)
 
 

time: 62.2 us -> 58.9 us (0.947)
  waiting for transfers between devices: 5.96 us -> 2.05 us
  Pallas kernels: 32.1 us -> 33.3 us
  starting transfers between devices: 22.8 us -> 22.1 us
    ppermute x1, waiting for transfers between devices: 4.43 us -> 0.01 us  [shards(): lax.ppermute(up, 'passage', [(i + 1, i) for i in range(passages - 1)])]
    pallas_call x1 -> x2, Pallas kernels: 10.5 us -> 11.7 us  [bulk_part(): pl.pallas_call(functools.partial(bulk_kernel, is_back, start, chunk), in_...]
    all_to_all x1, waiting for transfers between devices: 0.01 us -> 0.88 us  [shards(): recv = lax.all_to_all(route, ('passage', 'tile'), 0, 0, tiled=True)]
    all_to_all x1, starting transfers between devices: 5.67 us -> 4.8 us  [shards(): ret = lax.all_to_all(ret, ('passage', 'tile'), 0, 0, tiled=True)]
  transfers between devices with their start and end apart: 7 -> 7, of which waited for: 2 -> 2; matrix products, arithmetic and copies ran while one was open for 0% -> 0% of each run, Pallas kernels for 25% -> 29%
where the time goes in v5:
time: 58.9 us; the launch traced here: 58.5 us
  Pallas kernels  33.3 us (57%)
  starting transfers between devices  22.1 us (38%)
  waiting for transfers between devices  2.05 us (3%)
  between operations  1.02 us (2%)
    pallas_call x2, Pallas kernels, bulk_part(): pl.pallas_call(functools.partial(bulk_kernel, is_back, start, chunk), in_...  11.7 us
    all_to_all x1, starting transfers between devices, shards(): recv = lax.all_to_all(route, ('passage', 'tile'), 0, 0, tiled=True)  11.2 us
    pallas_call x1, Pallas kernels, shards(): pl.pallas_call(functools.partial(gas_kernel, tiles, per_owner), in_specs=...  8.1 us
    all_to_all x1, starting transfers between devices, shards(): ret = lax.all_to_all(ret, ('passage', 'tile'), 0, 0, tiled=True)  4.8 us
    pallas_call x1, Pallas kernels, shards(): pl.pallas_call(functools.partial(strip_kernel, per_owner), in_specs=[whol...  4.27 us
    ppermute x2, starting transfers between devices, run(): lax.ppermute(one, axis, both(first))  3.15 us
    pallas_call x1, Pallas kernels, shards(): pl.pallas_call(fetch, in_specs=[whole(pltpu.HBM)] * 2, out_specs=[whole()...  2.24 us
    pallas_call x1, Pallas kernels, shards(): pl.pallas_call(finish_kernel, in_specs=[whole()] * 5 + [whole(pltpu.HBM)]...  1.82 us
  transfers between devices with their start and end apart: 7, of which 2 were waited for; matrix products, arithmetic and copies ran while one was open for 0% of the time, Pallas kernels for 29%

profile of v5, /device:TPU:0, one launch (start us, length us, event | category | flops | bytes accessed | tf_op | source)
XLA Modules:
  0.0 58.5 jit_solution(11005293302023412303)
XLA Ops:
  0.6 1.8 %pack_columns.1 = (f32[16,256]{1,0:T(8,128)S(1)}, f32[16,256]{1,0:T(8,128)S(1)}, f32[6,8,2048]{2,1,0:T(8,128)S(1)}, s32[2,8,2048]{2,1,0:T(8,128)S(1)}) custom-call(f32[256,2048]{1,0:T(8,128)} %gas.3, f32[256,2048]{1,0:T(8,128)} %speed.3, f32[256,2048]{1,0:T(8,128)} %solid.7, s32[256,2048]{1,0:T(8,128)} %material.7), custom_call_target="tpu_custom_call" | custom-call | flops 1000000 | bytes 1048576 | tf_op jit(solution)/shard_map/pack_columns/pallas_call | solution.py:642
  2.4 0.5 collective-permute-start
  3.0 0.0 copy-start
  3.0 0.8 %collective-permute-start.1 = (f32[16,256]{1,0:T(8,128)S(1)}, f32[16,256]{1,0:T(8,128)S(1)}, u32[]{:S(2)}, u32[]{:S(2)}) collective-permute-start(f32[16,256]{1,0:T(8,128)S(1)} %get-tuple-element.28), channel_id=1, source_target_pairs={{1,2},{2,1},{5,6},{6,5},{9,10},{10,9},{13,14},{14,13},{17,18},{18,... | collective-permute-start | bytes 49160 | tf_op jit(solution)/shard_map/ppermute | solution.py:73
  3.8 2.2 %fetch.1 = (f32[256,2048]{1,0:T(8,128)S(1)}, f32[256,2048]{1,0:T(8,128)S(1)}, f32[8,128]{1,0:T(8,128)S(1)}) custom-call(f32[256,2048]{1,0:T(8,128)} %gas.3, f32[256,2048]{1,0:T(8,128)} %speed.3), custom_call_target="tpu_custom_call" | custom-call | bytes 8388608 | tf_op jit(solution)/shard_map/fetch/pallas_call | solution.py:658
  6.0 0.0 collective-permute-done.one
  6.0 0.0 collective-permute-done.1.two
  6.0 0.3 pack_rows.1
  6.3 2.6 %collective-permute-start.2 = (f32[16,2176]{1,0:T(8,128)S(1)}, f32[16,2176]{1,0:T(8,128)S(1)}, u32[]{:S(2)}, u32[]{:S(2)}) collective-permute-start(f32[16,2176]{1,0:T(8,128)S(1)} %get-tuple-element.33), channel_id=1, source_target_pairs={{0,4},{8,12},{16,20},{24,28},{4,0},{12,8},{20,16},{28,24},{1,5},{9... | collective-permute-start | bytes 417800 | tf_op jit(solution)/shard_map/ppermute | solution.py:73
  9.0 0.7 %collective-permute-start.3 = (f32[16,2176]{1,0:T(8,128)S(1)}, f32[16,2176]{1,0:T(8,128)S(1)}, u32[]{:S(2)}, u32[]{:S(2)}) collective-permute-start(f32[16,2176]{1,0:T(8,128)S(1)} %get-tuple-element.34), channel_id=1, source_target_pairs={{4,8},{12,16},{20,24},{8,4},{16,12},{24,20},{5,9},{13,17},{21,25},... | collective-permute-start | bytes 417800 | tf_op jit(solution)/shard_map/ppermute | solution.py:73
  9.6 0.0 copy-done
  9.6 0.0 copy-done.1
  9.6 0.0 copy-done.2
  9.6 1.3 %find_slots.1 = (s32[32,128]{1,0:T(8,128)S(1)}, s32[32,128]{1,0:T(8,128)S(1)}, f32[64,128]{1,0:T(8,128)S(1)}) custom-call(s32[32,128]{1,0:T(8,128)S(1)} %bitcast.7, s32[32,128]{1,0:T(8,128)S(1)} %bitcast.9, s32[32,128]{1,0:T(8,128)S(1)} %bitcast.11), custom_call_target="tpu_custom_call" | custom-call | flops 20000000 | bytes 1000000 | tf_op jit(solution)/shard_map/find_slots/pallas_call | solution.py:684
  10.9 0.0 copy-start.3
  10.9 0.0 copy-start.4
  10.9 1.8 %first_section.1.sone = f32[17,272,128]{2,1,0:T(8,128)S(1)} custom-call(f32[256,2048]{1,0:T(8,128)S(1)} %get-tuple-element.25.gas, f32[256,2048]{1,0:T(8,128)S(1)} %get-tuple-element.26.speed, f32[256,128]{1,0:T(8,128)S(1)} %get-tuple-element.32.w), custom_call_target="tpu_custom_call" | custom-call | flops 8000000 | bytes 6000000 | tf_op jit(solution)/shard_map/first_section/pallas_call | solution.py:701
  12.7 0.0 collective-permute-done.2.ra.refs_0_
  12.7 0.0 collective-permute-done.3.rb.refs_1_
  12.7 0.0 copy-done.3
  12.8 0.0 copy-done.4
  12.8 8.1 %gas_and_heat.1 = (f32[256,2048]{1,0:T(8,128)}, f32[32,8,128]{2,1,0:T(8,128)}, f32[17,272,128]{2,1,0:T(8,128)S(1)}) custom-call(f32[256,2048]{1,0:T(8,128)S(1)} %get-tuple-element.25.gas, f32[256,2048]{1,0:T(8,128)S(1)} %get-tuple-element.26.speed, f32[17,272,128]{2,1,0:T(8,128)S(1)} %first_section.1.sone, ...), custom_call_target="tpu_custom_call", output_to_operand_aliasing={{2}: (2, {})} | custom-call | flops 60000000 | bytes 40000000 | tf_op jit(solution)/shard_map/gas_and_heat/pallas_call | solution.py:711
  20.9 11.2 %all-to-all-start = ((f32[32,8,128]{2,1,0:T(8,128)}), f32[32,8,128]{2,1,0:T(8,128)S(1)}, u32[]{:S(2)}, u32[]{:S(2)}) async-start(f32[32,8,128]{2,1,0:T(8,128)} %get-tuple-element.39), calls=%async_computation | async-start | bytes 262144 | tf_op jit(solution)/shard_map/all_to_all | solution.py:734
  32.1 7.2 %solid_bulk.2 = (f32[256,2048]{1,0:T(8,128)}, f32[8,128]{1,0:T(8,128)S(1)}) custom-call(f32[256,2048]{1,0:T(8,128)} %solid.7, s32[256,2048]{1,0:T(8,128)} %material.7, f32[256,128]{1,0:T(8,128)S(1)} %get-tuple-element.32.w), custom_call_target="tpu_custom_call" | custom-call | flops 60000000 | bytes 30000000 | tf_op jit(solution)/shard_map/solid_bulk/pallas_call | solution.py:742
  39.3 0.9 %all-to-all-done.recv = f32[32,8,128]{2,1,0:T(8,128)S(1)} async-done(((f32[32,8,128]{2,1,0:T(8,128)}), f32[32,8,128]{2,1,0:T(8,128)S(1)}, u32[]{:S(2)}, u32[]{:S(2)}) %all-to-all-start) | async-done | bytes 131104 | tf_op jit(solution)/shard_map/all_to_all | solution.py:734
  40.2 4.3 %solid_strip.1 = (f32[8,2048]{1,0:T(8,128)S(1)}, f32[3,16,128]{2,1,0:T(8,128)S(1)}, f32[32,2,128]{2,1,0:T(2,128)}) custom-call(f32[32,8,128]{2,1,0:T(8,128)S(1)} %all-to-all-done.recv, f32[16,2176]{1,0:T(8,128)S(1)} %collective-permute-done.2.ra.refs_0_, f32[16,2176]{1,0:T(8,128)S(1)} %collective-permute-done.3.rb.refs_1_, ...), custom_call_target="tpu_custom_call" | custom-call | flops 20000000 | bytes 4000000 | tf_op jit(solution)/shard_map/solid_strip/pallas_call | solution.py:762
  44.4 4.8 %all-to-all-start.1 = ((f32[32,2,128]{2,1,0:T(2,128)}), f32[32,2,128]{2,1,0:T(2,128)S(1)}, u32[]{:S(2)}, u32[]{:S(2)}) async-start(f32[32,2,128]{2,1,0:T(2,128)} %get-tuple-element.41), calls=%async_computation.1 | async-start | bytes 65536 | tf_op jit(solution)/shard_map/all_to_all | solution.py:781
  49.2 1.5 %collective-permute-start.4 = (f32[3,16,128]{2,1,0:T(8,128)S(1)}, f32[3,16,128]{2,1,0:T(8,128)S(1)}, u32[]{:S(2)}, u32[]{:S(2)}) collective-permute-start(f32[3,16,128]{2,1,0:T(8,128)S(1)} %get-tuple-element.42), channel_id=1, source_target_pairs={{4,0},{8,4},{12,8},{16,12},{20,16},{24,20},{28,24},{5,1},{9,5},{13... | collective-permute-start | bytes 73736 | tf_op jit(solution)/shard_map/ppermute | solution.py:782
  50.8 4.6 %solid_bulk.3.back = f32[96,2048]{1,0:T(8,128)S(1)} custom-call(f32[256,2048]{1,0:T(8,128)} %solid.7, s32[256,2048]{1,0:T(8,128)} %material.7, f32[256,128]{1,0:T(8,128)S(1)} %get-tuple-element.32.w, f32[16,2176]{1,0:T(8,128)S(1)} %collective-permute-done.2.ra.refs_0_, f32[16,2176]{1,0:T(8,128)S(1)} %collective-permute-done.3.rb.refs_1_, ...), custom_call_target="tpu_custom_call" | custom-call | flops 60000000 | bytes 30000000 | tf_op jit(solution)/shard_map/solid_bulk/pallas_call | solution.py:742
  55.3 0.0 collective-permute-done.4.below
  55.3 1.2 %all-to-all-done.1.recv = f32[32,2,128]{2,1,0:T(2,128)S(1)} async-done(((f32[32,2,128]{2,1,0:T(2,128)}), f32[32,2,128]{2,1,0:T(2,128)S(1)}, u32[]{:S(2)}, u32[]{:S(2)}) %all-to-all-start.1) | async-done | bytes 32800 | tf_op jit(solution)/shard_map/all_to_all | solution.py:781
  56.5 1.8 %wall_temperatures.1 = (f32[32,128]{1,0:T(8,128)}, f32[256,2048]{1,0:T(8,128)}) custom-call(f32[32,2,128]{2,1,0:T(2,128)S(1)} %all-to-all-done.1.recv, s32[32,128]{1,0:T(8,128)S(1)} %get-tuple-element.36.slot, f32[3,16,128]{2,1,0:T(8,128)S(1)} %collective-permute-done.4.below, f32[96,2048]{1,0:T(8,128)S(1)} %solid_bulk.3.back, ...), custom_call_target="tpu_custom_call", output_to_operand_aliasing={{1}: (5, {})} | custom-call | flops 20000000 | bytes 4000000 | tf_op jit(solution)/shard_map/wall_temperatures/pallas_call | solution.py:787
  (2 shorter events, 0.0 us)
Async XLA Ops:
  2.4 3.6 %collective-permute-start = (f32[16,256]{1,0:T(8,128)S(1)}, f32[16,256]{1,0:T(8,128)S(1)}, u32[]{:S(2)}, u32[]{:S(2)}) collective-permute-start(f32[16,256]{1,0:T(8,128)S(1)} %get-tuple-element.27), channel_id=1, source_target_pairs={{0,1},{2,3},{1,0},{3,2},{4,5},{6,7},{5,4},{7,6},{8,9},{10,11},{9,8... | collective-permute-start | bytes 49160 | tf_op jit(solution)/shard_map/ppermute | solution.py:73
  3.0 6.7 %copy-start = (s32[4096,1]{0,1:T(1,128)S(1)}, s32[4096,1]{0,1:T(1,128)}, u32[]{:S(2)}) copy-start(s32[4096,1]{0,1:T(1,128)} %param.14) | copy-start | bytes 49156
  3.0 6.7 %copy-start.1 = (s32[4096]{0:T(1024)S(1)}, s32[4096]{0:T(1024)}, u32[]{:S(2)}) copy-start(s32[4096]{0:T(1024)} %param.15) | copy-start | bytes 49156
  3.0 6.7 %copy-start.2 = (s32[4096]{0:T(1024)S(1)}, s32[4096]{0:T(1024)}, u32[]{:S(2)}) copy-start(s32[4096]{0:T(1024)} %param.13) | copy-start | bytes 49156
  3.0 3.1 %collective-permute-start.1 = (f32[16,256]{1,0:T(8,128)S(1)}, f32[16,256]{1,0:T(8,128)S(1)}, u32[]{:S(2)}, u32[]{:S(2)}) collective-permute-start(f32[16,256]{1,0:T(8,128)S(1)} %get-tuple-element.28), channel_id=1, source_target_pairs={{1,2},{2,1},{5,6},{6,5},{9,10},{10,9},{13,14},{14,13},{17,18},{18,... | collective-permute-start | bytes 49160 | tf_op jit(solution)/shard_map/ppermute | solution.py:73
  6.3 6.4 %collective-permute-start.2 = (f32[16,2176]{1,0:T(8,128)S(1)}, f32[16,2176]{1,0:T(8,128)S(1)}, u32[]{:S(2)}, u32[]{:S(2)}) collective-permute-start(f32[16,2176]{1,0:T(8,128)S(1)} %get-tuple-element.33), channel_id=1, source_target_pairs={{0,4},{8,12},{16,20},{24,28},{4,0},{12,8},{20,16},{28,24},{1,5},{9... | collective-permute-start | bytes 417800 | tf_op jit(solution)/shard_map/ppermute | solution.py:73
  9.0 3.8 %collective-permute-start.3 = (f32[16,2176]{1,0:T(8,128)S(1)}, f32[16,2176]{1,0:T(8,128)S(1)}, u32[]{:S(2)}, u32[]{:S(2)}) collective-permute-start(f32[16,2176]{1,0:T(8,128)S(1)} %get-tuple-element.34), channel_id=1, source_target_pairs={{4,8},{12,16},{20,24},{8,4},{16,12},{24,20},{5,9},{13,17},{21,25},... | collective-permute-start | bytes 417800 | tf_op jit(solution)/shard_map/ppermute | solution.py:73
  10.9 1.8 %copy-start.3 = (f32[4096]{0:T(1024)S(1)}, f32[4096]{0:T(1024)}, u32[]{:S(2)}) copy-start(f32[4096]{0:T(1024)} %param.16) | copy-start | bytes 49156
  10.9 1.8 %copy-start.4 = (f32[4096]{0:T(1024)S(1)}, f32[4096]{0:T(1024)}, u32[]{:S(2)}) copy-start(f32[4096]{0:T(1024)} %param.17) | copy-start | bytes 49156
  20.9 19.3 %all-to-all-start = ((f32[32,8,128]{2,1,0:T(8,128)}), f32[32,8,128]{2,1,0:T(8,128)S(1)}, u32[]{:S(2)}, u32[]{:S(2)}) async-start(f32[32,8,128]{2,1,0:T(8,128)} %get-tuple-element.39), calls=%async_computation | async-start | bytes 262144 | tf_op jit(solution)/shard_map/all_to_all | solution.py:734
  44.4 12.1 %all-to-all-start.1 = ((f32[32,2,128]{2,1,0:T(2,128)}), f32[32,2,128]{2,1,0:T(2,128)S(1)}, u32[]{:S(2)}, u32[]{:S(2)}) async-start(f32[32,2,128]{2,1,0:T(2,128)} %get-tuple-element.41), calls=%async_computation.1 | async-start | bytes 65536 | tf_op jit(solution)/shard_map/all_to_all | solution.py:781
  49.2 6.1 %collective-permute-start.4 = (f32[3,16,128]{2,1,0:T(8,128)S(1)}, f32[3,16,128]{2,1,0:T(8,128)S(1)}, u32[]{:S(2)}, u32[]{:S(2)}) collective-permute-start(f32[3,16,128]{2,1,0:T(8,128)S(1)} %get-tuple-element.42), channel_id=1, source_target_pairs={{4,0},{8,4},{12,8},{16,12},{20,16},{24,20},{28,24},{5,1},{9,5},{13... | collective-permute-start | bytes 73736 | tf_op jit(solution)/shard_map/ppermute | solution.py:782

commit v6 on v5

--- a/solution.py
+++ b/solution.py
@@ -187,7 +187,7 @@
         b_ref[half * ROWS : (half + 1) * ROWS, :] = jnp.where(is_even, up[half], down[half])
 
 
-def find_slots(devices, per_owner, rows, cols, owner, surface, cell, slot_ref, row_ref, idx_ref, held, lhs, rhs):
+def find_slots(devices, per_owner, rows, cols, owner, surface, cell, slot_ref, row_ref, idx_ref, rhs, held, lhs):
     blocks = owner.shape[0]
     owners = iota((devices, LANES), 0)
     for b in range(blocks):
@@ -215,8 +215,11 @@
         at = slice(b * LANES, (b + 1) * LANES)
         lhs[0:table, at] = jnp.where(highs == hi, coarse, 0.0).astype(BF16)
         lhs[table : 2 * table, at] = jnp.where(highs == hi, fine, 0.0).astype(BF16)
-        rhs[:, at] = jnp.where(lows == lo, 1.0, 0.0).astype(BF16)
-    both = dot_lanes(lhs[...], rhs[...])
+        line, col = lax.div(value, cols), lax.rem(value, cols)
+        code = jnp.where(col >= cols - EDGE, col - (cols - EDGE), 16 + col) + 8 * line
+        rhs[0:LANES, at] = jnp.where(lows == lo, 1.0, 0.0).astype(BF16)
+        rhs[LANES : LANES + 32, at] = jnp.where(iota((32, LANES), 0) == code, 1.0, 0.0).astype(BF16)
+    both = dot_lanes(lhs[...], rhs[0:LANES, :])
     idx_ref[...] = both[0:table] + both[table : 2 * table]
     place = cell[...]
     row_ref[...] = lax.div(lax.rem(place, cols), LANES) * rows + lax.div(place, cols)
@@ -284,8 +287,8 @@
 
 
 def gas_kernel(
-    tiles_across, per_owner, gas, speed, sone, w, ra, rb, where_at, cell, owner, surface, slot, film, wall, idx,
-    out, route, s1, tab, final, stage, lhs, rhs, sums, rowidx, sem,
+    tiles_across, per_owner, gas, speed, sone, w, ra, rb, where_at, cell, owner, surface, slot, film, wall, idx, rhs,
+    out, route, s1, tab, final, stage, lhs, sums, rowidx, sem,
 ):
     rows, cols = gas.shape
     nt = cols // LANES
@@ -363,30 +366,31 @@
         heat = split3(film[one, :] * (face - wall[one, :]))
         place_of = slot[one, :]
         hi = lax.shift_right_logical(place_of, 7)
-        lo = place_of & (LANES - 1)
         mine = owner[one, :]
         voxel = surface[one, :]
-        line = lax.div(voxel, cols)
         col = lax.rem(voxel, cols)
         tile = lax.rem(mine, tiles_across)
         to_right = (col >= cols - EDGE) & (tile < tiles_across - 1)
         to_left = (col < EDGE) & (tile > 0)
         dest = jnp.where(to_right, mine + 1, jnp.where(to_left, mine - 1, -1))
-        code = jnp.where(to_right, col - (cols - EDGE), 16 + col) + 8 * line
         for k in range(3):
             lhs[k * part : k * part + table, at] = jnp.where(highs == hi, heat[k], 0.0).astype(BF16)
             lhs[k * part + table : (k + 1) * part, at] = jnp.where(owners == dest, heat[k], 0.0).astype(BF16)
-        rhs[0:LANES, at] = jnp.where(lanes_down == lo, 1.0, 0.0).astype(BF16)
-        rhs[LANES : LANES + 32, at] = jnp.where(iota((32, LANES), 0) == code, 1.0, 0.0).astype(BF16)
-
-    def both(b, carry):
-        place_heat(b - 1)
-        gather(b)
+
+    several = 8
+
+    def both(i, carry):
+        for j in range(several):
+            place_heat((i - 1) * several + j)
+        for j in range(several):
+            gather(i * several + j)
         return carry
 
-    gather(0)
-    lax.fori_loop(1, blocks, both, 0)
-    place_heat(blocks - 1)
+    for j in range(several):
+        gather(j)
+    lax.fori_loop(1, blocks // several, both, 0)
+    for j in range(several):
+        place_heat(blocks - several + j)
     three = dot_lanes(lhs[...], rhs[...])
     sums[...] = three[0:part] + three[part : 2 * part] + three[2 * part : 3 * part]
     route[...] = jnp.zeros_like(route)
@@ -681,15 +685,19 @@
         return x.reshape(blocks, LANES)
 
     owner, surface, cell = folded(face_owner), folded(face_surface), folded(face_cell)
-    slot, rowidx, idx = pl.pallas_call(
+    slot, rowidx, idx, lanes_of = pl.pallas_call(
         functools.partial(find_slots, devices, per_owner, rows, cols),
         in_specs=[whole()] * 3,
-        out_specs=[whole()] * 3,
-        out_shape=[shape((blocks, LANES), jnp.int32), shape((blocks, LANES), jnp.int32), shape((table, LANES))],
+        out_specs=[whole()] * 4,
+        out_shape=[
+            shape((blocks, LANES), jnp.int32),
+            shape((blocks, LANES), jnp.int32),
+            shape((table, LANES)),
+            shape((LANES + 32, faces), BF16),
+        ],
         scratch_shapes=[
             VMEM((blocks * devices, LANES), BF16),
             VMEM((2 * table, faces), BF16),
-            VMEM((LANES, faces), BF16),
         ],
         compiler_params=params(24),
         name="find_slots",
@@ -710,7 +718,7 @@
     )(g0, s0, w)
     gas_next, route, _ = pl.pallas_call(
         functools.partial(gas_kernel, tiles, per_owner),
-        in_specs=[whole()] * 6 + [whole(pl.ANY)] + [whole()] * 7,
+        in_specs=[whole()] * 6 + [whole(pl.ANY)] + [whole()] * 8,
         out_specs=[whole(pltpu.HBM), whole(), whole()],
         out_shape=[shape((rows, cols)), shape((devices, ROUTE_ROWS, LANES)), shape(ringed)],
         input_output_aliases={2: 2},
@@ -719,7 +727,6 @@
             VMEM((rows, cols), F32),
             VMEM((faces, LANES), F32),
             VMEM((3 * part, faces), BF16),
-            VMEM((LANES + 32, faces), BF16),
             VMEM((part, LANES + 32), F32),
             pltpu.SMEM((faces,), jnp.int32),
             pltpu.SemaphoreType.DMA((2,)),
@@ -729,7 +736,7 @@
         cost_estimate=cost(60000000, 40000000),
     )(
         g0, s0, sone, w, ra, rb, rowidx.reshape(faces), cell, owner, surface, slot,
-        folded(film), folded(wall_previous), idx,
+        folded(film), folded(wall_previous), idx, lanes_of,
     )
     recv = lax.all_to_all(route, ("passage", "tile"), 0, 0, tiled=True)
 

time: 58.9 us -> 58.1 us (0.986)
  Pallas kernels: 33.3 us -> 32.7 us
    pallas_call x1, Pallas kernels: 8.1 us -> 7.37 us  [shards(): pl.pallas_call(functools.partial(gas_kernel, tiles, per_owner), in_specs=...]
  transfers between devices with their start and end apart: 7 -> 7, of which waited for: 2 -> 2; matrix products, arithmetic and copies ran while one was open for 0% -> 0% of each run, Pallas kernels for 29% -> 30%
where the time goes in v6:
time: 58.1 us; the launch traced here: 57.7 us
  Pallas kernels  32.7 us (56%)
  starting transfers between devices  22 us (38%)
  waiting for transfers between devices  2.05 us (4%)
  between operations  1.02 us (2%)
    pallas_call x2, Pallas kernels, bulk_part(): pl.pallas_call(functools.partial(bulk_kernel, is_back, start, chunk), in_...  11.7 us
    all_to_all x1, starting transfers between devices, shards(): recv = lax.all_to_all(route, ('passage', 'tile'), 0, 0, tiled=True)  11.1 us
    pallas_call x1, Pallas kernels, shards(): pl.pallas_call(functools.partial(gas_kernel, tiles, per_owner), in_specs=...  7.37 us
    all_to_all x1, starting transfers between devices, shards(): ret = lax.all_to_all(ret, ('passage', 'tile'), 0, 0, tiled=True)  4.8 us
    pallas_call x1, Pallas kernels, shards(): pl.pallas_call(functools.partial(strip_kernel, per_owner), in_specs=[whol...  4.27 us
    ppermute x2, starting transfers between devices, run(): lax.ppermute(one, axis, both(first))  3.15 us
    pallas_call x1, Pallas kernels, shards(): pl.pallas_call(fetch, in_specs=[whole(pltpu.HBM)] * 2, out_specs=[whole()...  2.24 us
    pallas_call x1, Pallas kernels, shards(): pl.pallas_call(finish_kernel, in_specs=[whole()] * 5 + [whole(pltpu.HBM)]...  1.82 us
  transfers between devices with their start and end apart: 7, of which 2 were waited for; matrix products, arithmetic and copies ran while one was open for 0% of the time, Pallas kernels for 30%

profile of v6, /device:TPU:0, one launch (start us, length us, event | category | flops | bytes accessed | tf_op | source)
XLA Modules:
  0.0 57.7 jit_solution(8370385803653487879)
XLA Ops:
  0.6 1.8 %pack_columns.1 = (f32[16,256]{1,0:T(8,128)S(1)}, f32[16,256]{1,0:T(8,128)S(1)}, f32[6,8,2048]{2,1,0:T(8,128)S(1)}, s32[2,8,2048]{2,1,0:T(8,128)S(1)}) custom-call(f32[256,2048]{1,0:T(8,128)} %gas.3, f32[256,2048]{1,0:T(8,128)} %speed.3, f32[256,2048]{1,0:T(8,128)} %solid.7, s32[256,2048]{1,0:T(8,128)} %material.7), custom_call_target="tpu_custom_call" | custom-call | flops 1000000 | bytes 1048576 | tf_op jit(solution)/shard_map/pack_columns/pallas_call | solution.py:646
  2.4 0.5 collective-permute-start
  3.0 0.0 copy-start
  3.0 0.8 %collective-permute-start.1 = (f32[16,256]{1,0:T(8,128)S(1)}, f32[16,256]{1,0:T(8,128)S(1)}, u32[]{:S(2)}, u32[]{:S(2)}) collective-permute-start(f32[16,256]{1,0:T(8,128)S(1)} %get-tuple-element.29), channel_id=1, source_target_pairs={{1,2},{2,1},{5,6},{6,5},{9,10},{10,9},{13,14},{14,13},{17,18},{18,... | collective-permute-start | bytes 49160 | tf_op jit(solution)/shard_map/ppermute | solution.py:73
  3.8 2.2 %fetch.1 = (f32[256,2048]{1,0:T(8,128)S(1)}, f32[256,2048]{1,0:T(8,128)S(1)}, f32[8,128]{1,0:T(8,128)S(1)}) custom-call(f32[256,2048]{1,0:T(8,128)} %gas.3, f32[256,2048]{1,0:T(8,128)} %speed.3), custom_call_target="tpu_custom_call" | custom-call | bytes 8388608 | tf_op jit(solution)/shard_map/fetch/pallas_call | solution.py:662
  6.0 0.0 collective-permute-done.one
  6.0 0.0 collective-permute-done.1.two
  6.0 0.3 pack_rows.1
  6.3 2.6 %collective-permute-start.2 = (f32[16,2176]{1,0:T(8,128)S(1)}, f32[16,2176]{1,0:T(8,128)S(1)}, u32[]{:S(2)}, u32[]{:S(2)}) collective-permute-start(f32[16,2176]{1,0:T(8,128)S(1)} %get-tuple-element.34), channel_id=1, source_target_pairs={{0,4},{8,12},{16,20},{24,28},{4,0},{12,8},{20,16},{28,24},{1,5},{9... | collective-permute-start | bytes 417800 | tf_op jit(solution)/shard_map/ppermute | solution.py:73
  9.0 0.7 %collective-permute-start.3 = (f32[16,2176]{1,0:T(8,128)S(1)}, f32[16,2176]{1,0:T(8,128)S(1)}, u32[]{:S(2)}, u32[]{:S(2)}) collective-permute-start(f32[16,2176]{1,0:T(8,128)S(1)} %get-tuple-element.35), channel_id=1, source_target_pairs={{4,8},{12,16},{20,24},{8,4},{16,12},{24,20},{5,9},{13,17},{21,25},... | collective-permute-start | bytes 417800 | tf_op jit(solution)/shard_map/ppermute | solution.py:73
  9.6 0.0 copy-done
  9.6 0.0 copy-done.1
  9.6 0.0 copy-done.2
  9.6 1.4 %find_slots.1 = (s32[32,128]{1,0:T(8,128)S(1)}, s32[32,128]{1,0:T(8,128)S(1)}, f32[64,128]{1,0:T(8,128)S(1)}, bf16[160,4096]{1,0:T(8,128)(2,1)S(1)}) custom-call(s32[32,128]{1,0:T(8,128)S(1)} %bitcast.7, s32[32,128]{1,0:T(8,128)S(1)} %bitcast.9, s32[32,128]{1,0:T(8,128)S(1)} %bitcast.11), custom_call_target="tpu_custom_call" | custom-call | flops 20000000 | bytes 1000000 | tf_op jit(solution)/shard_map/find_slots/pallas_call | solution.py:688
  11.1 0.0 copy-start.3
  11.1 0.0 copy-start.4
  11.1 1.8 %first_section.1.sone = f32[17,272,128]{2,1,0:T(8,128)S(1)} custom-call(f32[256,2048]{1,0:T(8,128)S(1)} %get-tuple-element.26.gas, f32[256,2048]{1,0:T(8,128)S(1)} %get-tuple-element.27.speed, f32[256,128]{1,0:T(8,128)S(1)} %get-tuple-element.33.w), custom_call_target="tpu_custom_call" | custom-call | flops 8000000 | bytes 6000000 | tf_op jit(solution)/shard_map/first_section/pallas_call | solution.py:709
  12.9 0.0 collective-permute-done.2.ra.refs_0_
  12.9 0.0 collective-permute-done.3.rb.refs_1_
  12.9 0.0 copy-done.3
  12.9 0.0 copy-done.4
  12.9 7.4 %gas_and_heat.1 = (f32[256,2048]{1,0:T(8,128)}, f32[32,8,128]{2,1,0:T(8,128)}, f32[17,272,128]{2,1,0:T(8,128)S(1)}) custom-call(f32[256,2048]{1,0:T(8,128)S(1)} %get-tuple-element.26.gas, f32[256,2048]{1,0:T(8,128)S(1)} %get-tuple-element.27.speed, f32[17,272,128]{2,1,0:T(8,128)S(1)} %first_section.1.sone, ...), custom_call_target="tpu_custom_call", output_to_operand_aliasing={{2}: (2, {})} | custom-call | flops 60000000 | bytes 40000000 | tf_op jit(solution)/shard_map/gas_and_heat/pallas_call | solution.py:719
  20.3 11.1 %all-to-all-start = ((f32[32,8,128]{2,1,0:T(8,128)}), f32[32,8,128]{2,1,0:T(8,128)S(1)}, u32[]{:S(2)}, u32[]{:S(2)}) async-start(f32[32,8,128]{2,1,0:T(8,128)} %get-tuple-element.41), calls=%async_computation | async-start | bytes 262144 | tf_op jit(solution)/shard_map/all_to_all | solution.py:741
  31.4 7.2 %solid_bulk.2 = (f32[256,2048]{1,0:T(8,128)}, f32[8,128]{1,0:T(8,128)S(1)}) custom-call(f32[256,2048]{1,0:T(8,128)} %solid.7, s32[256,2048]{1,0:T(8,128)} %material.7, f32[256,128]{1,0:T(8,128)S(1)} %get-tuple-element.33.w), custom_call_target="tpu_custom_call" | custom-call | flops 60000000 | bytes 30000000 | tf_op jit(solution)/shard_map/solid_bulk/pallas_call | solution.py:749
  38.5 0.9 %all-to-all-done.recv = f32[32,8,128]{2,1,0:T(8,128)S(1)} async-done(((f32[32,8,128]{2,1,0:T(8,128)}), f32[32,8,128]{2,1,0:T(8,128)S(1)}, u32[]{:S(2)}, u32[]{:S(2)}) %all-to-all-start) | async-done | bytes 131104 | tf_op jit(solution)/shard_map/all_to_all | solution.py:741
  39.4 4.3 %solid_strip.1 = (f32[8,2048]{1,0:T(8,128)S(1)}, f32[3,16,128]{2,1,0:T(8,128)S(1)}, f32[32,2,128]{2,1,0:T(2,128)}) custom-call(f32[32,8,128]{2,1,0:T(8,128)S(1)} %all-to-all-done.recv, f32[16,2176]{1,0:T(8,128)S(1)} %collective-permute-done.2.ra.refs_0_, f32[16,2176]{1,0:T(8,128)S(1)} %collective-permute-done.3.rb.refs_1_, ...), custom_call_target="tpu_custom_call" | custom-call | flops 20000000 | bytes 4000000 | tf_op jit(solution)/shard_map/solid_strip/pallas_call | solution.py:769
  43.7 4.8 %all-to-all-start.1 = ((f32[32,2,128]{2,1,0:T(2,128)}), f32[32,2,128]{2,1,0:T(2,128)S(1)}, u32[]{:S(2)}, u32[]{:S(2)}) async-start(f32[32,2,128]{2,1,0:T(2,128)} %get-tuple-element.43), calls=%async_computation.1 | async-start | bytes 65536 | tf_op jit(solution)/shard_map/all_to_all | solution.py:788
  48.5 1.5 %collective-permute-start.4 = (f32[3,16,128]{2,1,0:T(8,128)S(1)}, f32[3,16,128]{2,1,0:T(8,128)S(1)}, u32[]{:S(2)}, u32[]{:S(2)}) collective-permute-start(f32[3,16,128]{2,1,0:T(8,128)S(1)} %get-tuple-element.44), channel_id=1, source_target_pairs={{4,0},{8,4},{12,8},{16,12},{20,16},{24,20},{28,24},{5,1},{9,5},{13... | collective-permute-start | bytes 73736 | tf_op jit(solution)/shard_map/ppermute | solution.py:789
  50.0 4.6 %solid_bulk.3.back = f32[96,2048]{1,0:T(8,128)S(1)} custom-call(f32[256,2048]{1,0:T(8,128)} %solid.7, s32[256,2048]{1,0:T(8,128)} %material.7, f32[256,128]{1,0:T(8,128)S(1)} %get-tuple-element.33.w, f32[16,2176]{1,0:T(8,128)S(1)} %collective-permute-done.2.ra.refs_0_, f32[16,2176]{1,0:T(8,128)S(1)} %collective-permute-done.3.rb.refs_1_, ...), custom_call_target="tpu_custom_call" | custom-call | flops 60000000 | bytes 30000000 | tf_op jit(solution)/shard_map/solid_bulk/pallas_call | solution.py:749
  54.6 0.0 collective-permute-done.4.below
  54.6 1.2 %all-to-all-done.1.recv = f32[32,2,128]{2,1,0:T(2,128)S(1)} async-done(((f32[32,2,128]{2,1,0:T(2,128)}), f32[32,2,128]{2,1,0:T(2,128)S(1)}, u32[]{:S(2)}, u32[]{:S(2)}) %all-to-all-start.1) | async-done | bytes 32800 | tf_op jit(solution)/shard_map/all_to_all | solution.py:788
  55.7 1.8 %wall_temperatures.1 = (f32[32,128]{1,0:T(8,128)}, f32[256,2048]{1,0:T(8,128)}) custom-call(f32[32,2,128]{2,1,0:T(2,128)S(1)} %all-to-all-done.1.recv, s32[32,128]{1,0:T(8,128)S(1)} %get-tuple-element.37.slot, f32[3,16,128]{2,1,0:T(8,128)S(1)} %collective-permute-done.4.below, f32[96,2048]{1,0:T(8,128)S(1)} %solid_bulk.3.back, ...), custom_call_target="tpu_custom_call", output_to_operand_aliasing={{1}: (5, {})} | custom-call | flops 20000000 | bytes 4000000 | tf_op jit(solution)/shard_map/wall_temperatures/pallas_call | solution.py:794
  (2 shorter events, 0.0 us)
Async XLA Ops:
  2.4 3.6 %collective-permute-start = (f32[16,256]{1,0:T(8,128)S(1)}, f32[16,256]{1,0:T(8,128)S(1)}, u32[]{:S(2)}, u32[]{:S(2)}) collective-permute-start(f32[16,256]{1,0:T(8,128)S(1)} %get-tuple-element.28), channel_id=1, source_target_pairs={{0,1},{2,3},{1,0},{3,2},{4,5},{6,7},{5,4},{7,6},{8,9},{10,11},{9,8... | collective-permute-start | bytes 49160 | tf_op jit(solution)/shard_map/ppermute | solution.py:73
  3.0 6.7 %copy-start = (s32[4096,1]{0,1:T(1,128)S(1)}, s32[4096,1]{0,1:T(1,128)}, u32[]{:S(2)}) copy-start(s32[4096,1]{0,1:T(1,128)} %param.14) | copy-start | bytes 49156
  3.0 6.7 %copy-start.1 = (s32[4096]{0:T(1024)S(1)}, s32[4096]{0:T(1024)}, u32[]{:S(2)}) copy-start(s32[4096]{0:T(1024)} %param.15) | copy-start | bytes 49156
  3.0 6.7 %copy-start.2 = (s32[4096]{0:T(1024)S(1)}, s32[4096]{0:T(1024)}, u32[]{:S(2)}) copy-start(s32[4096]{0:T(1024)} %param.13) | copy-start | bytes 49156
  3.0 3.1 %collective-permute-start.1 = (f32[16,256]{1,0:T(8,128)S(1)}, f32[16,256]{1,0:T(8,128)S(1)}, u32[]{:S(2)}, u32[]{:S(2)}) collective-permute-start(f32[16,256]{1,0:T(8,128)S(1)} %get-tuple-element.29), channel_id=1, source_target_pairs={{1,2},{2,1},{5,6},{6,5},{9,10},{10,9},{13,14},{14,13},{17,18},{18,... | collective-permute-start | bytes 49160 | tf_op jit(solution)/shard_map/ppermute | solution.py:73
  6.3 6.6 %collective-permute-start.2 = (f32[16,2176]{1,0:T(8,128)S(1)}, f32[16,2176]{1,0:T(8,128)S(1)}, u32[]{:S(2)}, u32[]{:S(2)}) collective-permute-start(f32[16,2176]{1,0:T(8,128)S(1)} %get-tuple-element.34), channel_id=1, source_target_pairs={{0,4},{8,12},{16,20},{24,28},{4,0},{12,8},{20,16},{28,24},{1,5},{9... | collective-permute-start | bytes 417800 | tf_op jit(solution)/shard_map/ppermute | solution.py:73
  9.0 3.9 %collective-permute-start.3 = (f32[16,2176]{1,0:T(8,128)S(1)}, f32[16,2176]{1,0:T(8,128)S(1)}, u32[]{:S(2)}, u32[]{:S(2)}) collective-permute-start(f32[16,2176]{1,0:T(8,128)S(1)} %get-tuple-element.35), channel_id=1, source_target_pairs={{4,8},{12,16},{20,24},{8,4},{16,12},{24,20},{5,9},{13,17},{21,25},... | collective-permute-start | bytes 417800 | tf_op jit(solution)/shard_map/ppermute | solution.py:73
  11.1 1.8 %copy-start.3 = (f32[4096]{0:T(1024)S(1)}, f32[4096]{0:T(1024)}, u32[]{:S(2)}) copy-start(f32[4096]{0:T(1024)} %param.16) | copy-start | bytes 49156
  11.1 1.8 %copy-start.4 = (f32[4096]{0:T(1024)S(1)}, f32[4096]{0:T(1024)}, u32[]{:S(2)}) copy-start(f32[4096]{0:T(1024)} %param.17) | copy-start | bytes 49156
  20.3 19.1 %all-to-all-start = ((f32[32,8,128]{2,1,0:T(8,128)}), f32[32,8,128]{2,1,0:T(8,128)S(1)}, u32[]{:S(2)}, u32[]{:S(2)}) async-start(f32[32,8,128]{2,1,0:T(8,128)} %get-tuple-element.41), calls=%async_computation | async-start | bytes 262144 | tf_op jit(solution)/shard_map/all_to_all | solution.py:741
  43.7 12.1 %all-to-all-start.1 = ((f32[32,2,128]{2,1,0:T(2,128)}), f32[32,2,128]{2,1,0:T(2,128)S(1)}, u32[]{:S(2)}, u32[]{:S(2)}) async-start(f32[32,2,128]{2,1,0:T(2,128)} %get-tuple-element.43), calls=%async_computation.1 | async-start | bytes 65536 | tf_op jit(solution)/shard_map/all_to_all | solution.py:788
  48.5 6.1 %collective-permute-start.4 = (f32[3,16,128]{2,1,0:T(8,128)S(1)}, f32[3,16,128]{2,1,0:T(8,128)S(1)}, u32[]{:S(2)}, u32[]{:S(2)}) collective-permute-start(f32[3,16,128]{2,1,0:T(8,128)S(1)} %get-tuple-element.44), channel_id=1, source_target_pairs={{4,0},{8,4},{12,8},{16,12},{20,16},{24,20},{28,24},{5,1},{9,5},{13... | collective-permute-start | bytes 73736 | tf_op jit(solution)/shard_map/ppermute | solution.py:789
